TPU v7x, 32 devices: a whole 2x2x4 slice. The times are simulated.
32 devices in a mesh: dp: 2 (over core), seq: 8 (over z, x), chan: 2 (over y).
Axes of the slice: x: 2, y: 2, z: 4, core: 2. Of those that a mesh axis runs over, the one named last changes fastest.
Arguments:
- inputs: float32 [16, 1024, 1024], P('dp', 'seq', 'chan'), may hold values from -6 to 6
- cotangent: float32 [16, 1024, 1024], P('dp', 'seq', 'chan'), may hold values from -6 to 6
- norm1_gain: float32 [1024], P('chan'), may hold values from 0.1 to 1.9
- norm1_bias: float32 [1024], P('chan'), may hold values from -3 to 3
- log_step: float32 [1024], P('chan'), may hold values from -6.9 to -2.3
- decay_log: float32 [1024, 32], P('chan'), may hold values from -4.6 to 0
- freq: float32 [1024, 32], P('chan'), may hold values from 0 to 8
- out_coef: float32 [2, 1024, 32], P(None, 'chan'), may hold values from -2 to 2
- skip: float32 [1024], P('chan'), may hold values from -4 to 4
- glu_weight: float32 [1024, 2, 1024], P(None, None, 'chan'), may hold values from -0.1875 to 0.1875
- glu_bias: float32 [2, 1024], P(None, 'chan'), may hold values from -3 to 3
- norm2_gain: float32 [1024], P('chan'), may hold values from 0.1 to 1.9
- norm2_bias: float32 [1024], P('chan'), may hold values from -3 to 3
- ffn_in: float32 [1024, 4096], P(None, 'chan'), may hold values from -0.1875 to 0.1875
- ffn_in_bias: float32 [4096], P('chan'), may hold values from -3 to 3
- ffn_out: float32 [4096, 1024], P('chan'), may hold values from -0.09375 to 0.09375
- ffn_out_bias: float32 [1024], P('chan'), may hold values from -3 to 3
Outputs:
- output: float32 [16, 1024, 1024], P('dp', 'seq', 'chan')
- grad_inputs: float32 [16, 1024, 1024], P('dp', 'seq', 'chan')
- grad_norm1_gain: float32 [1024], P('chan')
- grad_norm1_bias: float32 [1024], P('chan')
- grad_log_step: float32 [1024], P('chan')
- grad_decay_log: float32 [1024, 32], P('chan')
- grad_freq: float32 [1024, 32], P('chan')
- grad_out_coef: float32 [2, 1024, 32], P(None, 'chan')
- grad_skip: float32 [1024], P('chan')
- grad_glu_weight: float32 [1024, 2, 1024], P(('dp', 'seq'), None, 'chan')
- grad_glu_bias: float32 [2, 1024], P(None, 'chan')
- grad_norm2_gain: float32 [1024], P('chan')
- grad_norm2_bias: float32 [1024], P('chan')
- grad_ffn_in: float32 [1024, 4096], P(('dp', 'seq'), 'chan')
- grad_ffn_in_bias: float32 [4096], P('chan')
- grad_ffn_out: float32 [4096, 1024], P('chan', ('dp', 'seq'))
- grad_ffn_out_bias: float32 [1024], P('chan')
All inputs are finite; a program needn't handle non-finite values.
Results may differ from a plain program's by a relative error of at most 0.0003.
Values sent between devices are 32-bit elements; how exact they have to be, the bound alone decides.
No kernel may reach another device: no remote copies, remote signals or barrier semaphores. Data moves between devices by JAX's collectives and lax.ppermute only.
A program may use at most 256 MiB of HBM per device.

v0:
```python
from functools import partial
import math

import jax
import jax.numpy as jnp
from jax import lax
from jax.sharding import PartitionSpec as P

epsilon = 1e-05
highest = lax.Precision.HIGHEST


def product(left, right):
    return jnp.dot(left, right, precision=highest, preferred_element_type=jnp.float32)


def contract(form, table, values):
    return jnp.einsum(form, table, values, precision=highest, preferred_element_type=jnp.float32)


def gelu_exact(values):
    return jax.nn.gelu(values, approximate=False)


def glu_apply(stacked):
    return stacked[:, 0] * jax.nn.sigmoid(stacked[:, 1])


def kernel_rows(positions, log_step, decay_log, freq, out_coef):
    step = jnp.exp(log_step)[:, None]
    real_rate = -jnp.exp(decay_log)
    scaled_real = step * real_rate
    scaled_imag = step * freq
    minus_real = (
        jnp.expm1(scaled_real) * jnp.cos(scaled_imag) - 2.0 * jnp.sin(0.5 * scaled_imag) ** 2
    )
    minus_imag = jnp.exp(scaled_real) * jnp.sin(scaled_imag)
    modulus = real_rate * real_rate + freq * freq
    ratio_real = (minus_real * real_rate + minus_imag * freq) / modulus
    ratio_imag = (minus_imag * real_rate - minus_real * freq) / modulus
    weight_real = out_coef[0] * ratio_real - out_coef[1] * ratio_imag
    weight_imag = out_coef[0] * ratio_imag + out_coef[1] * ratio_real
    where = positions[:, None, None]
    magnitude = jnp.exp(where * scaled_real)
    angle = where * scaled_imag
    return 2.0 * jnp.sum(
        weight_real * magnitude * jnp.cos(angle) - weight_imag * magnitude * jnp.sin(angle), axis=2
    )


def dft_table(count_out, count_in, length, out_start, in_start):
    outer = jnp.arange(count_out, dtype=jnp.int32) + out_start
    inner = jnp.arange(count_in, dtype=jnp.int32) + in_start
    turns = outer[:, None] * inner[None, :] % length
    angle = turns.astype(jnp.float32) * (2.0 * math.pi / length)
    return (jnp.cos(angle), jnp.sin(angle))


def forward_spectrum(signal, rows, b_start, length, move):
    groups = signal.shape[1]
    b_count = signal.shape[2]
    doubled = 2 * groups
    cos_rows, sin_rows = dft_table(doubled, groups, doubled, 0, 0)
    real_part = contract("ka,sabc->skbc", cos_rows, signal)
    imag_part = -contract("ka,sabc->skbc", sin_rows, signal)
    cos_twist, sin_twist = dft_table(doubled, b_count, length, 0, b_start)
    cos_twist = cos_twist[None, :, :, None]
    sin_twist = sin_twist[None, :, :, None]
    real_part, imag_part = (
        cos_twist * real_part + sin_twist * imag_part,
        cos_twist * imag_part - sin_twist * real_part,
    )
    real_part, imag_part = move((real_part, imag_part))
    cos_cols, sin_cols = dft_table(rows, rows, rows, 0, 0)
    out_real = contract("qb,skbc->skqc", cos_cols, real_part) + contract(
        "qb,skbc->skqc", sin_cols, imag_part
    )
    out_imag = contract("qb,skbc->skqc", cos_cols, imag_part) - contract(
        "qb,skbc->skqc", sin_cols, real_part
    )
    return (out_real, out_imag)


def inverse_spectrum(real_part, imag_part, groups, rows, k_start, length, move):
    k_count = real_part.shape[1]
    doubled = 2 * groups
    cos_cols, sin_cols = dft_table(rows, rows, rows, 0, 0)
    back_real = contract("bq,skqc->skbc", cos_cols, real_part) - contract(
        "bq,skqc->skbc", sin_cols, imag_part
    )
    back_imag = contract("bq,skqc->skbc", cos_cols, imag_part) + contract(
        "bq,skqc->skbc", sin_cols, real_part
    )
    cos_twist, sin_twist = dft_table(k_count, rows, length, k_start, 0)
    cos_twist = cos_twist[None, :, :, None]
    sin_twist = sin_twist[None, :, :, None]
    real_part, imag_part = (
        cos_twist * back_real - sin_twist * back_imag,
        cos_twist * back_imag + sin_twist * back_real,
    )
    real_part, imag_part = move((real_part, imag_part))
    cos_rows, sin_rows = dft_table(groups, doubled, doubled, 0, 0)
    return (
        contract("ak,skbc->sabc", cos_rows, real_part)
        - contract("ak,skbc->sabc", sin_rows, imag_part)
    ) / length


def chan_sums(first, second):
    return lax.psum((first, second), "chan")


def norm_forward(values, gain, bias, width):
    total, squares = chan_sums(
        jnp.sum(values, axis=1, keepdims=True), jnp.sum(values * values, axis=1, keepdims=True)
    )
    mean = total / width
    scale = lax.rsqrt(squares / width - mean * mean + epsilon)
    unit = (values - mean) * scale
    return (unit * gain + bias, unit, scale)


def norm_backward(incoming, unit, scale, gain, width):
    scaled = incoming * gain
    total, along = chan_sums(
        jnp.sum(scaled, axis=1, keepdims=True), jnp.sum(scaled * unit, axis=1, keepdims=True)
    )
    back = scale * (scaled - total / width - unit * (along / width))
    return (back, jnp.sum(incoming * unit, axis=0), jnp.sum(incoming, axis=0))


def full_width(values):
    return lax.all_gather(values, "chan", axis=1, tiled=True)


def part_width(values):
    return lax.psum_scatter(values, "chan", scatter_dimension=1, tiled=True)


def body(
    inputs,
    cotangent,
    norm1_gain,
    norm1_bias,
    log_step,
    decay_log,
    freq,
    out_coef,
    skip,
    glu_weight,
    glu_bias,
    norm2_gain,
    norm2_bias,
    ffn_in,
    ffn_in_bias,
    ffn_out,
    ffn_out_bias,
):
    sequences, rows, channels = inputs.shape
    groups = lax.axis_size("seq")
    seq_index = lax.axis_index("seq")
    width = channels * lax.axis_size("chan")
    length = 2 * rows * groups
    count = sequences * rows
    block = rows // groups

    def enter(signal):
        moved = lax.all_to_all(signal[:, None], "seq", split_axis=2, concat_axis=1, tiled=True)
        return forward_spectrum(
            moved,
            rows,
            seq_index * block,
            length,
            lambda halves: (
                lax.all_to_all(halves[0], "seq", split_axis=1, concat_axis=2, tiled=True),
                lax.all_to_all(halves[1], "seq", split_axis=1, concat_axis=2, tiled=True),
            ),
        )

    def leave(spec_real, spec_imag):
        values = inverse_spectrum(
            spec_real,
            spec_imag,
            groups,
            rows,
            2 * seq_index,
            length,
            lambda halves: (
                lax.all_to_all(halves[0], "seq", split_axis=2, concat_axis=1, tiled=True),
                lax.all_to_all(halves[1], "seq", split_axis=2, concat_axis=1, tiled=True),
            ),
        )
        return lax.all_to_all(values, "seq", split_axis=1, concat_axis=2, tiled=True)[:, 0]

    positions = (seq_index * rows + jnp.arange(rows, dtype=jnp.int32)).astype(jnp.float32)
    kernel, kernel_back = jax.vjp(
        partial(kernel_rows, positions), log_step, decay_log, freq, out_coef
    )
    flat = inputs.reshape(count, channels)
    normed, unit1, scale1 = norm_forward(flat, norm1_gain, norm1_bias, width)
    stacked = jnp.concatenate([normed.reshape(sequences, rows, channels), kernel[None]], axis=0)
    spec_real, spec_imag = enter(stacked)
    signal_real, signal_imag = (spec_real[:sequences], spec_imag[:sequences])
    kernel_real, kernel_imag = (spec_real[sequences:], spec_imag[sequences:])
    conv = leave(
        signal_real * kernel_real - signal_imag * kernel_imag,
        signal_real * kernel_imag + signal_imag * kernel_real,
    ).reshape(count, channels)
    mixed, gelu_back = jax.vjp(gelu_exact, conv + skip * normed)
    gathered = full_width(mixed)
    glu_flat = glu_weight.reshape(width, 2 * channels)
    both_in = product(gathered, glu_flat).reshape(count, 2, channels) + glu_bias
    glu_out, glu_back = jax.vjp(glu_apply, both_in)
    resid = flat + glu_out
    normed2, unit2, scale2 = norm_forward(resid, norm2_gain, norm2_bias, width)
    gathered2 = full_width(normed2)
    hidden, hidden_back = jax.vjp(gelu_exact, product(gathered2, ffn_in) + ffn_in_bias)
    output = resid + part_width(product(hidden, ffn_out)) + ffn_out_bias
    grad_out = cotangent.reshape(count, channels)
    grad_out_full = full_width(grad_out)
    grad_ffn_out = product(hidden.T, grad_out_full)
    (grad_pre,) = hidden_back(product(grad_out_full, ffn_out.T))
    grad_ffn_in = product(gathered2.T, grad_pre)
    grad_normed2 = part_width(product(grad_pre, ffn_in.T))
    back2, grad_gain2, grad_bias2 = norm_backward(grad_normed2, unit2, scale2, norm2_gain, width)
    grad_resid = grad_out + back2
    (grad_both,) = glu_back(grad_resid)
    grad_both_flat = grad_both.reshape(count, 2 * channels)
    grad_glu = product(gathered.T, grad_both_flat).reshape(width, 2, channels)
    (grad_mix,) = gelu_back(part_width(product(grad_both_flat, glu_flat.T)))
    grad_skip = jnp.sum(grad_mix * normed, axis=0)
    delta_real, delta_imag = enter(grad_mix.reshape(sequences, rows, channels))
    back_real = jnp.concatenate(
        [
            delta_real * kernel_real + delta_imag * kernel_imag,
            jnp.sum(signal_real * delta_real + signal_imag * delta_imag, axis=0, keepdims=True),
        ],
        axis=0,
    )
    back_imag = jnp.concatenate(
        [
            delta_imag * kernel_real - delta_real * kernel_imag,
            jnp.sum(signal_real * delta_imag - signal_imag * delta_real, axis=0, keepdims=True),
        ],
        axis=0,
    )
    back_values = leave(back_real, back_imag)
    grad_normed = back_values[:sequences].reshape(count, channels) + skip * grad_mix
    grad_step, grad_decay, grad_freq, grad_coef = kernel_back(back_values[sequences])
    back1, grad_gain1, grad_bias1 = norm_backward(grad_normed, unit1, scale1, norm1_gain, width)
    grad_inputs = grad_resid + back1
    grad_glu_part, grad_in_part, grad_out_part = (
        lax.psum_scatter(grad_glu, ("dp", "seq"), scatter_dimension=0, tiled=True),
        lax.psum_scatter(grad_ffn_in, ("dp", "seq"), scatter_dimension=0, tiled=True),
        lax.psum_scatter(grad_ffn_out, ("dp", "seq"), scatter_dimension=1, tiled=True),
    )
    smalls = lax.psum(
        (
            grad_gain1,
            grad_bias1,
            grad_step,
            grad_decay,
            grad_freq,
            grad_coef,
            grad_skip,
            jnp.sum(grad_both, axis=0),
            grad_gain2,
            grad_bias2,
            jnp.sum(grad_pre, axis=0),
            jnp.sum(grad_out, axis=0),
        ),
        ("dp", "seq"),
    )
    return (
        output.reshape(sequences, rows, channels),
        grad_inputs.reshape(sequences, rows, channels),
        smalls[0],
        smalls[1],
        smalls[2],
        smalls[3],
        smalls[4],
        smalls[5],
        smalls[6],
        grad_glu_part,
        smalls[7],
        smalls[8],
        smalls[9],
        grad_in_part,
        smalls[10],
        grad_out_part,
        smalls[11],
    )


def solution(mesh):
    placed = (
        P("dp", "seq", "chan"),
        P("dp", "seq", "chan"),
        P("chan"),
        P("chan"),
        P("chan"),
        P("chan", None),
        P("chan", None),
        P(None, "chan", None),
        P("chan"),
        P(None, None, "chan"),
        P(None, "chan"),
        P("chan"),
        P("chan"),
        P(None, "chan"),
        P("chan"),
        P("chan", None),
        P("chan"),
    )
    return jax.shard_map(
        body,
        mesh=mesh,
        in_specs=placed,
        out_specs=(
            P("dp", "seq", "chan"),
            P("dp", "seq", "chan"),
            P("chan"),
            P("chan"),
            P("chan"),
            P("chan", None),
            P("chan", None),
            P(None, "chan", None),
            P("chan"),
            P(("dp", "seq"), None, "chan"),
            P(None, "chan"),
            P("chan"),
            P("chan"),
            P(("dp", "seq"), "chan"),
            P("chan"),
            P("chan", ("dp", "seq")),
            P("chan"),
        ),
        check_vma=False,
    )
```

profile of v0, /device:TPU:0, one launch (start us, length us, event | category | flops | bytes accessed | tf_op | source)
XLA Modules:
  0.0 2059.1 jit_solution(2457421566278956731)
XLA Ops:
  10.5 33.0 %fusion.17 = f32[128,512]{1,0:T(8,128)S(1)} fusion(f32[512,32]{0,1:T(8,128)S(1)} %fusion.112, f32[512,32]{0,1:T(8,128)S(1)} %get-tuple-element.211, f32[512,32]{0,1:T(8,128)S(1)} %get-tuple-element.210, f32[128]{0:T(128)S(1)} %add_convert_fusion, f32[512,32]{0,1:T(8,128)S(1)} %get-tuple-element.191), kind=kLoop, calls=%fused_computation.20 | loop fusion | flops 16711680 | bytes 524800 | tf_op jit(solution)/shard_map/jvp()/reduce_sum | solution.py:46
  61.5 52.6 %all-to-all-done = f32[9,1,128,512]{3,1,0,2:T(1,128)} async-done(((f32[9,1,128,512]{3,1,0,2:T(1,128)}), f32[9,1,128,512]{3,1,0,2:T(1,128)}, u32[]{:S(2)}, u32[]{:S(2)}) %all-to-all-start) | async-done | bytes 2359328 | tf_op jit(solution)/shard_map/all_to_all | solution.py:168
  146.4 96.5 %all-to-all-done.1 = f32[9,16,16,512]{3,2,0,1:T(8,128)} async-done(((f32[9,16,16,512]{3,2,0,1:T(8,128)}), f32[9,16,16,512]{3,2,0,1:T(8,128)}, u32[]{:S(2)}, u32[]{:S(2)}) %all-to-all-start.1) | async-done | bytes 4718624 | tf_op jit(solution)/shard_map/all_to_all | solution.py:175
  262.8 88.4 %all-to-all-done.2 = f32[9,16,16,512]{3,2,0,1:T(8,128)} async-done(((f32[9,16,16,512]{3,2,0,1:T(8,128)}), f32[9,16,16,512]{3,2,0,1:T(8,128)}, u32[]{:S(2)}, u32[]{:S(2)}) %all-to-all-start.2) | async-done | bytes 4718624 | tf_op jit(solution)/shard_map/all_to_all | solution.py:176
  416.2 85.3 %all-to-all-done.3 = f32[8,2,128,512]{3,1,0,2:T(2,128)} async-done(((f32[8,2,128,512]{3,1,0,2:T(2,128)}), f32[8,2,128,512]{3,1,0,2:T(2,128)}, u32[]{:S(2)}, u32[]{:S(2)}) %all-to-all-start.3) | async-done | bytes 4194336 | tf_op jit(solution)/shard_map/all_to_all | solution.py:189
  528.5 70.2 %all-to-all-done.4 = f32[8,2,128,512]{3,1,0,2:T(2,128)} async-done(((f32[8,2,128,512]{3,1,0,2:T(2,128)}), f32[8,2,128,512]{3,1,0,2:T(2,128)}, u32[]{:S(2)}, u32[]{:S(2)}) %all-to-all-start.4) | async-done | bytes 4194336 | tf_op jit(solution)/shard_map/all_to_all | solution.py:190
  621.5 51.8 %all_to_all.186 = f32[8,8,16,512]{3,2,0,1:T(8,128)S(1)} all-to-all(f32[8,8,16,512]{3,2,0,1:T(8,128)S(1)} %copy.319), channel_id=1, replica_groups=mesh['dp'=2,'seq'=8,'chan'=2] {'seq'}, dimensions={1} | all-to-all | bytes 4194304 | tf_op jit(solution)/shard_map/all_to_all | solution.py:193
  692.0 44.8 %all-gather.4.cloned.1.call-done = f32[1024,1024]{1,0:T(8,128)} async-done(((f32[1024,512]{1,0:T(8,128)}), f32[1024,1024]{1,0:T(8,128)}) %all-gather.4.cloned.1.call-update) | async-done | bytes 4194320 | tf_op jit(solution)/shard_map/all_gather | solution.py:133
  736.7 17.2 broadcast_add_fusion
  765.8 56.1 %all-gather.6.cloned.1.call-done = f32[1024,1024]{1,0:T(8,128)} async-done(((f32[1024,512]{1,0:T(8,128)}), f32[1024,1024]{1,0:T(8,128)}) %all-gather.6.cloned.1.call-update) | async-done | bytes 4194320 | tf_op jit(solution)/shard_map/all_gather | solution.py:133
  821.9 30.9 %fusion.302 = f32[1024,2048]{1,0:T(8,128)} fusion(f32[1024,1024]{1,0:T(8,128)} %all-gather.6.cloned.1.call-done, f32[1024,2048]{1,0:T(8,128)} %param.30), kind=kOutput, calls=%fused_computation.412 | convolution fusion | flops 25769803776 | bytes 20971520 | tf_op jit(solution)/shard_map/dot_general | solution.py:14
  852.9 27.4 %all-gather.8.cloned.1.call-done = f32[1024,1024]{1,0:T(8,128)} async-done(((f32[1024,512]{1,0:T(8,128)}), f32[1024,1024]{1,0:T(8,128)}) %all-gather.8.cloned.1.call-update) | async-done | bytes 4194320 | tf_op jit(solution)/shard_map/all_gather | solution.py:133
  880.3 52.0 %fusion.292 = (f32[2048]{0:T(1024)}, f32[1024,2048]{1,0:T(8,128)S(1)}, f32[1024,2048]{1,0:T(8,128)}) fusion(f32[1024,2048]{1,0:T(8,128)} %fusion.302, f32[2048]{0:T(1024)S(1)} %copy-done.68, f32[1024,1024]{1,0:T(8,128)} %all-gather.8.cloned.1.call-done, f32[2048,1024]{1,0:T(8,128)} %param.32), kind=kOutput, calls=%fused_computation.411 | convolution fusion | flops 25922893824 | bytes 37765120 | tf_op jit(solution)/shard_map/dot_general | solution.py:14
  935.6 35.6 %fusion.303 = f32[1024,1024]{1,0:T(8,128)} fusion(f32[1024,2048]{1,0:T(8,128)S(1)} %get-tuple-element.181, f32[1024,2048]{1,0:T(8,128)} %param.30), kind=kOutput, calls=%fused_computation.413 | convolution fusion | flops 25769803776 | bytes 20971520 | tf_op jit(solution)/shard_map/dot_general | solution.py:14
  971.3 32.8 %fusion.51 = f32[1024,1024]{1,0:T(8,128)} fusion(f32[2048,1024]{1,0:T(8,128)} %param.32, f32[1024,2048]{1,0:T(8,128)} %get-tuple-element.182, f32[1024,2048]{1,0:T(8,128)} %fusion.302, f32[2048]{0:T(1024)S(1)} %copy-done.68), kind=kOutput, calls=%fused_computation.94 | convolution fusion | flops 25776095232 | bytes 29368320 | tf_op jit(solution)/shard_map/dot_general | solution.py:14
  1004.1 21.6 %reduce-scatter.9.cloned.1.call-done = f32[1024,512]{1,0:T(8,128)} async-done(((f32[1024,1024]{1,0:T(8,128)}), f32[1024,512]{1,0:T(8,128)}) %reduce-scatter.9.cloned.1.call-update) | async-done | bytes 2097168 | tf_op jit(solution)/shard_map/reduce_scatter | solution.py:137
  1034.4 47.8 %reduce-scatter.7.cloned.1.call-done = f32[1024,512]{1,0:T(8,128)} async-done(((f32[1024,1024]{1,0:T(8,128)}), f32[1024,512]{1,0:T(8,128)}) %reduce-scatter.7.cloned.1.call-update) | async-done | bytes 2097168 | tf_op jit(solution)/shard_map/reduce_scatter | solution.py:137
  1092.6 15.1 fusion.58
  1107.8 54.4 %reduce-scatter.11.cloned.1.call-done = f32[1024,512]{1,0:T(8,128)} async-done(((f32[1024,1024]{1,0:T(8,128)}), f32[1024,512]{1,0:T(8,128)}) %reduce-scatter.11.cloned.1.call-update) | async-done | bytes 2097168 | tf_op jit(solution)/shard_map/reduce_scatter | solution.py:137
  1166.5 54.0 %all_to_all.187 = f32[8,1,128,512]{3,0,1,2:T(8,128)S(1)} all-to-all(f32[8,1,128,512]{3,0,1,2:T(8,128)S(1)} %copy.323), channel_id=1, replica_groups=mesh['dp'=2,'seq'=8,'chan'=2] {'seq'}, dimensions={2} | all-to-all | bytes 4194304 | tf_op jit(solution)/shard_map/all_to_all | solution.py:168
  1249.4 85.6 %all-to-all-done.7 = f32[8,16,16,512]{3,2,0,1:T(8,128)} async-done(((f32[8,16,16,512]{3,2,0,1:T(8,128)}), f32[8,16,16,512]{3,2,0,1:T(8,128)}, u32[]{:S(2)}, u32[]{:S(2)}) %all-to-all-start.7) | async-done | bytes 4194336 | tf_op jit(solution)/shard_map/all_to_all | solution.py:175
  1349.2 30.8 %fusion.31 = f32[1024,2,512]{2,0,1:T(8,128)} fusion(f32[1024,2,512]{0,2,1:T(8,128)} %copy.346, f32[1024,1024]{1,0:T(8,128)} %all-gather.4.cloned.1.call-done), kind=kOutput, calls=%fused_computation.55 | convolution fusion | flops 12884901888 | bytes 12582912 | tf_op jit(solution)/shard_map/dot_general | solution.py:14
  1385.1 64.0 %all-to-all-done.8 = f32[8,16,16,512]{3,2,0,1:T(8,128)} async-done(((f32[8,16,16,512]{3,2,0,1:T(8,128)}), f32[8,16,16,512]{3,2,0,1:T(8,128)}, u32[]{:S(2)}, u32[]{:S(2)}) %all-to-all-start.8) | async-done | bytes 4194336 | tf_op jit(solution)/shard_map/all_to_all | solution.py:176
  1477.1 13.1 fusion.33
  1524.6 32.0 %fusion.50 = f32[2048,1024]{0,1:T(8,128)} fusion(f32[1024,1024]{1,0:T(8,128)} %all-gather.8.cloned.1.call-done, f32[1024,2048]{1,0:T(8,128)} %get-tuple-element.182, f32[1024,2048]{1,0:T(8,128)} %fusion.302, f32[2048]{0:T(1024)S(1)} %copy-done.68), kind=kOutput, calls=%fused_computation.93 | convolution fusion | flops 25776095232 | bytes 29368320 | tf_op jit(solution)/shard_map/dot_general | solution.py:14
  1564.7 97.3 %all-to-all-done.9 = f32[9,2,128,512]{3,1,0,2:T(2,128)} async-done(((f32[9,2,128,512]{3,1,0,2:T(2,128)}), f32[9,2,128,512]{3,1,0,2:T(2,128)}, u32[]{:S(2)}, u32[]{:S(2)}) %all-to-all-start.9) | async-done | bytes 4718624 | tf_op jit(solution)/shard_map/all_to_all | solution.py:189
  1666.6 31.6 %fusion.304 = f32[1024,2048]{1,0:T(8,128)} fusion(f32[1024,1024]{1,0:T(8,128)} %all-gather.6.cloned.1.call-done, f32[1024,2048]{1,0:T(8,128)} %copy-done.72), kind=kOutput, calls=%fused_computation.414 | convolution fusion | flops 25769803776 | bytes 20971520 | tf_op jit(solution)/shard_map/dot_general | solution.py:14
  1714.5 94.0 %all-to-all-done.10 = f32[9,2,128,512]{3,1,0,2:T(2,128)} async-done(((f32[9,2,128,512]{3,1,0,2:T(2,128)}), f32[9,2,128,512]{3,1,0,2:T(2,128)}, u32[]{:S(2)}, u32[]{:S(2)}) %all-to-all-start.10) | async-done | bytes 4718624 | tf_op jit(solution)/shard_map/all_to_all | solution.py:190
  1842.2 63.6 %all-to-all-done.11 = f32[9,8,16,512]{3,2,0,1:T(8,128)} async-done(((f32[9,8,16,512]{3,2,0,1:T(8,128)}), f32[9,8,16,512]{3,2,0,1:T(8,128)}, u32[]{:S(2)}, u32[]{:S(2)}) %all-to-all-start.11) | async-done | bytes 2359328 | tf_op jit(solution)/shard_map/all_to_all | solution.py:193
  1917.2 36.9 %fusion.14 = (f32[512,32]{0,1:T(8,128)S(1)}, f32[512,32]{0,1:T(8,128)S(1)}, f32[512,32]{0,1:T(8,128)S(1)}, f32[512,32]{0,1:T(8,128)S(1)}) fusion(f32[128,512]{1,0:T(8,128)S(1)} %bitcast.392, f32[128,512]{1,0:T(8,128)S(1)} %bitcast_negate_fusion, f32[512,32]{0,1:T(8,128)S(1)} %copy-done.48, f32[512,32]{0,1:T(8,128)S(1)} %copy-done.46, ...), kind=kLoop, calls=%fused_computation.17 | loop fusion | flops 50266112 | bytes 1049088 | tf_op jit(solution)/shard_map/transpose(jvp())/reduce_sum | solution.py:44
  1959.7 58.9 %all-reduce.6 = (f32[512]{0:T(512)}, f32[512]{0:T(512)}, f32[512]{0:T(512)}, f32[512]{0:T(512)}, f32[2,512]{1,0:T(2,128)}, /*index=5*/f32[512]{0:T(512)}, f32[512]{0:T(512)}, f32[2048]{0:T(1024)}, f32[512]{0:T(512)}) all-reduce(f32[512]{0:T(512)S(1)} %get-tuple-element.140, ...), channel_id=1, replica_groups=mesh['dp'=2,'seq'=8,'chan'=2] {'dp','seq'}, use_global_device_ids=true, to_apply=%region_23.24 | all-reduce | flops 6656 | bytes 53248 | tf_op jit(solution)/shard_map/psum | solution.py:257
  2018.6 28.8 %all-reduce.14.cloned.1.call-done = (f32[512,32]{0,1:T(8,128)}, f32[512,32]{0,1:T(8,128)}, f32[2,512,32]{1,2,0:T(8,128)}) async-done(((f32[512,32]{0,1:T(8,128)}, f32[512,32]{0,1:T(8,128)}, f32[2,512,32]{1,2,0:T(8,128)}), (f32[512,32]{0,1:T(8,128)}, f32[512,32]{0,1:T(8,128)}, f32[2,512,32]{1,2,0:T(8,128)})) %all-reduce.14.cloned.1.call-update) | async-done | bytes 262160 | tf_op jit(solution)/shard_map/psum | solution.py:257
  (302 shorter events, 438.9 us)
Async XLA Ops:
  49.9 623.7 %copy-start.33 = (f32[1024,1]{0,1:T(1,128)}, f32[1024,1]{0,1:T(1,128)S(1)}, u32[]{:S(2)}) copy-start(f32[1024,1]{0,1:T(1,128)S(1)} %get-tuple-element.221) | copy-start | bytes 12292
  49.9 623.7 %copy-start.35 = (f32[1024,1]{0,1:T(1,128)}, f32[1024,1]{0,1:T(1,128)S(1)}, u32[]{:S(2)}) copy-start(f32[1024,1]{0,1:T(1,128)S(1)} %get-tuple-element.222) | copy-start | bytes 12292
  54.5 59.6 %all-to-all-start = ((f32[9,1,128,512]{3,1,0,2:T(1,128)}), f32[9,1,128,512]{3,1,0,2:T(1,128)}, u32[]{:S(2)}, u32[]{:S(2)}) async-start(f32[9,1,128,512]{3,1,0,2:T(1,128)} %copy.299), calls=%async_computation | async-start | bytes 4718592 | tf_op jit(solution)/shard_map/all_to_all | solution.py:168
  134.3 108.5 %all-to-all-start.1 = ((f32[9,16,16,512]{3,2,0,1:T(8,128)}), f32[9,16,16,512]{3,2,0,1:T(8,128)}, u32[]{:S(2)}, u32[]{:S(2)}) async-start(f32[9,16,16,512]{3,2,0,1:T(8,128)} %copy.303), calls=%async_computation.1 | async-start | bytes 9437184 | tf_op jit(solution)/shard_map/all_to_all | solution.py:175
  242.9 108.3 %all-to-all-start.2 = ((f32[9,16,16,512]{3,2,0,1:T(8,128)}), f32[9,16,16,512]{3,2,0,1:T(8,128)}, u32[]{:S(2)}, u32[]{:S(2)}) async-start(f32[9,16,16,512]{3,2,0,1:T(8,128)} %copy.307), calls=%async_computation.2 | async-start | bytes 9437184 | tf_op jit(solution)/shard_map/all_to_all | solution.py:176
  247.6 142.6 %copy-start.56 = (f32[2,128]{1,0:T(2,128)}, f32[2,128]{1,0:T(2,128)S(1)}, u32[]{:S(2)}) copy-start(f32[2,128]{1,0:T(2,128)S(1)} %get-tuple-element.223) | copy-start | bytes 3076
  247.6 142.6 %copy-start.58 = (f32[2,128]{1,0:T(2,128)}, f32[2,128]{1,0:T(2,128)S(1)}, u32[]{:S(2)}) copy-start(f32[2,128]{1,0:T(2,128)S(1)} %get-tuple-element.224) | copy-start | bytes 3076
  404.4 97.1 %all-to-all-start.3 = ((f32[8,2,128,512]{3,1,0,2:T(2,128)}), f32[8,2,128,512]{3,1,0,2:T(2,128)}, u32[]{:S(2)}, u32[]{:S(2)}) async-start(f32[8,2,128,512]{3,1,0,2:T(2,128)} %copy.313), calls=%async_computation.3 | async-start | bytes 8388608 | tf_op jit(solution)/shard_map/all_to_all | solution.py:189
  501.5 97.1 %all-to-all-start.4 = ((f32[8,2,128,512]{3,1,0,2:T(2,128)}), f32[8,2,128,512]{3,1,0,2:T(2,128)}, u32[]{:S(2)}, u32[]{:S(2)}) async-start(f32[8,2,128,512]{3,1,0,2:T(2,128)} %copy.316), calls=%async_computation.4 | async-start | bytes 8388608 | tf_op jit(solution)/shard_map/all_to_all | solution.py:190
  506.1 230.7 %all-gather.4.cloned.1.call-start = ((), (), s32[]{:S(2)}) async-start(), calls=%async_computation.18 | async-start | bytes 6291456 | tf_op jit(solution)/shard_map/all_gather | solution.py:133
  680.7 141.2 %all-gather.6.cloned.1.call-start = ((), (), s32[]{:S(2)}) async-start(), calls=%async_computation.19 | async-start | bytes 6291456 | tf_op jit(solution)/shard_map/all_gather | solution.py:133
  765.0 115.2 %all-gather.8.cloned.1.call-start = ((), (), s32[]{:S(2)}) async-start(), calls=%async_computation.21 | async-start | bytes 6291456 | tf_op jit(solution)/shard_map/all_gather | solution.py:133
  765.8 114.5 %copy-start.68 = (f32[2048]{0:T(1024)S(1)}, f32[2048]{0:T(1024)}, u32[]{:S(2)}) copy-start(f32[2048]{0:T(1024)} %param.31) | copy-start | bytes 24580
  765.8 259.9 %reduce-scatter.9.cloned.1.call-start = ((), (), s32[]{:S(2)}) async-start(), calls=%async_computation.22 | async-start | bytes 6291456 | tf_op jit(solution)/shard_map/reduce_scatter | solution.py:137
  971.2 111.0 %reduce-scatter.7.cloned.1.call-start = ((), (), s32[]{:S(2)}) async-start(), calls=%async_computation.20 | async-start | bytes 6291456 | tf_op jit(solution)/shard_map/reduce_scatter | solution.py:137
  1004.0 78.2 %copy-start.10 = (f32[8,128,512]{2,1,0:T(8,128)S(1)}, f32[8,128,512]{2,1,0:T(8,128)}, u32[]{:S(2)}) copy-start(f32[8,128,512]{2,1,0:T(8,128)} %param.18) | copy-start | bytes 6291460
  1004.0 78.2 %copy-start.66 = (f32[512]{0:T(512)S(1)}, f32[512]{0:T(512)}, u32[]{:S(2)}) copy-start(f32[512]{0:T(512)} %param.33) | copy-start | bytes 6148
  1004.0 158.2 %reduce-scatter.11.cloned.1.call-start = ((), (), s32[]{:S(2)}) async-start(), calls=%async_computation.23 | async-start | bytes 6291456 | tf_op jit(solution)/shard_map/reduce_scatter | solution.py:137
  1238.2 96.9 %all-to-all-start.7 = ((f32[8,16,16,512]{3,2,0,1:T(8,128)}), f32[8,16,16,512]{3,2,0,1:T(8,128)}, u32[]{:S(2)}, u32[]{:S(2)}) async-start(f32[8,16,16,512]{3,2,0,1:T(8,128)} %copy.327), calls=%async_computation.10 | async-start | bytes 8388608 | tf_op jit(solution)/shard_map/all_to_all | solution.py:175
  1249.4 90.2 %copy-start.20 = (f32[1024,1,512]{2,0,1:T(8,128)S(1)}, f32[1024,1,512]{2,0,1:T(8,128)}, u32[]{:S(2)}) copy-start(f32[1024,1,512]{2,0,1:T(8,128)} %copy-done.19) | copy-start | bytes 6291460
  1335.1 114.0 %all-to-all-start.8 = ((f32[8,16,16,512]{3,2,0,1:T(8,128)}), f32[8,16,16,512]{3,2,0,1:T(8,128)}, u32[]{:S(2)}, u32[]{:S(2)}) async-start(f32[8,16,16,512]{3,2,0,1:T(8,128)} %copy.331), calls=%async_computation.11 | async-start | bytes 8388608 | tf_op jit(solution)/shard_map/all_to_all | solution.py:176
  1339.6 500.6 %reduce-scatter.13.cloned.1.call-start = ((), (), s32[]{:S(2)}) async-start(), calls=%async_computation.24 | async-start | bytes 4456448 | tf_op jit(solution)/shard_map/reduce_scatter | solution.py:253
  1519.9 142.1 %all-to-all-start.9 = ((f32[9,2,128,512]{3,1,0,2:T(2,128)}), f32[9,2,128,512]{3,1,0,2:T(2,128)}, u32[]{:S(2)}, u32[]{:S(2)}) async-start(f32[9,2,128,512]{3,1,0,2:T(2,128)} %copy.337), calls=%async_computation.12 | async-start | bytes 9437184 | tf_op jit(solution)/shard_map/all_to_all | solution.py:189
  1524.5 494.1 %reduce-scatter.17.cloned.1.call-start = ((), (), s32[]{:S(2)}) async-start(), calls=%async_computation.26 | async-start | bytes 8912896 | tf_op jit(solution)/shard_map/reduce_scatter | solution.py:255
  1662.0 146.4 %all-to-all-start.10 = ((f32[9,2,128,512]{3,1,0,2:T(2,128)}), f32[9,2,128,512]{3,1,0,2:T(2,128)}, u32[]{:S(2)}, u32[]{:S(2)}) async-start(f32[9,2,128,512]{3,1,0,2:T(2,128)} %copy.340), calls=%async_computation.13 | async-start | bytes 9437184 | tf_op jit(solution)/shard_map/all_to_all | solution.py:190
  1666.6 352.0 %reduce-scatter.15.cloned.1.call-start = ((), (), s32[]{:S(2)}) async-start(), calls=%async_computation.25 | async-start | bytes 8912896 | tf_op jit(solution)/shard_map/reduce_scatter | solution.py:254
  1835.6 70.1 %all-to-all-start.11 = ((f32[9,8,16,512]{3,2,0,1:T(8,128)}), f32[9,8,16,512]{3,2,0,1:T(8,128)}, u32[]{:S(2)}, u32[]{:S(2)}) async-start(f32[9,8,16,512]{3,2,0,1:T(8,128)} %copy.343), calls=%async_computation.14 | async-start | bytes 4718592 | tf_op jit(solution)/shard_map/all_to_all | solution.py:193
  1840.0 207.5 %all-reduce.14.cloned.1.call-start = ((), (), s32[]{:S(2)}) async-start(), calls=%async_computation.27 | async-start | bytes 524288 | tf_op jit(solution)/shard_map/psum | solution.py:257
  1842.1 65.8 %copy-start.36 = (f32[1024,1]{0,1:T(1,128)S(1)}, f32[1024,1]{0,1:T(1,128)}, u32[]{:S(2)}) copy-start(f32[1024,1]{0,1:T(1,128)} %copy-done.35) | copy-start | bytes 12292
  1842.1 65.8 %copy-start.50 = (f32[512]{0:T(512)S(1)}, f32[512]{0:T(512)}, u32[]{:S(2)}) copy-start(f32[512]{0:T(512)} %param.19) | copy-start | bytes 6148
  1842.1 65.8 %copy-start.54 = (f32[512]{0:T(512)S(1)}, f32[512]{0:T(512)}, u32[]{:S(2)}) copy-start(f32[512]{0:T(512)} %param.20) | copy-start | bytes 6148
  1842.1 65.8 %copy-start.61 = (f32[512]{0:T(512)S(1)}, f32[512]{0:T(512)}, u32[]{:S(2)}) copy-start(f32[512]{0:T(512)} %param.25) | copy-start | bytes 6148
  (69 other events, 1321.4 us)
Sparse Core Ops, SparseCore 0:
  680.9 55.8 all-gather.3
  765.1 56.7 all-gather.5
  823.5 56.7 all-gather.7
  971.3 54.2 reduce-scatter.8
  1027.9 54.3 reduce-scatter.6
  1107.9 54.2 reduce-scatter.10
  1380.2 89.7 reduce-scatter.12
  1556.7 161.1 reduce-scatter.16
  1722.6 151.2 reduce-scatter.14
  1959.7 87.6 all-reduce.13
where the time goes:
time: 2070 us; the launch traced here: 2060 us
  waiting for transfers between devices  1080 us (52%)
  matrix products  435 us (21%)
  blocking collectives  186 us (9%)
  local copies, waits for them, and re-layouts  182 us (9%)
  other arithmetic  113 us (5%)
  starting transfers between devices  48.5 us (2%)
    dot_general x9, matrix products, product(): jnp.dot(left, right, precision=highest, preferred_element_type=jnp.float32)  278 us
    all_to_all x2, waiting for transfers between devices, leave(): lax.all_to_all(halves[0], 'seq', split_axis=2, concat_axis=1, tiled=True)  183 us
    all_to_all x2, waiting for transfers between devices, enter(): lax.all_to_all(halves[0], 'seq', split_axis=1, concat_axis=2, tiled=True)  182 us
    all_to_all x2, waiting for transfers between devices, leave(): lax.all_to_all(halves[1], 'seq', split_axis=2, concat_axis=1, tiled=True)  164 us
    dot_general x24, matrix products, contract(): jnp.einsum(form, table, values, precision=highest, preferred_element_type...  157 us
    all_to_all x2, waiting for transfers between devices, enter(): lax.all_to_all(halves[1], 'seq', split_axis=1, concat_axis=2, tiled=True)  152 us
    all_gather x3, waiting for transfers between devices, full_width(): return lax.all_gather(values, 'chan', axis=1, tiled=True)  128 us
    reduce_scatter x3, waiting for transfers between devices, part_width(): return lax.psum_scatter(values, 'chan', scatter_dimension=1, tiled=True)  124 us
  transfers between devices with their start and end apart: 20, of which 17 were waited for; matrix products, arithmetic and copies ran while one was open for 19% of the time, Pallas kernels for 0%

commit v1 on v0

v1 whole, which is shorter than its diff:
```python
from functools import partial

import jax
import jax.numpy as jnp
from jax import lax
from jax.experimental import pallas as pl
from jax.experimental.pallas import tpu as pltpu
from jax.sharding import PartitionSpec as P

epsilon = 1e-05
high = lax.Precision.HIGH
highest = lax.Precision.HIGHEST
swap = [(0, 1), (1, 0)]


def contract(left, right, left_dim, right_dim):
    return lax.dot_general(
        left,
        right,
        (((left_dim,), (right_dim,)), ((), ())),
        precision=high,
        preferred_element_type=jnp.float32,
    )


def state_modes(log_step, decay_log, freq, out_coef):
    step = jnp.exp(log_step)[:, None]
    real_rate = -jnp.exp(decay_log)
    scaled_real = step * real_rate
    scaled_imag = step * freq
    minus_real = (
        jnp.expm1(scaled_real) * jnp.cos(scaled_imag) - 2.0 * jnp.sin(0.5 * scaled_imag) ** 2
    )
    minus_imag = jnp.exp(scaled_real) * jnp.sin(scaled_imag)
    modulus = real_rate * real_rate + freq * freq
    ratio_real = (minus_real * real_rate + minus_imag * freq) / modulus
    ratio_imag = (minus_imag * real_rate - minus_real * freq) / modulus
    weight_real = out_coef[0] * ratio_real - out_coef[1] * ratio_imag
    weight_imag = out_coef[0] * ratio_imag + out_coef[1] * ratio_real
    return (weight_real, weight_imag, scaled_real, scaled_imag)


def powers(positions, scaled_real, scaled_imag):
    where = positions[None, None, :]
    magnitude = jnp.exp(where * scaled_real[:, :, None])
    angle = where * scaled_imag[:, :, None]
    return (magnitude * jnp.cos(angle), magnitude * jnp.sin(angle))


def toeplitz_pair(kernel_ref, channel, lag, before, keep):
    rows = kernel_ref.shape[2]
    out = []
    for step in range(2):
        line = kernel_ref[channel, pl.ds(lag + step, 1), :]
        now = pltpu.roll(jnp.broadcast_to(line, (rows, rows)), 0, 1, stride=1, stride_axis=0)
        out.append(jnp.where(keep, now, before))
        before = now
    return (jnp.concatenate(out, axis=1), before)


def conv_kernel(unit_ref, kernel_ref, table_ref, mixed_ref, slope_ref):
    groups, block, sequences, rows = unit_ref.shape
    count = groups * sequences
    row_at = lax.broadcasted_iota(jnp.int32, (rows, rows), 0)
    lane_at = lax.broadcasted_iota(jnp.int32, (rows, rows), 1)
    keep = lane_at >= row_at

    def one(channel, carry):
        unit = unit_ref[:, channel].reshape(count, rows)
        gain = table_ref[channel, 0:1, :]
        bias = table_ref[channel, 1:2, :]
        skip = table_ref[channel, 2:3, :]
        normed = unit * gain + bias
        before = jnp.zeros((rows, rows), jnp.float32)
        sums = [None] * groups
        for lag in range(0, groups, 2):
            table, before = toeplitz_pair(kernel_ref, channel, lag, before, keep)
            part = jnp.dot(
                normed, table, precision=high, preferred_element_type=jnp.float32
            )
            for step in range(2):
                for group in range(groups - lag - step):
                    piece = part[
                        group * sequences : (group + 1) * sequences,
                        step * rows : (step + 1) * rows,
                    ]
                    at = group + lag + step
                    sums[at] = piece if sums[at] is None else sums[at] + piece
        inner = jnp.concatenate(sums, axis=0) + skip * normed
        below = 0.5 * (1.0 + lax.erf(inner * 0.7071067811865476))
        density = 0.3989422804014327 * jnp.exp(-0.5 * inner * inner)
        mixed_ref[:, channel] = (inner * below).reshape(groups, sequences, rows)
        slope_ref[:, channel] = (below + inner * density).reshape(groups, sequences, rows)
        return carry

    lax.fori_loop(0, block, one, 0)


def conv_back_kernel(
    unit_ref, slope_ref, grad_ref, kernel_ref, table_ref, back_ref, lags_ref, sums_ref
):
    groups, block, sequences, rows = unit_ref.shape
    count = groups * sequences
    row_at = lax.broadcasted_iota(jnp.int32, (rows, rows), 0)
    lane_at = lax.broadcasted_iota(jnp.int32, (rows, rows), 1)
    keep = lane_at >= row_at
    line_at = lane_at[:8]
    tile_row = row_at[:8]

    def tiles(cross):
        out = [cross[:8]]
        for tile in range(1, rows // 8):
            out.append(pltpu.roll(cross[8 * tile : 8 * tile + 8], rows - 8 * tile, 1))
        return out

    def merge(first, second):
        out = first[0]
        for tile in range(1, rows // 8):
            out = out + jnp.where(line_at < rows - 8 * tile, first[tile], second[tile])
        for bit in (1, 2, 4):
            out = jnp.where(tile_row & bit != 0, pltpu.roll(out, rows - bit, 1), out)
        return out

    def one(channel, carry):
        unit = unit_ref[:, channel].reshape(count, rows)
        gain = table_ref[channel, 0:1, :]
        bias = table_ref[channel, 1:2, :]
        skip = table_ref[channel, 2:3, :]
        normed = unit * gain + bias
        grad = (grad_ref[:, channel] * slope_ref[:, channel]).reshape(count, rows)
        normed_t = normed.T
        before = jnp.zeros((rows, rows), jnp.float32)
        total = skip * grad
        held = None
        lines = []
        for lag in range(0, groups, 2):
            table, before = toeplitz_pair(kernel_ref, channel, lag, before, keep)
            for step in range(2):
                at = lag + step
                shift = at * sequences
                moved = grad[shift:]
                if at:
                    moved = jnp.concatenate(
                        [moved, jnp.zeros((shift, rows), jnp.float32)], axis=0
                    )
                total = total + lax.dot_general(
                    moved,
                    table[:, step * rows : (step + 1) * rows],
                    (((1,), (1,)), ((), ())),
                    precision=high,
                    preferred_element_type=jnp.float32,
                )
                cross = tiles(
                    jnp.dot(normed_t, moved, precision=high, preferred_element_type=jnp.float32)
                )
                if at:
                    lines.append(merge(held, cross))
                held = cross
        nothing = jnp.zeros((8, rows), jnp.float32)
        lines.append(merge(held, [nothing] * (rows // 8)))
        lines.append(nothing)
        for at in range(groups):
            line = jnp.where(line_at + tile_row < rows, lines[at], lines[at + 1])
            lags_ref[channel, at : at + 1, :] = jnp.sum(line, axis=0, keepdims=True)
        back_ref[:, channel] = (total * gain).reshape(groups, sequences, rows)
        sums_ref[channel, 0:1, :] = jnp.sum(total * unit, axis=0, keepdims=True)
        sums_ref[channel, 1:2, :] = jnp.sum(total, axis=0, keepdims=True)
        sums_ref[channel, 2:3, :] = jnp.sum(grad * normed, axis=0, keepdims=True)
        sums_ref[channel, 3:8, :] = jnp.zeros((5, rows), jnp.float32)
        return carry

    lax.fori_loop(0, block, one, 0)


def channel_blocks(part):
    return 8 if part % 8 == 0 else part


def long_conv(unit, kernel, table):
    groups, part, sequences, rows = unit.shape
    block = channel_blocks(part)
    wide = pl.BlockSpec((groups, block, sequences, rows), lambda i: (0, i, 0, 0))
    return pl.pallas_call(
        conv_kernel,
        grid=(part // block,),
        in_specs=[
            wide,
            pl.BlockSpec((block, groups, rows), lambda i: (i, 0, 0)),
            pl.BlockSpec((block, 8, rows), lambda i: (i, 0, 0)),
        ],
        out_specs=[wide, wide],
        out_shape=[jax.ShapeDtypeStruct(unit.shape, jnp.float32)] * 2,
        compiler_params=pltpu.CompilerParams(vmem_limit_bytes=48 * 1024 * 1024),
        name="conv_forward",
    )(unit, kernel, table)


def long_conv_back(unit, slope, grad, kernel, table):
    groups, part, sequences, rows = unit.shape
    block = channel_blocks(part)
    wide = pl.BlockSpec((groups, block, sequences, rows), lambda i: (0, i, 0, 0))
    lags = pl.BlockSpec((block, groups, rows), lambda i: (i, 0, 0))
    few = pl.BlockSpec((block, 8, rows), lambda i: (i, 0, 0))
    return pl.pallas_call(
        conv_back_kernel,
        grid=(part // block,),
        in_specs=[wide, wide, wide, lags, few],
        out_specs=[wide, lags, few],
        out_shape=[
            jax.ShapeDtypeStruct(unit.shape, jnp.float32),
            jax.ShapeDtypeStruct(kernel.shape, jnp.float32),
            jax.ShapeDtypeStruct((part, 8, rows), jnp.float32),
        ],
        compiler_params=pltpu.CompilerParams(vmem_limit_bytes=48 * 1024 * 1024),
        name="conv_backward",
    )(unit, slope, grad, kernel, table)


def body(
    inputs,
    cotangent,
    norm1_gain,
    norm1_bias,
    log_step,
    decay_log,
    freq,
    out_coef,
    skip,
    glu_weight,
    glu_bias,
    norm2_gain,
    norm2_bias,
    ffn_in,
    ffn_in_bias,
    ffn_out,
    ffn_out_bias,
):
    sequences, rows, channels = inputs.shape
    groups = lax.axis_size("seq")
    seq_index = lax.axis_index("seq")
    chan_index = lax.axis_index("chan")
    dp_index = lax.axis_index("dp")
    width = channels * lax.axis_size("chan")
    count = sequences * rows
    part = channels // groups
    hidden_count = ffn_in.shape[1]

    def to_chan(values):
        return lax.ppermute(values, "chan", swap)

    def spread(values):
        return lax.all_to_all(values, "seq", 0, 0, tiled=True)

    def own_part(values, dim):
        return lax.dynamic_slice_in_dim(values, seq_index * part, part, dim)

    own_at = chan_index * channels
    other_at = channels - own_at

    own_coef = own_part(out_coef, 1)
    modes, modes_back = jax.vjp(
        state_modes, own_part(log_step, 0), own_part(decay_log, 0), own_part(freq, 0), own_coef
    )
    weight_real, weight_imag, scaled_real, scaled_imag = modes
    fine_at = jnp.arange(rows, dtype=jnp.int32).astype(jnp.float32)
    coarse_at = (jnp.arange(groups, dtype=jnp.int32) * rows).astype(jnp.float32)
    fine_real, fine_imag = powers(fine_at, scaled_real, scaled_imag)
    coarse_real, coarse_imag = powers(coarse_at, scaled_real, scaled_imag)
    fine = jnp.concatenate([fine_real, fine_imag], axis=1)
    start_real = weight_real[:, :, None] * coarse_real - weight_imag[:, :, None] * coarse_imag
    start_imag = weight_real[:, :, None] * coarse_imag + weight_imag[:, :, None] * coarse_real
    kernel = 2.0 * jnp.einsum(
        "hnd,hnb->hdb",
        jnp.concatenate([start_real, -start_imag], axis=1),
        fine,
        precision=highest,
        preferred_element_type=jnp.float32,
    )
    table = jnp.stack(
        [own_part(norm1_gain, 0), own_part(norm1_bias, 0), own_part(skip, 0)]
        + [jnp.zeros((part,), jnp.float32)] * 5,
        axis=1,
    )
    table = jnp.broadcast_to(table[:, :, None], (part, 8, rows))

    flat = inputs.reshape(count, channels)
    grad_out = cotangent.reshape(count, channels)
    grad_out_other = to_chan(grad_out)
    total, squares = lax.psum(
        (jnp.sum(flat, axis=1, keepdims=True), jnp.sum(flat * flat, axis=1, keepdims=True)), "chan"
    )
    mean = total / width
    scale1 = lax.rsqrt(squares / width - mean * mean + epsilon)
    unit1 = (flat - mean) * scale1
    unit_parts = spread(unit1.T.reshape(groups, part, sequences, rows))
    mixed_parts, slope_parts = long_conv(unit_parts, kernel, table)
    mixed_t = spread(mixed_parts).reshape(channels, count)
    mixed_t_other = to_chan(mixed_t)

    glu_flat = glu_weight.reshape(width, 2 * channels)
    glu_own = lax.dynamic_slice_in_dim(glu_flat, own_at, channels, 0)
    glu_other = lax.dynamic_slice_in_dim(glu_flat, other_at, channels, 0)
    both = (
        contract(mixed_t, glu_own, 0, 0)
        + contract(mixed_t_other, glu_other, 0, 0)
        + glu_bias.reshape(1, 2 * channels)
    )
    value = both[:, :channels]
    gate = jax.nn.sigmoid(both[:, channels:])
    resid = flat + value * gate
    resid_other = to_chan(resid)

    gain2_other, bias2_other = to_chan((norm2_gain, norm2_bias))
    total = jnp.sum(resid, axis=1, keepdims=True) + jnp.sum(resid_other, axis=1, keepdims=True)
    squares = jnp.sum(resid * resid, axis=1, keepdims=True) + jnp.sum(
        resid_other * resid_other, axis=1, keepdims=True
    )
    mean = total / width
    scale2 = lax.rsqrt(squares / width - mean * mean + epsilon)
    unit2 = (resid - mean) * scale2
    normed2 = unit2 * norm2_gain + norm2_bias
    normed2_other = (resid_other - mean) * scale2 * gain2_other + bias2_other

    in_own = lax.dynamic_slice_in_dim(ffn_in, own_at, channels, 0)
    in_other = lax.dynamic_slice_in_dim(ffn_in, other_at, channels, 0)
    out_own = lax.dynamic_slice_in_dim(ffn_out, own_at, channels, 1)
    out_other = lax.dynamic_slice_in_dim(ffn_out, other_at, channels, 1)
    grad_hidden = contract(grad_out, out_own, 1, 1) + contract(grad_out_other, out_other, 1, 1)
    pre = contract(normed2, in_own, 1, 0) + contract(normed2_other, in_other, 1, 0) + ffn_in_bias
    below = 0.5 * (1.0 + lax.erf(pre * 0.7071067811865476))
    hidden = pre * below
    grad_pre = grad_hidden * (below + pre * (0.3989422804014327 * jnp.exp(-0.5 * pre * pre)))
    grad_normed2 = to_chan(contract(grad_pre, in_other, 1, 1)) + contract(grad_pre, in_own, 1, 1)
    output = (
        to_chan(contract(hidden, out_other, 1, 0))
        + contract(hidden, out_own, 1, 0)
        + resid
        + ffn_out_bias
    )

    scaled = grad_normed2 * norm2_gain
    total, along = lax.psum(
        (
            jnp.sum(scaled, axis=1, keepdims=True),
            jnp.sum(scaled * unit2, axis=1, keepdims=True),
        ),
        "chan",
    )
    grad_resid = grad_out + scale2 * (scaled - total / width - unit2 * (along / width))
    grad_value = grad_resid * gate
    grad_both = jnp.concatenate([grad_value, grad_value * value * (1.0 - gate)], axis=1)
    grad_mixed_t = to_chan(contract(glu_other, grad_both, 1, 1)) + contract(
        glu_own, grad_both, 1, 1
    )
    grad_parts = spread(grad_mixed_t.reshape(groups, part, sequences, rows))
    back_parts, grad_kernel, conv_sums = long_conv_back(
        unit_parts, slope_parts, grad_parts, kernel, table
    )
    scaled = spread(back_parts).reshape(channels, count).T
    total, along = lax.psum(
        (
            jnp.sum(scaled, axis=1, keepdims=True),
            jnp.sum(scaled * unit1, axis=1, keepdims=True),
        ),
        "chan",
    )
    grad_inputs = grad_resid + scale1 * (scaled - total / width - unit1 * (along / width))

    pulled = jnp.einsum(
        "hdb,hnb->hnd",
        jnp.concatenate([grad_kernel, grad_kernel * fine_at], axis=1),
        fine,
        precision=highest,
        preferred_element_type=jnp.float32,
    )
    modes_count = freq.shape[1]
    flat_real, flat_imag = pulled[:, :modes_count, :groups], pulled[:, modes_count:, :groups]
    slant_real = pulled[:, :modes_count, groups:] + coarse_at * flat_real
    slant_imag = pulled[:, modes_count:, groups:] + coarse_at * flat_imag
    zero_real = jnp.sum(coarse_real * flat_real - coarse_imag * flat_imag, axis=2)
    zero_imag = jnp.sum(coarse_real * flat_imag + coarse_imag * flat_real, axis=2)
    one_real = jnp.sum(coarse_real * slant_real - coarse_imag * slant_imag, axis=2)
    one_imag = jnp.sum(coarse_real * slant_imag + coarse_imag * slant_real, axis=2)
    grad_step, grad_decay, grad_freq, grad_coef = modes_back(
        (
            2.0 * zero_real,
            -2.0 * zero_imag,
            2.0 * (weight_real * one_real - weight_imag * one_imag),
            -2.0 * (weight_real * one_imag + weight_imag * one_real),
        )
    )
    sums = jnp.sum(conv_sums, axis=2)
    states = lax.psum(
        jnp.concatenate(
            [grad_decay, grad_freq, grad_coef[0], grad_coef[1], sums[:, :3], grad_step[:, None]],
            axis=1,
        ),
        "dp",
    )
    states = lax.all_gather(states, "seq", axis=0, tiled=True)

    same = chan_index == dp_index

    def halves(own, other):
        return (jnp.where(same, own, other), jnp.where(same, other, own))

    def summed(keep, send, right, left_dim):
        sent = lax.ppermute(contract(send, right, left_dim, 0), "dp", swap)
        return lax.psum_scatter(
            contract(keep, right, left_dim, 0) + sent, "seq", scatter_dimension=0, tiled=True
        )

    grad_ffn_out = summed(*halves(grad_out, grad_out_other), hidden, 0).T
    grad_ffn_in = summed(*halves(normed2, normed2_other), grad_pre, 0)
    grad_glu = summed(*halves(mixed_t, mixed_t_other), grad_both, 1)
    locals_flat = jnp.concatenate(
        [
            jnp.sum(grad_both, axis=0),
            jnp.sum(grad_normed2 * unit2, axis=0),
            jnp.sum(grad_normed2, axis=0),
            jnp.sum(grad_out, axis=0),
            jnp.sum(grad_pre, axis=0),
        ]
    )
    locals_flat = lax.psum(locals_flat, ("dp", "seq"))
    c = channels
    return (
        output.reshape(sequences, rows, channels),
        grad_inputs.reshape(sequences, rows, channels),
        states[:, 4 * modes_count],
        states[:, 4 * modes_count + 1],
        states[:, 4 * modes_count + 3],
        states[:, :modes_count],
        states[:, modes_count : 2 * modes_count],
        jnp.stack(
            [
                states[:, 2 * modes_count : 3 * modes_count],
                states[:, 3 * modes_count : 4 * modes_count],
            ]
        ),
        states[:, 4 * modes_count + 2],
        grad_glu.reshape(-1, 2, channels),
        locals_flat[: 2 * c].reshape(2, c),
        locals_flat[2 * c : 3 * c],
        locals_flat[3 * c : 4 * c],
        grad_ffn_in,
        locals_flat[5 * c :],
        grad_ffn_out,
        locals_flat[4 * c : 5 * c],
    )


def solution(mesh):
    placed = (
        P("dp", "seq", "chan"),
        P("dp", "seq", "chan"),
        P("chan"),
        P("chan"),
        P("chan"),
        P("chan", None),
        P("chan", None),
        P(None, "chan", None),
        P("chan"),
        P(None, None, "chan"),
        P(None, "chan"),
        P("chan"),
        P("chan"),
        P(None, "chan"),
        P("chan"),
        P("chan", None),
        P("chan"),
    )
    return jax.shard_map(
        body,
        mesh=mesh,
        in_specs=placed,
        out_specs=(
            P("dp", "seq", "chan"),
            P("dp", "seq", "chan"),
            P("chan"),
            P("chan"),
            P("chan"),
            P("chan", None),
            P("chan", None),
            P(None, "chan", None),
            P("chan"),
            P(("dp", "seq"), None, "chan"),
            P(None, "chan"),
            P("chan"),
            P("chan"),
            P(("dp", "seq"), "chan"),
            P("chan"),
            P("chan", ("dp", "seq")),
            P("chan"),
        ),
        check_vma=False,
    )
```

time: 2070 us -> 852 us (0.41)
  waiting for transfers between devices: 1080 us -> 261 us
  matrix products: 435 us -> 175 us
  local copies, waits for them, and re-layouts: 182 us -> 32.5 us
  Pallas kernels: 0 us -> 98.5 us
  other arithmetic: 113 us -> 31.5 us
  starting transfers between devices: 48.5 us -> 26.8 us
    all_to_all x10 -> x3, waiting for transfers between devices: 797 us -> 79.7 us  [spread(): return lax.all_to_all(values, 'seq', 0, 0, tiled=True)]
    dot_general x33 -> x20, matrix products: 435 us -> 175 us  [the longest x18 170 us: contract(): lax.dot_general(left, right, (((left_dim,), (right_dim,)), ((), ())), pre...]
    ppermute x0 -> x11, waiting for transfers between devices: none -> 181 us  [the longest x8 179 us: to_chan(): return lax.ppermute(values, 'chan', swap)]
    all_gather x3 -> x0, waiting for transfers between devices: 128 us -> none  [full_width(): return lax.all_gather(values, 'chan', axis=1, tiled=True)]
    reduce_scatter x6 -> x3, waiting for transfers between devices: 124 us -> 0.01 us  [summed(): lax.psum_scatter(contract(keep, right, left_dim, 0) + sent, 'seq', scatte...]
    pallas_call x0 -> x2, Pallas kernels: none -> 98.5 us  [the longest x1 72.9 us: long_conv_back(): pl.pallas_call(conv_back_kernel, grid=(part // block,), in_specs=[wide, w...]
    all_to_all x18 -> x0, local copies, waits for them, and re-layouts: 81.6 us -> none  [the longest x6 32.5 us: leave(): lax.all_to_all(halves[0], 'seq', split_axis=2, concat_axis=1, tiled=True)]
    reduce_sum x7 -> x8, other arithmetic: 78.9 us -> 12 us  [the longest x1 2.67 us: body(): jnp.sum(grad_both, axis=0)]
  transfers between devices with their start and end apart: 20 -> 17, of which waited for: 17 -> 8; matrix products, arithmetic and copies ran while one was open for 19% -> 20% of each run, Pallas kernels for 0% -> 9%
where the time goes in v1:
time: 852 us; the launch traced here: 844 us
  waiting for transfers between devices  261 us (31%)
  blocking collectives  204 us (24%)
  matrix products  175 us (21%)
  Pallas kernels  98.5 us (12%)
  local copies, waits for them, and re-layouts  32.5 us (4%)
  other arithmetic  31.5 us (4%)
  starting transfers between devices  26.8 us (3%)
  between operations  14.9 us (2%)
    ppermute x8, waiting for transfers between devices, to_chan(): return lax.ppermute(values, 'chan', swap)  179 us
    dot_general x18, matrix products, contract(): lax.dot_general(left, right, (((left_dim,), (right_dim,)), ((), ())), pre...  170 us
    psum x1, blocking collectives, body(): locals_flat = lax.psum(locals_flat, ('dp', 'seq'))  102 us
    all_to_all x3, waiting for transfers between devices, spread(): return lax.all_to_all(values, 'seq', 0, 0, tiled=True)  79.7 us
    pallas_call x1, Pallas kernels, long_conv_back(): pl.pallas_call(conv_back_kernel, grid=(part // block,), in_specs=[wide, w...  72.9 us
    all_to_all x1, blocking collectives, spread(): return lax.all_to_all(values, 'seq', 0, 0, tiled=True)  51.8 us
    all_gather x1, blocking collectives, body(): states = lax.all_gather(states, 'seq', axis=0, tiled=True)  31.2 us
    pallas_call x1, Pallas kernels, long_conv(): pl.pallas_call(conv_kernel, grid=(part // block,), in_specs=[wide, pl.Blo...  25.6 us
  transfers between devices with their start and end apart: 17, of which 8 were waited for; matrix products, arithmetic and copies ran while one was open for 20% of the time, Pallas kernels for 9%

profile of v1, /device:TPU:0, one launch (start us, length us, event | category | flops | bytes accessed | tf_op | source)
XLA Modules:
  0.0 844.3 jit_solution(8347660625700356267)
XLA Ops:
  9.3 5.9 all-reduce.6
  20.7 6.5 all-to-all-start
  38.5 35.7 %all-to-all-done.unit_ref = f32[8,64,8,128]{3,2,1,0:T(8,128)S(1)} async-done(((f32[8,64,8,128]{3,2,1,0:T(8,128)}), f32[8,64,8,128]{3,2,1,0:T(8,128)S(1)}, u32[]{:S(2)}, u32[]{:S(2)}) %all-to-all-start) | async-done | bytes 2097184 | tf_op jit(solution)/shard_map/all_to_all | solution.py:252
  75.5 25.6 %conv_forward.1 = (f32[8,64,8,128]{3,2,1,0:T(8,128)S(1)}, f32[8,64,8,128]{3,2,1,0:T(8,128)S(1)}) custom-call(f32[8,64,8,128]{3,2,1,0:T(8,128)} %copy-done.2, f32[64,8,128]{2,1,0:T(8,128)S(1)} %fusion.63.kernel_ref, f32[64,8,128]{2,1,0:T(8,128)S(1)} %broadcast_in_dim.26.table_ref), custom_call_target="tpu_custom_call" | custom-call | tf_op jit(solution)/shard_map/conv_forward/pallas_call | solution.py:183
  101.1 51.8 %all_to_all.20 = f32[8,64,8,128]{3,2,1,0:T(8,128)S(1)} all-to-all(f32[8,64,8,128]{3,2,1,0:T(8,128)S(1)} %get-tuple-element.22), channel_id=1, replica_groups=mesh['dp'=2,'seq'=8,'chan'=2] {'seq'}, dimensions={0} | all-to-all | bytes 4194304 | tf_op jit(solution)/shard_map/all_to_all | solution.py:252
  161.6 5.6 fusion.48
  167.2 34.2 %collective-permute-done = f32[512,1024]{1,0:T(8,128)} collective-permute-done((f32[512,1024]{1,0:T(8,128)}, f32[512,1024]{1,0:T(8,128)}, u32[]{:S(2)}, u32[]{:S(2)}) %collective-permute-start) | collective-permute-done | bytes 2097184 | tf_op jit(solution)/shard_map/ppermute | solution.py:249
  201.4 5.9 add_add_fusion.1
  213.5 7.5 fusion.5
  221.0 37.0 %collective-permute-done.1 = f32[1024,512]{1,0:T(8,128)S(1)} collective-permute-done((f32[1024,512]{1,0:T(8,128)S(1)}, f32[1024,512]{1,0:T(8,128)S(1)}, u32[]{:S(2)}, u32[]{:S(2)}) %collective-permute-start.1) | collective-permute-done | bytes 2097184 | tf_op jit(solution)/shard_map/ppermute | solution.py:249
  258.4 9.1 %fusion.19 = f32[1024,2048]{1,0:T(8,128)} fusion(f32[1024,2048]{1,0:T(8,128)S(1)} %bitcast.143, s32[]{:T(128)S(6)} %select_n.52, f32[512]{0:T(512)S(1)} %copy-done.36, f32[512]{0:T(512)S(1)} %copy-done.32, f32[1024,512]{1,0:T(8,128)S(1)} %get-tuple-element.128, f32[1024]{0:T(1024)S(1)} %get-tuple-element.126, f32[1024]{0:T(1024)S(1)} %get-tuple-element.127), kind=kOutput, calls=%fused_computation.24 | convolution fusion | flops 6444548096 | bytes 14692356 | tf_op jit(solution)/shard_map/dot_general | solution.py:17
  267.6 14.8 %fusion.125 = (f32[1024,2048]{1,0:T(8,128)}, f32[1024,2048]{1,0:T(8,128)}) fusion(f32[2048]{0:T(1024)S(1)} %copy-done.35, f32[1024,2048]{1,0:T(8,128)} %fusion.19, f32[1024,2048]{1,0:T(8,128)} %param.30, s32[]{:T(128)S(6)} %select_n.53, f32[1024,512]{1,0:T(8,128)S(1)} %collective-permute-done.1, f32[512]{0:T(512)S(1)} %collective-permute-done.3, ...), kind=kOutput, calls=%fused_computation.216 | convolution fusion | flops 6457131008 | bytes 31477764 | tf_op jit(solution)/shard_map/dot_general | solution.py:17
  282.3 17.3 %collective-permute-done.5 = f32[1024,512]{1,0:T(8,128)S(1)} collective-permute-done((f32[1024,512]{1,0:T(8,128)S(1)}, f32[1024,512]{1,0:T(8,128)S(1)}, u32[]{:S(2)}, u32[]{:S(2)}) %collective-permute-start.5) | collective-permute-done | bytes 2097184 | tf_op jit(solution)/shard_map/ppermute | solution.py:249
  300.9 13.1 %fusion.131 = (f32[2048]{0:T(1024)S(1)}, f32[1024,2048]{1,0:T(8,128)S(1)}) fusion(f32[1024,2048]{1,0:T(8,128)} %get-tuple-element.161, f32[2048,1024]{0,1:T(8,128)S(1)} %fusion.5, f32[1024,512]{1,0:T(8,128)} %copy-done.24, f32[2048,1024]{1,0:T(8,128)} %param.32, s32[]{:T(128)S(6)} %select_n.53), kind=kOutput, calls=%fused_computation.219 | convolution fusion | flops 6465517568 | bytes 31465476 | tf_op jit(solution)/shard_map/dot_general | solution.py:17
  314.0 11.4 %fusion.13 = f32[1024,512]{1,0:T(8,128)} fusion(f32[1024,2048]{1,0:T(8,128)S(1)} %get-tuple-element.164, f32[1024,2048]{1,0:T(8,128)} %param.30, s32[]{:T(128)S(6)} %select_n.53), kind=kOutput, calls=%fused_computation.18 | convolution fusion | flops 6442450944 | bytes 14680068 | tf_op jit(solution)/shard_map/dot_general | solution.py:17
  326.9 43.0 %collective-permute-done.6 = f32[1024,512]{1,0:T(8,128)} collective-permute-done((f32[1024,512]{1,0:T(8,128)}, f32[1024,512]{1,0:T(8,128)}, u32[]{:S(2)}, u32[]{:S(2)}) %collective-permute-start.6) | collective-permute-done | bytes 2097184 | tf_op jit(solution)/shard_map/ppermute | solution.py:249
  369.9 12.7 %multiply_reduce_fusion = (f32[512]{0:T(512)S(1)}, f32[1024]{0:T(1024)S(1)}, f32[1024]{0:T(1024)S(1)}, f32[512]{0:T(512)S(1)}, f32[1024,512]{1,0:T(8,128)}) fusion(f32[1024]{0:T(1024)S(1)} %get-tuple-element.126, f32[1024,512]{1,0:T(8,128)S(1)} %get-tuple-element.128, f32[1024]{0:T(1024)S(1)} %get-tuple-element.127, f32[512]{0:T(512)S(1)} %copy-done.32, ...), kind=kOutput, calls=%fused_computation.50 | convolution fusion | flops 6447690752 | bytes 18896900 | tf_op jit(solution)/shard_map/dot_general | solution.py:17
  387.7 6.0 subtract_multiply_fusion
  393.7 7.0 fusion.39
  400.8 9.6 %fusion.36 = f32[512,2048]{1,0:T(8,128)} fusion(f32[1024,2048]{1,0:T(8,128)S(1)} %copy-done.12, f32[1024,512]{1,0:T(8,128)S(1)} %copy-done.30, f32[512]{0:T(512)S(1)} %collective-permute-done.3, f32[512]{0:T(512)S(1)} %collective-permute-done.2, f32[512]{0:T(512)S(1)} %copy-done.36, f32[512]{0:T(512)S(1)} %copy-done.32, f32[1024]{0:T(1024)S(1)} %get-tuple-element.126, ...), kind=kOutput, calls=%fused_computation.47 | convolution fusion | flops 6447169536 | bytes 16793600 | tf_op jit(solution)/shard_map/dot_general | solution.py:17
  411.0 5.3 fusion.52
  418.1 13.5 %convolution_add_fusion.1 = f32[512,2048]{1,0:T(8,128)} fusion(f32[512,2048]{1,0:T(8,128)} %collective-permute-done.9, f32[1024,2048]{1,0:T(8,128)} %copy-done.11, f32[1024,512]{1,0:T(8,128)} %copy-done.29, f32[512]{0:T(512)S(1)} %collective-permute-done.3, f32[512]{0:T(512)S(1)} %collective-permute-done.2, f32[512]{0:T(512)S(1)} %copy-done.36, ...), kind=kOutput, calls=%fused_computation.27 | convolution fusion | flops 6448218112 | bytes 20987904 | tf_op jit(solution)/shard_map/dot_general | solution.py:17
  431.6 11.8 %fusion.33 = f32[512,2048]{1,0:T(8,128)} fusion(f32[1024,2048]{1,0:T(8,128)} %get-tuple-element.160, f32[1024,512]{1,0:T(8,128)} %copy-done.24, f32[1024,512]{1,0:T(8,128)} %bitcast.130, pred[]{:T(512)S(6)} %eq.3), kind=kOutput, calls=%fused_computation.44 | convolution fusion | flops 6442975232 | bytes 16777216 | tf_op jit(solution)/shard_map/dot_general | solution.py:17
  447.6 47.6 %collective-permute-done.7 = f32[512,1024]{1,0:T(8,128)S(1)} collective-permute-done((f32[512,1024]{1,0:T(8,128)S(1)}, f32[512,1024]{1,0:T(8,128)S(1)}, u32[]{:S(2)}, u32[]{:S(2)}) %collective-permute-start.7) | collective-permute-done | bytes 2097184 | tf_op jit(solution)/shard_map/ppermute | solution.py:249
  500.7 6.6 all-to-all-start.2
  507.4 11.7 %convolution_add_fusion = f32[512,2048]{1,0:T(8,128)} fusion(f32[512,2048]{1,0:T(8,128)} %collective-permute-done.10, f32[1024,2048]{1,0:T(8,128)} %get-tuple-element.160, f32[1024,512]{1,0:T(8,128)S(1)} %bitcast.133, f32[1024,512]{1,0:T(8,128)} %copy-done.24, pred[]{:T(512)S(6)} %eq.3), kind=kOutput, calls=%fused_computation.26 | convolution fusion | flops 6444023808 | bytes 20971520 | tf_op jit(solution)/shard_map/dot_general | solution.py:17
  519.2 11.6 %fusion.11 = f32[1024,512]{1,0:T(8,128)} fusion(f32[1024,2048]{1,0:T(8,128)} %get-tuple-element.160, f32[2048,1024]{1,0:T(8,128)} %param.32, s32[]{:T(128)S(6)} %select_n.53), kind=kOutput, calls=%fused_computation.16 | convolution fusion | flops 6442450944 | bytes 14680068 | tf_op jit(solution)/shard_map/dot_general | solution.py:17
  534.6 44.0 %all-to-all-done.2.grad_ref = f32[8,64,8,128]{3,2,1,0:T(8,128)} async-done(((f32[8,64,8,128]{3,2,1,0:T(8,128)}), f32[8,64,8,128]{3,2,1,0:T(8,128)}, u32[]{:S(2)}, u32[]{:S(2)}) %all-to-all-start.2) | async-done | bytes 2097184 | tf_op jit(solution)/shard_map/all_to_all | solution.py:252
  578.6 72.9 %conv_backward.1 = (f32[8,64,8,128]{3,2,1,0:T(8,128)S(1)}, f32[64,8,128]{2,1,0:T(8,128)S(1)}, f32[64,8,128]{2,1,0:T(8,128)S(1)}) custom-call(f32[8,64,8,128]{3,2,1,0:T(8,128)S(1)} %copy-done.3, f32[8,64,8,128]{3,2,1,0:T(8,128)} %copy-done.4, f32[8,64,8,128]{3,2,1,0:T(8,128)} %all-to-all-done.2.grad_ref, f32[64,8,128]{2,1,0:T(8,128)S(1)} %fusion.63.kernel_ref, ...), custom_call_target="tpu_custom_call" | custom-call | tf_op jit(solution)/shard_map/conv_backward/pallas_call | solution.py:204
  657.4 101.8 %psum.63 = f32[4608]{0:T(1024)S(1)} all-reduce(f32[4608]{0:T(1024)S(1)} %constant_dynamic-update-slice_fusion), channel_id=1, replica_groups=mesh['dp'=2,'seq'=8,'chan'=2] {'dp','seq'}, use_global_device_ids=true, to_apply=%region_30.31 | all-reduce | flops 4608 | bytes 36864 | tf_op jit(solution)/shard_map/psum | solution.py:425
  761.0 12.0 %add_add_fusion.2 = f32[1024,512]{1,0:T(8,128)} fusion(f32[1024,512]{1,0:T(8,128)S(1)} %copy-done.20, f32[1024,512]{1,0:T(8,128)} %collective-permute-done.4, f32[1024,2048]{1,0:T(8,128)} %get-tuple-element.160, f32[2048,1024]{1,0:T(8,128)} %param.32, s32[]{:T(128)S(6)} %select_n.52, f32[512]{0:T(512)S(1)} %copy-done.38), kind=kOutput, calls=%fused_computation.59 | convolution fusion | flops 6444023808 | bytes 18876420 | tf_op jit(solution)/shard_map/dot_general | solution.py:17
  783.5 31.2 %all_gather.3 = f32[512,132]{1,0:T(8,128)S(1)} all-gather(f32[64,132]{1,0:T(8,128)S(1)} %copy.92), channel_id=1, replica_groups=mesh['dp'=2,'seq'=8,'chan'=2] {'seq'}, dimensions={0}, use_global_device_ids=true | all-gather | bytes 304128 | tf_op jit(solution)/shard_map/all_gather | solution.py:400
  (196 shorter events, 99.8 us)
Async XLA Ops:
  7.2 22.1 %copy-start = (f32[512]{0:T(512)S(1)}, f32[512]{0:T(512)}, u32[]{:S(2)}) copy-start(f32[512]{0:T(512)} %param.19) | copy-start | bytes 6148
  20.7 53.5 %all-to-all-start = ((f32[8,64,8,128]{3,2,1,0:T(8,128)}), f32[8,64,8,128]{3,2,1,0:T(8,128)S(1)}, u32[]{:S(2)}, u32[]{:S(2)}) async-start(f32[8,64,8,128]{3,2,1,0:T(8,128)} %bitcast.146), calls=%async_computation | async-start | bytes 4194304 | tf_op jit(solution)/shard_map/all_to_all | solution.py:252
  27.1 791.4 %reduce-scatter.4.cloned.1.call-start = ((), (), s32[]{:S(2)}) async-start(), calls=%async_computation.7 | async-start | bytes 2359296 | tf_op jit(solution)/shard_map/reduce_scatter | solution.py:409
  101.1 51.8 %copy-start.4 = (f32[8,64,8,128]{3,2,1,0:T(8,128)}, f32[8,64,8,128]{3,2,1,0:T(8,128)S(1)}, u32[]{:S(2)}) copy-start(f32[8,64,8,128]{3,2,1,0:T(8,128)S(1)} %get-tuple-element.23.slope_ref) | copy-start | bytes 6291460
  154.9 46.4 %collective-permute-start = (f32[512,1024]{1,0:T(8,128)}, f32[512,1024]{1,0:T(8,128)}, u32[]{:S(2)}, u32[]{:S(2)}) collective-permute-start(f32[512,1024]{1,0:T(8,128)} %bitcast.128), channel_id=1, source_target_pairs={{0,1},{1,0},{2,3},{3,2},{4,5},{5,4},{6,7},{7,6},{8,9},{9,8},{10,11... | collective-permute-start | bytes 6291464 | tf_op jit(solution)/shard_map/ppermute | solution.py:249
  161.6 39.8 %copy-start.22 = (f32[128,8,2,512]{3,1,2,0:T(8,128)S(1)}, f32[128,8,2,512]{3,1,2,0:T(8,128)}, u32[]{:S(2)}) copy-start(f32[128,8,2,512]{3,1,2,0:T(8,128)} %copy.100) | copy-start | bytes 12582916
  161.6 51.8 %slice-start.2 = ((s8[8388608]{0:T(1024)(128)(4,1)}), s8[4194304]{0:T(1024)(128)(4,1)S(1)}, s32[]{:S(2)}) async-start(s8[8388608]{0:T(1024)(128)(4,1)} %bitcast.144), calls=%async_computation.12 | async-start | bytes 8388608
  207.3 51.0 %slice-start = ((s8[8388608]{0:T(1024)(128)(4,1)}), s8[4194304]{0:T(1024)(128)(4,1)S(1)}, s32[]{:S(2)}) async-start(s8[8388608]{0:T(1024)(128)(4,1)} %bitcast.142), calls=%async_computation.10 | async-start | bytes 8388608
  209.4 160.5 %copy-start.18 = (f32[1024,512]{1,0:T(8,128)}, f32[1024,512]{1,0:T(8,128)S(1)}, u32[]{:S(2)}) copy-start(f32[1024,512]{1,0:T(8,128)S(1)} %get-tuple-element.128) | copy-start | bytes 6291460
  209.4 48.6 %collective-permute-start.1 = (f32[1024,512]{1,0:T(8,128)S(1)}, f32[1024,512]{1,0:T(8,128)S(1)}, u32[]{:S(2)}, u32[]{:S(2)}) collective-permute-start(f32[1024,512]{1,0:T(8,128)S(1)} %get-tuple-element.128), channel_id=1, source_target_pairs={{0,1},{1,0},{2,3},{3,2},{4,5},{5,4},{6,7},{7,6},{8,9},{9,8},{10,11... | collective-permute-start | bytes 6291464 | tf_op jit(solution)/shard_map/ppermute | solution.py:249
  210.9 56.6 %collective-permute-start.2 = (f32[512]{0:T(512)S(1)}, f32[512]{0:T(512)S(1)}, u32[]{:S(2)}, u32[]{:S(2)}) collective-permute-start(f32[512]{0:T(512)S(1)} %copy-done.32), channel_id=1, source_target_pairs={{0,1},{1,0},{2,3},{3,2},{4,5},{5,4},{6,7},{7,6},{8,9},{9,8},{10,11... | collective-permute-start | bytes 6152 | tf_op jit(solution)/shard_map/ppermute | solution.py:249
  211.4 56.1 %collective-permute-start.3 = (f32[512]{0:T(512)S(1)}, f32[512]{0:T(512)S(1)}, u32[]{:S(2)}, u32[]{:S(2)}) collective-permute-start(f32[512]{0:T(512)S(1)} %copy-done.36), channel_id=1, source_target_pairs={{0,1},{1,0},{2,3},{3,2},{4,5},{5,4},{6,7},{7,6},{8,9},{9,8},{10,11... | collective-permute-start | bytes 6152 | tf_op jit(solution)/shard_map/ppermute | solution.py:249
  212.9 45.4 %slice-start.1 = ((s8[8388608]{0:T(1024)(128)(4,1)}), s8[4194304]{0:T(1024)(128)(4,1)S(1)}, s32[]{:S(2)}) async-start(s8[8388608]{0:T(1024)(128)(4,1)} %bitcast.142), calls=%async_computation.11 | async-start | bytes 8388608
  213.0 86.6 %collective-permute-start.5 = (f32[1024,512]{1,0:T(8,128)S(1)}, f32[1024,512]{1,0:T(8,128)S(1)}, u32[]{:S(2)}, u32[]{:S(2)}) collective-permute-start(f32[1024,512]{1,0:T(8,128)S(1)} %bitcast.131), channel_id=1, source_target_pairs={{0,1},{1,0},{2,3},{3,2},{4,5},{5,4},{6,7},{7,6},{8,9},{9,8},{10,11... | collective-permute-start | bytes 6291464 | tf_op jit(solution)/shard_map/ppermute | solution.py:249
  325.4 44.6 %collective-permute-start.6 = (f32[1024,512]{1,0:T(8,128)}, f32[1024,512]{1,0:T(8,128)}, u32[]{:S(2)}, u32[]{:S(2)}) collective-permute-start(f32[1024,512]{1,0:T(8,128)} %fusion.13), channel_id=1, source_target_pairs={{0,1},{1,0},{2,3},{3,2},{4,5},{5,4},{6,7},{7,6},{8,9},{9,8},{10,11... | collective-permute-start | bytes 6291464 | tf_op jit(solution)/shard_map/ppermute | solution.py:249
  387.7 13.1 %copy-start.30 = (f32[1024,512]{1,0:T(8,128)S(1)}, f32[1024,512]{1,0:T(8,128)}, u32[]{:S(2)}) copy-start(f32[1024,512]{1,0:T(8,128)} %copy-done.29) | copy-start | bytes 6291460
  393.7 17.3 %copy-start.7 = (f32[1024,512]{1,0:T(8,128)}, f32[1024,512]{1,0:T(8,128)S(1)}, u32[]{:S(2)}) copy-start(f32[1024,512]{1,0:T(8,128)S(1)} %get-tuple-element.124) | copy-start | bytes 6291460
  393.7 101.6 %copy-start.6 = (f32[1024,512]{1,0:T(8,128)}, f32[1024,512]{1,0:T(8,128)S(1)}, u32[]{:S(2)}) copy-start(f32[1024,512]{1,0:T(8,128)S(1)} %get-tuple-element.123) | copy-start | bytes 6291460
  400.7 10.2 %collective-permute-start.8 = (f32[512,1024]{1,0:T(8,128)S(1)}, f32[512,1024]{1,0:T(8,128)S(1)}, u32[]{:S(2)}, u32[]{:S(2)}) collective-permute-start(f32[512,1024]{1,0:T(8,128)S(1)} %fusion.39), channel_id=1, source_target_pairs={{0,16},{16,0},{1,17},{17,1},{2,18},{18,2},{3,19},{19,3},{4,20},{20... | collective-permute-start | bytes 6291464 | tf_op jit(solution)/shard_map/ppermute | solution.py:408
  410.5 7.6 collective-permute-start.9
  416.3 421.1 %reduce-scatter.6.cloned.1.call-start = ((), (), s32[]{:S(2)}) async-start(), calls=%async_computation.8 | async-start | bytes 4718592 | tf_op jit(solution)/shard_map/reduce_scatter | solution.py:409
  431.6 12.3 %copy-start.8 = (f32[1024,512]{1,0:T(8,128)S(1)}, f32[1024,512]{1,0:T(8,128)}, u32[]{:S(2)}) copy-start(f32[1024,512]{1,0:T(8,128)} %copy-done.7) | copy-start | bytes 6291460
  431.6 12.3 %copy-start.23 = (f32[128,8,2,512]{3,1,2,0:T(8,128)S(1)}, f32[128,8,2,512]{3,1,2,0:T(8,128)}, u32[]{:S(2)}) copy-start(f32[128,8,2,512]{3,1,2,0:T(8,128)} %copy.100) | copy-start | bytes 12582916
  443.4 64.0 %collective-permute-start.10 = (f32[512,2048]{1,0:T(8,128)}, f32[512,2048]{1,0:T(8,128)}, u32[]{:S(2)}, u32[]{:S(2)}) collective-permute-start(f32[512,2048]{1,0:T(8,128)} %fusion.33), channel_id=1, source_target_pairs={{0,16},{16,0},{1,17},{17,1},{2,18},{18,2},{3,19},{19,3},{4,20},{20... | collective-permute-start | bytes 12582920 | tf_op jit(solution)/shard_map/ppermute | solution.py:408
  447.6 47.7 %collective-permute-start.7 = (f32[512,1024]{1,0:T(8,128)S(1)}, f32[512,1024]{1,0:T(8,128)S(1)}, u32[]{:S(2)}, u32[]{:S(2)}) collective-permute-start(f32[512,1024]{1,0:T(8,128)S(1)} %fusion.43), channel_id=1, source_target_pairs={{0,1},{1,0},{2,3},{3,2},{4,5},{5,4},{6,7},{7,6},{8,9},{9,8},{10,11... | collective-permute-start | bytes 6291464 | tf_op jit(solution)/shard_map/ppermute | solution.py:249
  500.7 77.9 %all-to-all-start.2 = ((f32[8,64,8,128]{3,2,1,0:T(8,128)}), f32[8,64,8,128]{3,2,1,0:T(8,128)}, u32[]{:S(2)}, u32[]{:S(2)}) async-start(f32[8,64,8,128]{3,2,1,0:T(8,128)} %bitcast.147), calls=%async_computation.2 | async-start | bytes 4194304 | tf_op jit(solution)/shard_map/all_to_all | solution.py:252
  507.3 330.0 %reduce-scatter.8.cloned.1.call-start = ((), (), s32[]{:S(2)}) async-start(), calls=%async_computation.9 | async-start | bytes 4718592 | tf_op jit(solution)/shard_map/reduce_scatter | solution.py:409
  530.7 230.3 %collective-permute-start.4 = (f32[1024,512]{1,0:T(8,128)}, f32[1024,512]{1,0:T(8,128)}, u32[]{:S(2)}, u32[]{:S(2)}) collective-permute-start(f32[1024,512]{1,0:T(8,128)} %fusion.11), channel_id=1, source_target_pairs={{0,1},{1,0},{2,3},{3,2},{4,5},{5,4},{6,7},{7,6},{8,9},{9,8},{10,11... | collective-permute-start | bytes 6291464 | tf_op jit(solution)/shard_map/ppermute | solution.py:249
  531.9 46.7 %copy-start.3 = (f32[8,64,8,128]{3,2,1,0:T(8,128)S(1)}, f32[8,64,8,128]{3,2,1,0:T(8,128)}, u32[]{:S(2)}) copy-start(f32[8,64,8,128]{3,2,1,0:T(8,128)} %copy-done.2) | copy-start | bytes 6291460
  652.9 108.1 %copy-start.20 = (f32[1024,512]{1,0:T(8,128)S(1)}, f32[1024,512]{1,0:T(8,128)}, u32[]{:S(2)}) copy-start(f32[1024,512]{1,0:T(8,128)} %copy-done.18) | copy-start | bytes 6291460
  652.9 108.2 %copy-start.38 = (f32[512]{0:T(512)S(1)}, f32[512]{0:T(512)}, u32[]{:S(2)}) copy-start(f32[512]{0:T(512)} %param.33) | copy-start | bytes 6148
  652.9 167.5 %all-to-all-start.3 = ((f32[8,64,8,128]{3,2,1,0:T(8,128)}), f32[8,64,8,128]{3,2,1,0:T(8,128)}, u32[]{:S(2)}, u32[]{:S(2)}) async-start(f32[8,64,8,128]{3,2,1,0:T(8,128)} %copy-done.5), calls=%async_computation.3 | async-start | bytes 4194304 | tf_op jit(solution)/shard_map/all_to_all | solution.py:252
  (28 other events, 168.9 us)
Sparse Core Ops, SparseCore 0:
  416.4 69.9 reduce-scatter.3
  490.6 123.3 reduce-scatter.5
  618.7 119.2 reduce-scatter.7

commit v2 on v1

v2 whole, which is shorter than its diff:
```python
from functools import partial

import jax
import jax.numpy as jnp
from jax import lax
from jax.experimental import pallas as pl
from jax.experimental.pallas import tpu as pltpu
from jax.sharding import PartitionSpec as P

epsilon = 1e-05
high = lax.Precision.HIGH
highest = lax.Precision.HIGHEST
swap = [(0, 1), (1, 0)]
anywhere = pl.BlockSpec(memory_space=pl.ANY)
window = 30


def tie(values, *earlier):
    def kernel(*refs):
        pass

    return pl.pallas_call(
        kernel,
        in_specs=[anywhere] * (1 + len(earlier)),
        out_specs=anywhere,
        out_shape=jax.ShapeDtypeStruct(values.shape, values.dtype),
        input_output_aliases={0: 0},
        name="tie",
    )(values, *earlier)


def split(values):
    first = values.astype(jnp.bfloat16)
    return (first, (values - first.astype(jnp.float32)).astype(jnp.bfloat16))


def dot(left, right):
    return jnp.dot(left, right, preferred_element_type=jnp.float32)


def contract(left, right, left_dim, right_dim):
    return lax.dot_general(
        left,
        right,
        (((left_dim,), (right_dim,)), ((), ())),
        precision=high,
        preferred_element_type=jnp.float32,
    )


def state_modes(log_step, decay_log, freq, out_coef):
    step = jnp.exp(log_step)[:, None]
    real_rate = -jnp.exp(decay_log)
    scaled_real = step * real_rate
    scaled_imag = step * freq
    minus_real = (
        jnp.expm1(scaled_real) * jnp.cos(scaled_imag) - 2.0 * jnp.sin(0.5 * scaled_imag) ** 2
    )
    minus_imag = jnp.exp(scaled_real) * jnp.sin(scaled_imag)
    modulus = real_rate * real_rate + freq * freq
    ratio_real = (minus_real * real_rate + minus_imag * freq) / modulus
    ratio_imag = (minus_imag * real_rate - minus_real * freq) / modulus
    weight_real = out_coef[0] * ratio_real - out_coef[1] * ratio_imag
    weight_imag = out_coef[0] * ratio_imag + out_coef[1] * ratio_real
    return (weight_real, weight_imag, scaled_real, scaled_imag)


def powers(positions, scaled_real, scaled_imag):
    where = positions[None, None, :]
    magnitude = jnp.exp(where * scaled_real[:, :, None])
    angle = where * scaled_imag[:, :, None]
    return (magnitude * jnp.cos(angle), magnitude * jnp.sin(angle))


def split(values):
    first = values.astype(jnp.bfloat16)
    return (first, (values - first.astype(jnp.float32)).astype(jnp.bfloat16))

def dot(left, right):
    return jnp.dot(left, right, preferred_element_type=jnp.float32)

def toeplitz_pair(line_ref, channel, lag, before, keep, turn):
    size, rows = keep.shape
    out = []
    for step in range(2):
        line = line_ref[channel, pl.ds(lag + step, 1), :]
        now = pltpu.roll(jnp.broadcast_to(line, (size, rows)), turn, 1, stride=1, stride_axis=0)
        out.append(jnp.where(keep, now, before))
        before = now
    high, low = split(jnp.concatenate(out, axis=1))
    return (jnp.concatenate([high, high, low, jnp.zeros_like(low)], axis=0), before)


def half_blocks(values, left):
    size = values.shape[1] // 2
    high = values.astype(jnp.bfloat16).astype(jnp.float32)
    low = values - high
    high_turned, low_turned = pltpu.roll(high, size, 1), pltpu.roll(low, size, 1)
    first = jnp.concatenate([jnp.where(left, high, low_turned), high], axis=1)
    second = jnp.concatenate([jnp.where(left, high_turned, low), high_turned], axis=1)
    return jnp.concatenate([first, second], axis=0).astype(jnp.bfloat16)


def conv_kernel(unit_ref, kernel_ref, table_ref, *rest):
    mixed_ref, slope_ref = rest[-2:]
    groups, block, sequences, rows = unit_ref.shape
    count, half = groups * sequences, rows // 2
    keep = lax.broadcasted_iota(jnp.int32, (half, rows), 1) >= lax.broadcasted_iota(
        jnp.int32, (half, rows), 0
    )
    left = lax.broadcasted_iota(jnp.int32, (count, rows), 1) < half

    def one(channel, carry):
        unit = unit_ref[:, channel].reshape(count, rows)
        gain = table_ref[channel, 0:1, :]
        bias = table_ref[channel, 1:2, :]
        skip = table_ref[channel, 2:3, :]
        normed = unit * gain + bias
        signal = half_blocks(normed, left)
        before = jnp.zeros((half, rows), jnp.float32)
        even, odd = [0.0] * groups, [0.0] * groups
        for lag in range(0, groups, 2):
            table, before = toeplitz_pair(kernel_ref, channel, lag, before, keep, 0)
            part = dot(signal, table)
            for step in range(2):
                lanes = slice(step * rows, (step + 1) * rows)
                for group in range(groups - lag - step):
                    at, to = group * sequences, group + lag + step
                    even[to] += part[at : at + sequences, lanes]
                    odd[to] += part[count + at : count + at + sequences, lanes]
        turned = pltpu.roll(jnp.concatenate(odd, axis=0), half, 1)
        late = jnp.concatenate(
            [jnp.zeros((sequences, rows), jnp.float32), turned[: count - sequences]], axis=0
        )
        inner = (
            jnp.concatenate(even, axis=0) + jnp.where(left, late, turned) + skip * normed
        )
        below = 0.5 + 0.5 * lax.erf(inner * 0.7071067811865476)
        density = 0.3989422804014327 * jnp.exp(-0.5 * inner * inner)
        mixed_ref[:, channel] = (inner * below).reshape(groups, sequences, rows)
        slope_ref[:, channel] = (below + inner * density).reshape(groups, sequences, rows)
        return carry

    lax.fori_loop(0, block, one, 0, unroll=block)


def conv_back_kernel(unit_ref, slope_ref, grad_ref, kernel_ref, table_ref, *rest):
    back_ref, lags_ref, sums_ref, cross_ref = rest[-4:]
    groups, block, sequences, rows = unit_ref.shape
    count, half = groups * sequences, rows // 2
    keep = (
        lax.broadcasted_iota(jnp.int32, (half, rows), 1)
        <= lax.broadcasted_iota(jnp.int32, (half, rows), 0) + half
    )
    left = lax.broadcasted_iota(jnp.int32, (count, rows), 1) < half
    line_at = lax.broadcasted_iota(jnp.int32, (8, rows), 1)
    tile_row = lax.broadcasted_iota(jnp.int32, (8, rows), 0)

    def diagonals(channel, carry):
        lines = [None] * groups
        for tile in range(half // 8):
            turned = []
            for lag in range(groups):
                now = cross_ref[
                    channel,
                    lag // 2,
                    8 * tile : 8 * tile + 8,
                    (lag % 2) * rows : (lag % 2 + 1) * rows,
                ]
                turned.append(pltpu.roll(now, rows - 8 * tile, 1) if tile else now)
            turned.append(jnp.zeros((8, rows), jnp.float32))
            for lag in range(groups):
                now = turned[lag]
                if tile:
                    now = jnp.where(line_at < rows - 8 * tile, now, turned[lag + 1])
                lines[lag] = now if lines[lag] is None else lines[lag] + now
        lines.append(jnp.zeros((8, rows), jnp.float32))
        for lag in range(groups):
            line = lines[lag]
            for bit in (1, 2, 4):
                line = jnp.where(tile_row & bit != 0, pltpu.roll(line, rows - bit, 1), line)
            lines[lag] = line
        for lag in range(groups):
            line = jnp.where(line_at + tile_row < rows, lines[lag], lines[lag + 1])
            lags_ref[channel, lag : lag + 1, :] = jnp.sum(line, axis=0, keepdims=True)
        return carry

    def one(channel, carry):
        unit = unit_ref[:, channel].reshape(count, rows)
        gain = table_ref[channel, 0:1, :]
        bias = table_ref[channel, 1:2, :]
        skip = table_ref[channel, 2:3, :]
        normed = unit * gain + bias
        grad = (grad_ref[:, channel] * slope_ref[:, channel]).reshape(count, rows)
        nothing = jnp.zeros((sequences, rows), jnp.float32)
        signal = half_blocks(grad, left)
        turned = pltpu.roll(grad, half, 1)
        between = jnp.where(
            left, turned, jnp.concatenate([turned[sequences:], nothing], axis=0)
        )
        sides = jnp.concatenate([normed, pltpu.roll(normed, half, 1)], axis=0)
        sides, sides_low = split(sides.T[:half])
        sides = jnp.concatenate([sides, sides_low, sides], axis=1)
        before = jnp.zeros((half, rows), jnp.float32)
        even, odd = [0.0] * groups, [0.0] * groups
        for lag in range(0, groups, 2):
            table, before = toeplitz_pair(kernel_ref, channel, lag, before, keep, half)
            part = dot(signal, table)
            moved = []
            for step in range(2):
                lanes = slice(step * rows, (step + 1) * rows)
                shift = (lag + step) * sequences
                for group in range(groups - lag - step):
                    at = group * sequences + shift
                    even[group] += part[at : at + sequences, lanes]
                    odd[group] += part[count + at : count + at + sequences, lanes]
                pad = [jnp.zeros((shift, rows), jnp.float32)] if shift else []
                moved.append(
                    jnp.concatenate([grad[shift:], *pad, between[shift:], *pad], axis=0)
                )
            right, right_low = split(jnp.concatenate(moved, axis=1))
            cross_ref[channel, lag // 2] = dot(
                sides, jnp.concatenate([right, right, right_low], axis=0)
            )
        turned = pltpu.roll(jnp.concatenate(even, axis=0), half, 1)
        early = jnp.concatenate([turned[sequences:], nothing], axis=0)
        total = jnp.concatenate(odd, axis=0) + jnp.where(left, turned, early) + skip * grad
        back_ref[:, channel] = (total * gain).reshape(groups, sequences, rows)
        sums_ref[channel, 0:1, :] = jnp.sum(total * unit, axis=0, keepdims=True)
        sums_ref[channel, 1:2, :] = jnp.sum(total, axis=0, keepdims=True)
        sums_ref[channel, 2:3, :] = jnp.sum(grad * normed, axis=0, keepdims=True)
        sums_ref[channel, 3:8, :] = jnp.zeros((5, rows), jnp.float32)
        return carry

    lax.fori_loop(0, block, one, 0, unroll=min(4, block))
    lax.fori_loop(0, block, diagonals, 0, unroll=min(2, block))


def channel_blocks(groups, part):
    block = max(1, 64 // groups)
    return block if part % block == 0 else 1


def long_conv(unit, kernel, table, tokens):
    groups, part, sequences, rows = unit.shape
    block = channel_blocks(groups, part)
    wide = pl.BlockSpec((groups, block, sequences, rows), lambda i: (0, i, 0, 0))
    return pl.pallas_call(
        conv_kernel,
        grid=(part // block,),
        in_specs=[
            wide,
            pl.BlockSpec((block, groups, rows), lambda i: (i, 0, 0)),
            pl.BlockSpec((block, 8, rows), lambda i: (i, 0, 0)),
        ]
        + [anywhere] * len(tokens),
        out_specs=[wide, wide],
        out_shape=[jax.ShapeDtypeStruct(unit.shape, jnp.float32)] * 2,
        compiler_params=pltpu.CompilerParams(vmem_limit_bytes=48 * 1024 * 1024),
        cost_estimate=pl.CostEstimate(
            flops=part * groups * groups * sequences * rows * rows * 6 * window,
            bytes_accessed=12 * unit.size,
            transcendentals=2 * unit.size,
        ),
        name="conv_forward",
    )(unit, kernel, table, *tokens)

def long_conv_back(unit, slope, grad, kernel, table, tokens):
    groups, part, sequences, rows = unit.shape
    block = channel_blocks(groups, part)
    wide = pl.BlockSpec((groups, block, sequences, rows), lambda i: (0, i, 0, 0))
    lags = pl.BlockSpec((block, groups, rows), lambda i: (i, 0, 0))
    few = pl.BlockSpec((block, 8, rows), lambda i: (i, 0, 0))
    return pl.pallas_call(
        conv_back_kernel,
        grid=(part // block,),
        in_specs=[wide, wide, wide, lags, few] + [anywhere] * len(tokens),
        out_specs=[wide, lags, few],
        out_shape=[
            jax.ShapeDtypeStruct(unit.shape, jnp.float32),
            jax.ShapeDtypeStruct(kernel.shape, jnp.float32),
            jax.ShapeDtypeStruct((part, 8, rows), jnp.float32),
        ],
        scratch_shapes=[pltpu.VMEM((block, groups // 2, rows // 2, 2 * rows), jnp.float32)],
        compiler_params=pltpu.CompilerParams(vmem_limit_bytes=48 * 1024 * 1024),
        cost_estimate=pl.CostEstimate(
            flops=part * groups * groups * sequences * rows * rows * 12 * window,
            bytes_accessed=16 * unit.size,
            transcendentals=0,
        ),
        name="conv_backward",
    )(unit, slope, grad, kernel, table, *tokens)


def turned_dot(left, right):
    return lax.dot_general(
        left, right, (((1,), (1,)), ((), ())), preferred_element_type=jnp.float32
    )


def feed_forward_kernel(
    index_ref, resid_ref, other_ref, norm_ref, weight_ref, line_ref, back_ref, *rest
):
    (
        hidden_ref,
        grad_ref,
        keep_ref,
        send_ref,
        unit_ref,
        kept_ref,
        sums_ref,
        bias_ref,
        sent_ref,
        high_ref,
        low_ref,
        total_ref,
    ) = rest[-12:]
    count, channels = resid_ref.shape
    step = pl.program_id(0)
    own_at = pl.ds(pl.multiple_of(index_ref[0] * channels, channels), channels)
    other_at = pl.ds(pl.multiple_of((1 - index_ref[0]) * channels, channels), channels)

    @pl.when(step == 0)
    def _():
        resid, other = resid_ref[...], other_ref[...]
        width = 2.0 * channels
        mean = (
            jnp.sum(resid, axis=1, keepdims=True) + jnp.sum(other, axis=1, keepdims=True)
        ) / width
        squares = jnp.sum(resid * resid, axis=1, keepdims=True) + jnp.sum(
            other * other, axis=1, keepdims=True
        )
        scale = lax.rsqrt(squares / width - mean * mean + epsilon)
        lane = lax.broadcasted_iota(jnp.int32, (count, 128), 1)
        sums_ref[...] = jnp.where(lane == 2, scale, 0.0)
        total_ref[...] = jnp.zeros(total_ref.shape, jnp.float32)
        unit = (resid - mean) * scale
        unit_ref[...] = unit
        same = index_ref[1] == 1
        for values, at, first in (
            (unit, own_at, same),
            ((other - mean) * scale, other_at, jnp.logical_not(same)),
        ):
            normed = values * norm_ref[0:1, at] + norm_ref[1:2, at]
            high, low = split(normed)
            high_ref[:, at] = high
            low_ref[:, at] = low

            @pl.when(first)
            def _():
                keep_ref[...] = normed.T

            @pl.when(jnp.logical_not(first))
            def _():
                send_ref[...] = normed.T

    weight, weight_low = split(weight_ref[...])
    size = weight.shape[1]
    total = jnp.zeros((8, size), jnp.float32)
    chunk = min(count, 256)
    for start in range(0, count, chunk):
        at = slice(start, start + chunk)
        high, low = high_ref[at], low_ref[at]
        pre = dot(high, weight) + dot(low, weight) + dot(high, weight_low) + line_ref[0:1]
        below = 0.5 + 0.5 * lax.erf(pre * 0.7071067811865476)
        density = 0.3989422804014327 * jnp.exp(-0.5 * pre * pre)
        hidden_ref[at] = pre * below
        grad = back_ref[at] * (below + pre * density)
        grad_ref[at] = grad
        total = total + jnp.sum(grad.reshape(chunk // 8, 8, size), axis=0)
        first = jnp.sum(grad * line_ref[1:2], axis=1, keepdims=True)
        second = jnp.sum(grad * (pre - line_ref[2:3]), axis=1, keepdims=True)
        lane = lax.broadcasted_iota(jnp.int32, (chunk, 128), 1)
        sums_ref[at] += jnp.where(lane == 0, first, jnp.where(lane == 1, second, 0.0))
        high, low = split(grad)
        total_ref[at] += (
            turned_dot(high, weight) + turned_dot(low, weight) + turned_dot(high, weight_low)
        )
    bias_ref[...] = total

    @pl.when(step == pl.num_programs(0) - 1)
    def _():
        kept_ref[...] = total_ref[:, own_at]
        sent_ref[...] = total_ref[:, other_at]


def feed_forward(index, resid, other, norm, weight, lines, back, held, tokens, place, spans):
    count, channels = resid.shape
    width, hidden = weight.shape
    size = min(512, hidden)
    full = spans * count
    held = list(held)

    def whole(j, c):
        return (0, 0)

    wide = pl.BlockSpec((count, size), lambda j, c: (place, j))
    narrow = pl.BlockSpec((count, channels), whole)
    turned = pl.BlockSpec((channels, count), lambda j, c: (0, place))
    spot = pl.BlockSpec((count, channels), lambda j, c: (place, 0))
    return pl.pallas_call(
        feed_forward_kernel,
        grid_spec=pltpu.PrefetchScalarGridSpec(
            num_scalar_prefetch=1,
            grid=(hidden // size,),
            in_specs=[
                narrow,
                narrow,
                pl.BlockSpec((8, width), whole),
                pl.BlockSpec((width, size), lambda j, c: (0, j)),
                pl.BlockSpec((8, size), lambda j, c: (0, j)),
                wide,
            ]
            + [anywhere] * (len(held) + len(tokens)),
            out_specs=[
                wide,
                wide,
                turned,
                turned,
                spot,
                spot,
                pl.BlockSpec((count, 128), whole),
                pl.BlockSpec((8, size), lambda j, c: (0, j)),
                narrow,
            ],
            scratch_shapes=[
                pltpu.VMEM((count, width), jnp.bfloat16),
                pltpu.VMEM((count, width), jnp.bfloat16),
                pltpu.VMEM((count, width), jnp.float32),
            ],
        ),
        out_shape=[
            jax.ShapeDtypeStruct(shape, jnp.float32)
            for shape in (
                (full, hidden),
                (full, hidden),
                (channels, full),
                (channels, full),
                (full, channels),
                (full, channels),
                (count, 128),
                (8, hidden),
                (count, channels),
            )
        ],
        input_output_aliases={7 + i: i for i in range(len(held))},
        compiler_params=pltpu.CompilerParams(vmem_limit_bytes=56 * 1024 * 1024),
        cost_estimate=pl.CostEstimate(
            flops=count * width * hidden * 12 * window,
            bytes_accessed=4 * (width * hidden + 3 * count * hidden + 8 * count * channels),
            transcendentals=2 * count * hidden,
        ),
        name="feed_forward",
    )(index, resid, other, norm, weight, lines, back, *held, *tokens)


def weight_kernel(rows, turns, index_ref, keep_ref, send_ref, right_ref, *rest):
    high_ref, low_ref = rest[-2:]
    kept_ref, *sent_refs = rest[-3 - turns : -2]
    size = keep_ref.shape[0]
    turn = pl.program_id(0)

    @pl.when(turn == 0)
    def _():
        for at, ref in ((0, send_ref), (size, keep_ref)):
            high, low = split(ref[...])
            high_ref[at : at + size] = high
            low_ref[at : at + size] = low

    right, right_low = split(right_ref[...])
    chunk = min(size, 256)

    def parts(at, ref):
        for start in range(0, size, chunk):
            rows_at = slice(at + start, at + start + chunk)
            left, left_low = high_ref[rows_at], low_ref[rows_at]
            part = dot(left, right) + dot(left_low, right) + dot(left, right_low)
            for first in range(0, chunk, rows):
                block = (start + first) // rows
                stays = (block % 2 == index_ref[2]).astype(jnp.int32)
                to = pl.multiple_of(stays * (size // 2) + block // 2 * rows, rows)
                ref[pl.ds(to, rows)] = part[first : first + rows]

    parts(size, kept_ref)
    for piece in range(turns):

        @pl.when(turn == piece)
        def _():
            parts(0, sent_refs[piece])


def weight_grad(index, groups, keep, send, right, tokens):
    size, depth = keep.shape
    columns = right.shape[1]
    block = min(512, columns)
    turns = columns // block
    whole = pl.BlockSpec((size, depth), lambda j, c: (0, 0))
    kept, *sent = pl.pallas_call(
        partial(weight_kernel, size // groups, turns),
        grid_spec=pltpu.PrefetchScalarGridSpec(
            num_scalar_prefetch=1,
            grid=(turns,),
            in_specs=[whole, whole, pl.BlockSpec((depth, block), lambda j, c: (0, j))]
            + [anywhere] * len(tokens),
            out_specs=[pl.BlockSpec((size, block), lambda j, c: (0, j))]
            + [pl.BlockSpec((size, block), lambda j, c: (0, 0))] * turns,
            scratch_shapes=[pltpu.VMEM((2 * size, depth), jnp.bfloat16)] * 2,
        ),
        out_shape=[jax.ShapeDtypeStruct((size, columns), jnp.float32)]
        + [jax.ShapeDtypeStruct((size, block), jnp.float32)] * turns,
        compiler_params=pltpu.CompilerParams(vmem_limit_bytes=56 * 1024 * 1024),
        cost_estimate=pl.CostEstimate(
            flops=12 * window * size * depth * columns,
            bytes_accessed=4 * (2 * size * depth + depth * columns + 2 * size * columns),
            transcendentals=0,
        ),
        name="weight_gradient",
    )(index, keep, send, right, *tokens)
    return (kept, sent)


def glu_back_kernel(spans, index_ref, keep_ref, unit_ref, norm_ref, grad_ref, weight_ref, *rest):
    by_span = [rest[i * spans : (i + 1) * spans] for i in range(5)]
    out = rest[-(7 + spans) :]
    resid_ref, both_ref, kept_ref, gain_ref, bias_ref = out[:5]
    sent_refs = out[5 : 5 + spans]
    high_ref, low_ref = out[5 + spans :]
    full, channels = keep_ref.shape
    count = full // spans
    width = 2.0 * channels

    @pl.when(pl.program_id(0) == 0)
    def _():
        chunk = min(count, 128)
        gains = jnp.zeros((8, channels), jnp.float32)
        biases, value_sums, gate_sums, grad_sums = gains, gains, gains, gains

        def fold(values):
            return jnp.sum(values.reshape(chunk // 8, 8, channels), axis=0)

        for start in range(0, full, chunk):
            at = slice(start, start + chunk)
            span, local = start // count, slice(start % count, start % count + chunk)
            other, own_sums, other_sums, value, gate = [refs[span][local] for refs in by_span]
            grad_normed = keep_ref[at] + other
            sums = own_sums + other_sums
            total, along, scale = sums[:, 0:1], sums[:, 1:2], own_sums[:, 2:3]
            unit = unit_ref[at]
            grad_resid = grad_ref[at] + scale * (
                grad_normed * norm_ref[0:1] - total / width - unit * (along / width)
            )
            resid_ref[at] = grad_resid
            grad_value = grad_resid * gate
            grad_gate = grad_value * value * (1.0 - gate)
            gains = gains + fold(grad_normed * unit)
            biases = biases + fold(grad_normed)
            value_sums = value_sums + fold(grad_value)
            gate_sums = gate_sums + fold(grad_gate)
            grad_sums = grad_sums + fold(grad_ref[at])
            for first, values in ((0, grad_value), (channels, grad_gate)):
                lanes = slice(first, first + channels)
                both_ref[at, lanes] = values
                high, low = split(values)
                high_ref[at, lanes] = high
                low_ref[at, lanes] = low
        gain_ref[:, :channels] = gains
        gain_ref[:, channels : 2 * channels] = biases
        gain_ref[:, 2 * channels :] = grad_sums
        bias_ref[:, :channels] = value_sums
        bias_ref[:, channels:] = gate_sums

    weight, weight_low = split(weight_ref[...])
    sending = pl.program_id(0) < pl.num_programs(0) // 2
    for span in range(spans):
        at = slice(span * count, (span + 1) * count)
        high = high_ref[at]
        mixed = (
            turned_dot(weight, high) + turned_dot(weight, low_ref[at]) + turned_dot(weight_low, high)
        )

        @pl.when(sending)
        def _():
            sent_refs[span][...] = mixed

        @pl.when(jnp.logical_not(sending))
        def _():
            kept_ref[:, at] = mixed


def glu_back(index, keep, unit, norm, grad, weight, others, sums, other_sums, values, gates, tokens):
    full, channels = keep.shape
    width, columns = weight.shape
    spans = len(others)
    count = full // spans
    block = min(256, channels)
    turns = channels // block

    def whole(j, c):
        return (0, 0)

    def rows_at(j, c):
        return (jnp.where(j < turns, (1 - c[0]) * turns + j, (c[0] - 1) * turns + j), 0)

    wide = pl.BlockSpec((full, channels), whole)
    span_wide = pl.BlockSpec((count, channels), whole)
    span_few = pl.BlockSpec((count, 128), whole)
    few = pl.BlockSpec((8, columns), whole)
    return pl.pallas_call(
        partial(glu_back_kernel, spans),
        grid_spec=pltpu.PrefetchScalarGridSpec(
            num_scalar_prefetch=1,
            grid=(2 * turns,),
            in_specs=[wide, wide, pl.BlockSpec((8, channels), whole), wide]
            + [pl.BlockSpec((block, columns), rows_at)]
            + ([span_wide] * spans + [span_few] * (2 * spans) + [span_wide] * (2 * spans))
            + [anywhere] * len(tokens),
            out_specs=[
                wide,
                pl.BlockSpec((full, columns), whole),
                pl.BlockSpec((block, full), lambda j, c: (jnp.maximum(j - turns, 0), 0)),
                pl.BlockSpec((8, 3 * channels), whole),
                few,
            ]
            + [pl.BlockSpec((block, count), lambda j, c: (jnp.minimum(j, turns - 1), 0))] * spans,
            scratch_shapes=[pltpu.VMEM((full, columns), jnp.bfloat16)] * 2,
        ),
        out_shape=[
            jax.ShapeDtypeStruct(shape, jnp.float32)
            for shape in (
                (full, channels),
                (full, columns),
                (channels, full),
                (8, 3 * channels),
                (8, columns),
            )
            + ((channels, count),) * spans
        ],
        compiler_params=pltpu.CompilerParams(vmem_limit_bytes=60 * 1024 * 1024),
        cost_estimate=pl.CostEstimate(
            flops=6 * window * full * width * columns,
            bytes_accessed=4 * (11 * full * channels + width * columns),
            transcendentals=0,
        ),
        name="glu_backward",
    )(
        index,
        keep,
        unit,
        norm,
        grad,
        weight,
        *others,
        *sums,
        *other_sums,
        *values,
        *gates,
        *tokens,
    )


def body(
    inputs,
    cotangent,
    norm1_gain,
    norm1_bias,
    log_step,
    decay_log,
    freq,
    out_coef,
    skip,
    glu_weight,
    glu_bias,
    norm2_gain,
    norm2_bias,
    ffn_in,
    ffn_in_bias,
    ffn_out,
    ffn_out_bias,
):
    sequences, rows, channels = inputs.shape
    groups = lax.axis_size("seq")
    seq_index = lax.axis_index("seq")
    chan_index = lax.axis_index("chan")
    dp_index = lax.axis_index("dp")
    width = channels * lax.axis_size("chan")
    count = sequences * rows
    part = channels // groups
    steps = [1 << bit for bit in range(groups.bit_length() - 1)]
    bands = 2
    band = channels // bands
    share = part // bands
    spans = 2
    span = count // spans
    spots = [slice(i * span, (i + 1) * span) for i in range(spans)]

    def to_chan(values):
        return lax.ppermute(values, "chan", swap)

    def to_seq(values, step):
        return lax.ppermute(values, "seq", [(a, a ^ step) for a in range(groups)])

    def spread(values):
        return lax.all_to_all(values, "seq", 0, 0, tiled=True)

    def own_part(values, dim):
        pieces = [
            lax.dynamic_slice_in_dim(values, i * band + seq_index * share, share, dim)
            for i in range(bands)
        ]
        return jnp.concatenate(pieces, axis=dim)

    def in_order(own, other):
        first = chan_index == 0
        return jnp.concatenate(
            [jnp.where(first, own, other), jnp.where(first, other, own)], axis=1
        )

    def halve(values, step, *earlier):
        pairs = values.reshape(-1, 2, *values.shape[1:])
        mine = (seq_index & step) // step
        keep = lax.dynamic_index_in_dim(pairs, mine, 1, keepdims=False)
        send = lax.dynamic_index_in_dim(pairs, 1 - mine, 1, keepdims=False)
        got = to_seq(send, step)
        return keep + (tie(got, *earlier) if earlier else got)

    def finish(values, start):
        for step in steps[start:]:
            values = halve(values, step)
        return values[0]

    own_at = chan_index * channels
    other_at = channels - own_at

    flat = inputs.reshape(count, channels)
    grad_out = cotangent.reshape(count, channels)
    stats = jnp.concatenate([jnp.sum(inputs, axis=2), jnp.sum(inputs * inputs, axis=2)], axis=0)
    stats = lax.psum(stats, "chan")
    mean = stats[:sequences] / width
    scale1 = lax.rsqrt(stats[sequences:] / width - mean * mean + epsilon).reshape(count, 1)
    unit1 = (flat - mean.reshape(count, 1)) * scale1
    grad_out_other = to_chan(tie(grad_out, stats))
    same = chan_index == dp_index
    index = jnp.stack([chan_index, same.astype(jnp.int32), seq_index & 1]).astype(jnp.int32)

    def kept_and_sent(own, other):
        return (jnp.where(same, own, other), jnp.where(same, other, own))

    columns_own = lax.dynamic_slice_in_dim(ffn_out, own_at, channels, 1)
    columns_other = lax.dynamic_slice_in_dim(ffn_out, other_at, channels, 1)
    grad_hidden = contract(grad_out, columns_own, 1, 1)
    grad_hidden_own = grad_hidden
    grad_hidden = grad_hidden + contract(grad_out_other, columns_other, 1, 1)
    norms = jnp.stack([norm2_gain, norm2_bias] + [jnp.zeros((channels,), jnp.float32)] * 6)
    norms = in_order(norms, to_chan(tie(norms, grad_out_other)))
    lines = jnp.dot(norms, ffn_in, precision=highest, preferred_element_type=jnp.float32)
    lines = jnp.stack(
        [ffn_in_bias, lines[0], ffn_in_bias + lines[1]] + [jnp.zeros_like(ffn_in_bias)] * 5
    )

    modes, modes_back = jax.vjp(
        state_modes,
        own_part(log_step, 0),
        own_part(decay_log, 0),
        own_part(freq, 0),
        own_part(out_coef, 1),
    )
    weight_real, weight_imag, scaled_real, scaled_imag = modes
    fine_at = jnp.arange(rows, dtype=jnp.int32).astype(jnp.float32)
    coarse_at = (jnp.arange(groups, dtype=jnp.int32) * rows).astype(jnp.float32)
    fine_real, fine_imag = powers(fine_at, scaled_real, scaled_imag)
    coarse_real, coarse_imag = powers(coarse_at, scaled_real, scaled_imag)
    fine = jnp.concatenate([fine_real, fine_imag], axis=1)
    start_real = weight_real[:, :, None] * coarse_real - weight_imag[:, :, None] * coarse_imag
    start_imag = weight_real[:, :, None] * coarse_imag + weight_imag[:, :, None] * coarse_real
    kernel = 2.0 * jnp.einsum(
        "hnd,hnb->hdb",
        jnp.concatenate([start_real, -start_imag], axis=1),
        fine,
        precision=highest,
        preferred_element_type=jnp.float32,
    )
    table = jnp.stack(
        [own_part(norm1_gain, 0), own_part(norm1_bias, 0), own_part(skip, 0)]
        + [jnp.zeros((part,), jnp.float32)] * 5,
        axis=1,
    )
    table = jnp.broadcast_to(table[:, :, None], (part, 8, rows))
    kernel_turned = jnp.roll(kernel[:, :, ::-1], 1, axis=2)
    kernels_turned = [kernel_turned[i * share : (i + 1) * share] for i in range(bands)]
    kernels = [kernel[i * share : (i + 1) * share] for i in range(bands)]
    tables = [table[i * share : (i + 1) * share] for i in range(bands)]

    unit_parts, slope_parts, mixed, mixed_other = [], [], [], []
    for i in range(bands):
        turned = unit1[:, i * band : (i + 1) * band].T.reshape(groups, share, sequences, rows)
        unit_parts.append(spread(tie(turned, kernel, grad_hidden_own) if i else turned))
    for i in range(bands):
        tokens = (grad_hidden, lines) if i else (grad_out_other,)
        mixed_part, slope_part = long_conv(unit_parts[i], kernels[i], tables[i], tokens)
        slope_parts.append(slope_part)
        arrived = spread(mixed_part).reshape(band, count)
        if i:
            arrived = tie(arrived, mixed_other[0])
        mixed.append(arrived)
        mixed_other.append(to_chan(arrived))

    glu_flat = glu_weight.reshape(width, 2 * channels)
    glu_own = lax.dynamic_slice_in_dim(glu_flat, own_at, channels, 0)
    glu_rows_other = lax.dynamic_slice_in_dim(glu_flat, other_at, channels, 0)
    both_held = glu_bias.reshape(1, 2 * channels)
    for i in range(bands):
        both_held = both_held + contract(mixed[i], glu_own[i * band : (i + 1) * band], 0, 0)
    for i in range(bands - 1):
        both_held = both_held + contract(mixed_other[i], glu_rows_other[i * band : (i + 1) * band], 0, 0)
    values, gates, resids, resids_other = [], [], [], []
    for at in spots:
        both = both_held[at] + contract(
            mixed_other[-1][:, at], glu_rows_other[(bands - 1) * band :], 0, 0
        )
        values.append(both[:, :channels])
        gates.append(jax.nn.sigmoid(both[:, channels:]))
        resids.append(flat[at] + values[-1] * gates[-1])
        resids_other.append(to_chan(resids[-1]))

    grad_out_turned = [v.T for v in kept_and_sent(grad_out, tie(grad_out_other, resids[1]))]
    mixed_pair = kept_and_sent(
        jnp.concatenate(mixed, axis=0), tie(jnp.concatenate(mixed_other, axis=0), resids[1])
    )
    held, tokens = (), (*grad_out_turned, *mixed_pair, *kernels_turned)
    row_sums, hidden_sums, sent = [], [], []
    for i in range(spans):
        *held, row_sum, hidden_sum, send = feed_forward(
            index, resids[i], resids_other[i], norms, ffn_in, lines, grad_hidden, held, tokens, i, spans
        )
        tokens = ()
        row_sums.append(row_sum)
        hidden_sums.append(hidden_sum)
        sent.append(send)
    hidden, grad_pre, normed_keep, normed_send, units, kept = held
    arrived = [to_chan(v) for v in sent]
    other_sums = [to_chan(v) for v in row_sums]

    def to_dp(values):
        return lax.ppermute(values, "dp", swap)

    def ready(keep, others, first, last):
        half, size = keep.shape[0] // 2, others[0].shape[1]
        other = jnp.concatenate([v[:half] for v in others[first:last]], axis=1)
        total = keep[:half, first * size : last * size] + other
        return total.reshape(groups // 2, -1, total.shape[1])

    def joined(keep, others, got, first, last):
        half, size = keep.shape[0] // 2, others[0].shape[1]
        other = jnp.concatenate([v[half:] for v in others[first:last]], axis=1)
        return (keep[half:, first * size : last * size] + other).reshape(got.shape) + got

    out_keep, out_send = weight_grad(
        index, groups, *grad_out_turned, hidden, (sent[1], arrived[0], other_sums[0])
    )
    out_other = [to_dp(v) for v in out_send]
    pieces = len(out_other)
    middle, late = pieces // 2, pieces - pieces // 4
    out_keep = tie(out_keep, arrived[1], other_sums[1])
    out_ready = [
        ready(out_keep, out_other, 0, middle),
        ready(out_keep, out_other, middle, pieces),
    ]

    grad_resid, grad_both, mixed_kept, norm_sums, glu_sums, *mixed_sent = glu_back(
        index,
        kept,
        units,
        jnp.broadcast_to(norm2_gain, (8, channels)),
        grad_out,
        glu_flat,
        arrived,
        row_sums,
        other_sums,
        values,
        gates,
        out_ready,
    )
    out_got = [to_seq(v, steps[0]) for v in out_ready]
    out_first = joined(out_keep, out_other, tie(out_got[0], mixed_sent[1]), 0, middle)
    in_keep, in_send = weight_grad(
        index, groups, normed_keep, normed_send, grad_pre, (mixed_sent[1], out_first)
    )
    in_other = [to_dp(v) for v in in_send]

    few = sequences // spans
    spread_spans = []
    tokens = (in_send[0],)
    for i, at in enumerate(spots):
        total = mixed_kept[:, at] + tie(to_chan(mixed_sent[i]), *tokens)
        moved = total.reshape(bands, groups, share, few, rows)
        spread_spans.append(lax.all_to_all(moved, "seq", 1, 1, tiled=True))
        if not i:
            out_second = joined(out_keep, out_other, tie(out_got[1], moved), middle, pieces)
            glu_keep, glu_send = weight_grad(
                index, groups, *mixed_pair, grad_both, (moved, out_second)
            )
            glu_other = [to_dp(v) for v in glu_send]
            in_keep = tie(in_keep, glu_send[0])
            in_ready = [
                ready(in_keep, in_other, 0, late),
                ready(in_keep, in_other, late, pieces),
            ]
            tokens = (*in_ready, spread_spans[0])
    grad_parts = jnp.concatenate(spread_spans, axis=3)
    hidden = tie(hidden, out_keep, moved)
    output_send = contract(hidden, columns_other, 1, 0)
    glu_keep = tie(glu_keep, output_send)
    glu_ready = ready(glu_keep, glu_other, 0, len(glu_other))
    in_got = [to_seq(v, steps[0]) for v in in_ready]
    out_half = jnp.concatenate([out_first, out_second], axis=2)
    out_more = halve(out_half, steps[1], output_send)
    in_first = joined(in_keep, in_other, tie(in_got[0], output_send), 0, late)
    glu_got = to_seq(glu_ready, steps[0])
    backs, grad_kernels, conv_sums = [], [], []
    for i in range(bands):
        if i:
            in_second = joined(in_keep, in_other, tie(in_got[1], backs[0][0]), late, pieces)
            out_most = halve(out_more, steps[2], backs[0][0]) if len(steps) > 2 else out_more
            tokens = (in_second, out_most)
        else:
            tokens = (glu_ready, in_first, out_more)
        back, grad_kernel, conv_sum = long_conv_back(
            unit_parts[i], slope_parts[i], grad_parts[i], kernels_turned[i], tables[i], tokens
        )
        if i:
            back = tie(back, backs[0][1])
            hidden = tie(hidden, output_send, back)
            output_keep = contract(hidden, columns_own, 1, 0)
            output = to_chan(output_send) + (
                output_keep + jnp.concatenate(resids, axis=0) + ffn_out_bias
            )
            glu_half = joined(glu_keep, glu_other, tie(glu_got, output_keep), 0, len(glu_other))
            in_more = halve(
                jnp.concatenate([in_first, in_second], axis=2), steps[1], output_keep
            )
        backs.append((back, spread(back).reshape(band, count)))
        grad_kernels.append(grad_kernel)
        conv_sums.append(conv_sum)
    backs = [v[1] for v in backs]
    scaled = jnp.concatenate([v.T for v in backs], axis=1)
    sums = jnp.stack([jnp.sum(scaled, axis=1), jnp.sum(scaled * unit1, axis=1)])
    sums = sums + to_chan(sums)
    total, along = sums[0][:, None], sums[1][:, None]
    grad_inputs = tie(grad_resid, backs[1]) + scale1 * (
        scaled - total / width - unit1 * (along / width)
    )

    grad_kernel = jnp.concatenate(grad_kernels, axis=0)
    pulled = jnp.einsum(
        "hdb,hnb->hnd",
        jnp.concatenate([grad_kernel, grad_kernel * fine_at], axis=1),
        fine,
        precision=highest,
        preferred_element_type=jnp.float32,
    )
    modes_count = freq.shape[1]
    flat_real, flat_imag = pulled[:, :modes_count, :groups], pulled[:, modes_count:, :groups]
    slant_real = pulled[:, :modes_count, groups:] + coarse_at * flat_real
    slant_imag = pulled[:, modes_count:, groups:] + coarse_at * flat_imag
    zero_real = jnp.sum(coarse_real * flat_real - coarse_imag * flat_imag, axis=2)
    zero_imag = jnp.sum(coarse_real * flat_imag + coarse_imag * flat_real, axis=2)
    one_real = jnp.sum(coarse_real * slant_real - coarse_imag * slant_imag, axis=2)
    one_imag = jnp.sum(coarse_real * slant_imag + coarse_imag * slant_real, axis=2)
    grad_step, grad_decay, grad_freq, grad_coef = modes_back(
        (
            2.0 * zero_real,
            -2.0 * zero_imag,
            2.0 * (weight_real * one_real - weight_imag * one_imag),
            -2.0 * (weight_real * one_imag + weight_imag * one_real),
        )
    )
    sums = jnp.sum(jnp.concatenate(conv_sums, axis=0), axis=2)
    states = jnp.concatenate(
        [grad_decay, grad_freq, grad_coef[0], grad_coef[1], sums[:, :3], grad_step[:, None]], axis=1
    )
    locals_flat = jnp.concatenate(
        [
            jnp.sum(glu_sums, axis=0),
            jnp.sum(norm_sums, axis=0),
            jnp.sum(sum(hidden_sums), axis=0),
        ]
    )
    columns = 2 * rows
    own_states = jnp.pad(states, ((0, 0), (0, columns - states.shape[1]))).reshape(-1, rows)
    few = own_states.shape[0]
    smalls = jnp.concatenate([own_states, locals_flat.reshape(-1, rows)], axis=0)
    glu_more = halve(glu_half, steps[1])
    smalls = tie(smalls + to_dp(smalls), backs[1], glu_more)
    smalls = spread(jnp.broadcast_to(smalls, (groups, *smalls.shape)))
    states = smalls[:, :few].reshape(groups, bands, share, columns)
    states = states.swapaxes(0, 1).reshape(channels, columns)
    locals_flat = jnp.sum(smalls[:, few:], axis=0).reshape(-1)
    grad_ffn_out = finish(out_most, 3).T
    grad_ffn_in = finish(in_more, 2)
    grad_glu = finish(glu_more, 2)
    c = channels
    return (
        output.reshape(sequences, rows, channels),
        grad_inputs.reshape(sequences, rows, channels),
        states[:, 4 * modes_count],
        states[:, 4 * modes_count + 1],
        states[:, 4 * modes_count + 3],
        states[:, :modes_count],
        states[:, modes_count : 2 * modes_count],
        jnp.stack(
            [
                states[:, 2 * modes_count : 3 * modes_count],
                states[:, 3 * modes_count : 4 * modes_count],
            ]
        ),
        states[:, 4 * modes_count + 2],
        grad_glu.reshape(-1, 2, channels),
        locals_flat[: 2 * c].reshape(2, c),
        locals_flat[2 * c : 3 * c],
        locals_flat[3 * c : 4 * c],
        grad_ffn_in,
        locals_flat[5 * c :],
        grad_ffn_out,
        locals_flat[4 * c : 5 * c],
    )


def solution(mesh):
    placed = (
        P("dp", "seq", "chan"),
        P("dp", "seq", "chan"),
        P("chan"),
        P("chan"),
        P("chan"),
        P("chan", None),
        P("chan", None),
        P(None, "chan", None),
        P("chan"),
        P(None, None, "chan"),
        P(None, "chan"),
        P("chan"),
        P("chan"),
        P(None, "chan"),
        P("chan"),
        P("chan", None),
        P("chan"),
    )
    return jax.shard_map(
        body,
        mesh=mesh,
        in_specs=placed,
        out_specs=(
            P("dp", "seq", "chan"),
            P("dp", "seq", "chan"),
            P("chan"),
            P("chan"),
            P("chan"),
            P("chan", None),
            P("chan", None),
            P(None, "chan", None),
            P("chan"),
            P(("dp", "seq"), None, "chan"),
            P(None, "chan"),
            P("chan"),
            P("chan"),
            P(("dp", "seq"), "chan"),
            P("chan"),
            P("chan", ("dp", "seq")),
            P("chan"),
        ),
        check_vma=False,
    )
```

time: 852 us -> 617 us (0.72)
  blocking collectives: 204 us -> 6.53 us
  waiting for transfers between devices: 261 us -> 101 us
  matrix products: 175 us -> 67.6 us
  Pallas kernels: 98.5 us -> 168 us
  local copies, waits for them, and re-layouts: 32.5 us -> 91.6 us
  starting transfers between devices: 26.8 us -> 83.6 us
  other arithmetic: 31.5 us -> 84.4 us
  between operations: 14.9 us -> 2.52 us
    ppermute x8 -> x14, waiting for transfers between devices: 179 us -> 27.4 us  [to_chan(): return lax.ppermute(values, 'chan', swap)]
    pallas_call x0 -> x30, Pallas kernels: none -> 128 us  [the longest x3 55.5 us: weight_grad(): pl.pallas_call(partial(weight_kernel, size // groups, turns), grid_spec=p...]
    psum x5 -> x1, blocking collectives: 121 us -> 6.53 us  [body(): stats = lax.psum(stats, 'chan')]
    dot_general x18 -> x9, matrix products: 170 us -> 57.5 us  [contract(): lax.dot_general(left, right, (((left_dim,), (right_dim,)), ((), ())), pre...]
    all_to_all x1 -> x0, blocking collectives: 51.8 us -> none  [spread(): return lax.all_to_all(values, 'seq', 0, 0, tiled=True)]
    all_to_all x3 -> x7, waiting for transfers between devices: 79.7 us -> 28.9 us  [spread(): return lax.all_to_all(values, 'seq', 0, 0, tiled=True)]
    pallas_call x1 -> x2, Pallas kernels: 72.9 us -> 30.1 us  [long_conv_back(): pl.pallas_call(conv_back_kernel, grid=(part // block,), in_specs=[wide, w...]
    add x1 -> x21, other arithmetic: 3.63 us -> 36.8 us  [the longest x5 9.95 us: joined(): (keep[half:, first * size:last * size] + other).reshape(got.shape) + got]
  transfers between devices with their start and end apart: 17 -> 45, of which waited for: 8 -> 11; matrix products, arithmetic and copies ran while one was open for 20% -> 34% of each run, Pallas kernels for 9% -> 28%
where the time goes in v2:
time: 617 us; the launch traced here: 605 us
  Pallas kernels  168 us (27%)
  waiting for transfers between devices  101 us (16%)
  local copies, waits for them, and re-layouts  91.6 us (15%)
  other arithmetic  84.4 us (14%)
  starting transfers between devices  83.6 us (14%)
  matrix products  67.6 us (11%)
  blocking collectives  6.53 us (1%)
    dot_general x9, matrix products, contract(): lax.dot_general(left, right, (((left_dim,), (right_dim,)), ((), ())), pre...  57.5 us
    pallas_call x3, Pallas kernels, weight_grad(): pl.pallas_call(partial(weight_kernel, size // groups, turns), grid_spec=p...  55.5 us
    pallas_call x2, Pallas kernels, feed_forward(): pl.pallas_call(feed_forward_kernel, grid_spec=pltpu.PrefetchScalarGridSpe...  52.5 us
    unnamed x264, local copies, waits for them, and re-layouts  42 us
    all_to_all x7, starting transfers between devices, spread(): return lax.all_to_all(values, 'seq', 0, 0, tiled=True)  35.4 us
    pallas_call x2, Pallas kernels, long_conv_back(): pl.pallas_call(conv_back_kernel, grid=(part // block,), in_specs=[wide, w...  30.1 us
    all_to_all x7, waiting for transfers between devices, spread(): return lax.all_to_all(values, 'seq', 0, 0, tiled=True)  28.9 us
    ppermute x14, waiting for transfers between devices, to_chan(): return lax.ppermute(values, 'chan', swap)  27.4 us
  transfers between devices with their start and end apart: 45, of which 11 were waited for; matrix products, arithmetic and copies ran while one was open for 34% of the time, Pallas kernels for 28%

profile of v2, /device:TPU:0, one launch (start us, length us, event | category | flops | bytes accessed | tf_op | source)
XLA Modules:
  0.0 605.2 jit_solution(4600656462083608694)
XLA Ops:
  2.8 6.5 %psum.7.refs_1_ = f32[16,128]{1,0:T(8,128)} all-reduce(f32[16,128]{1,0:T(8,128)S(1)} %pad_maximum_fusion.15), channel_id=1, replica_groups=mesh['dp'=2,'seq'=8,'chan'=2] {'chan'}, use_global_device_ids=true, to_apply=%region_2.0 | all-reduce | flops 2048 | bytes 16384 | tf_op jit(solution)/shard_map/psum | solution.py:737
  20.4 5.8 all-to-all-start
  40.5 10.7 %convolution_bitcast_fusion.refs_2_ = f32[1024,2048]{1,0:T(8,128)} fusion(f32[1024,512]{1,0:T(8,128)S(1)} %bitcast.199, f32[2048,1024]{1,0:T(8,128)} %param.32, s32[]{:T(128)S(6)} %select_n.100), kind=kOutput, calls=%fused_computation | convolution fusion | flops 6442450944 | bytes 14680068 | tf_op jit(solution)/shard_map/dot_general | solution.py:42
  60.4 5.8 all-to-all-start.2
  66.4 4.6 conv_forward.2
  71.0 12.7 %fusion.7.rest_0_.back_ref = f32[1024,2048]{1,0:T(8,128)} fusion(f32[1024,2048]{1,0:T(8,128)} %convolution_bitcast_fusion.refs_2_, f32[1024,512]{1,0:T(8,128)S(1)} %copy-done.1, f32[2048,1024]{1,0:T(8,128)} %param.32, s32[]{:T(128)S(6)} %select_n.101), kind=kOutput, calls=%fused_computation.9 | convolution fusion | flops 6444548096 | bytes 23068676 | tf_op jit(solution)/shard_map/dot_general | solution.py:42
  94.3 5.6 conv_forward.3
  101.6 17.2 %all-to-all-done.1 = f32[8,32,8,128]{3,2,1,0:T(8,128)} async-done(((f32[8,32,8,128]{3,2,1,0:T(8,128)}), f32[8,32,8,128]{3,2,1,0:T(8,128)}, u32[]{:S(2)}, u32[]{:S(2)}) %all-to-all-start.1) | async-done | bytes 1048608 | tf_op jit(solution)/shard_map/all_to_all | solution.py:703
  118.8 4.4 all-to-all-start.3
  126.3 5.3 copy.284
  138.8 9.7 %all-to-all-done.3 = f32[8,32,8,128]{3,2,1,0:T(8,128)} async-done(((f32[8,32,8,128]{3,2,1,0:T(8,128)}), f32[8,32,8,128]{3,2,1,0:T(8,128)}, u32[]{:S(2)}, u32[]{:S(2)}) %all-to-all-start.3) | async-done | bytes 1048608 | tf_op jit(solution)/shard_map/all_to_all | solution.py:703
  160.4 13.8 %collective-permute-done.3 = f32[256,1024]{1,0:T(8,128)S(1)} collective-permute-done((f32[256,1024]{1,0:T(8,128)}, f32[256,1024]{1,0:T(8,128)S(1)}, u32[]{:S(2)}, u32[]{:S(2)}) %collective-permute-start.3) | collective-permute-done | bytes 1048608 | tf_op jit(solution)/shard_map/ppermute | solution.py:697
  186.6 4.4 select_bitcast_fusion
  203.7 26.1 %feed_forward.2 = (f32[1024,2048]{1,0:T(8,128)}, f32[1024,2048]{1,0:T(8,128)}, f32[512,1024]{1,0:T(8,128)}, f32[512,1024]{1,0:T(8,128)}, f32[1024,512]{1,0:T(8,1...) custom-call(s32[3]{0:T(128)} %pad_add_fusion.1.index_ref, ...), custom_call_target="tpu_custom_call" | custom-call | flops 386547056640 | bytes 29360128 | tf_op jit(solution)/shard_map/feed_forward/pallas_call | solution.py:401
  231.9 26.4 %feed_forward.3 = (f32[1024,2048]{1,0:T(8,128)}, f32[1024,2048]{1,0:T(8,128)}, f32[512,1024]{1,0:T(8,128)}, f32[512,1024]{1,0:T(8,128)}, f32[1024,512]{1,0:T(8,1...) custom-call(s32[3]{0:T(128)} %pad_add_fusion.1.index_ref, ...), custom_call_target="tpu_custom_call", output_to_operand_aliasing={{0}: (7, {}), {1}: (8, {}), {2}: (9, {}), {3}: (10, {}), {4... | custom-call | flops 386547056640 | bytes 29360128 | tf_op jit(solution)/shard_map/feed_forward/pallas_call | solution.py:401
  259.1 21.3 %weight_gradient.3 = (f32[512,2048]{1,0:T(8,128)}, f32[512,512]{1,0:T(8,128)}, f32[512,512]{1,0:T(8,128)}, f32[512,512]{1,0:T(8,128)}, f32[512,512]{1,0:T(8,128)}) custom-call(s32[3]{0:T(128)} %pad_add_fusion.1.index_ref, f32[512,1024]{1,0:T(8,128)} %copy.233.rest_0_.keep_ref, f32[512,1024]{1,0:T(8,128)} %copy.234.rest_1_.send_ref, ...), custom_call_target="tpu_custom_call" | custom-call | flops 386547056640 | bytes 20971520 | tf_op jit(solution)/shard_map/weight_gradient/pallas_call | solution.py:498
  282.4 7.3 %collective-permute-done.9.refs_2_.rest_5_ = f32[512,128]{1,0:T(8,128)S(1)} collective-permute-done((f32[512,128]{1,0:T(8,128)S(1)}, f32[512,128]{1,0:T(8,128)S(1)}, u32[]{:S(2)}, u32[]{:S(2)}) %collective-permute-start.9) | collective-permute-done | bytes 262176 | tf_op jit(solution)/shard_map/ppermute | solution.py:697
  300.6 20.0 %glu_backward.1 = (f32[1024,512]{1,0:T(8,128)}, f32[1024,1024]{1,0:T(8,128)}, f32[512,1024]{1,0:T(8,128)}, f32[8,1536]{1,0:T(8,128)}, f32[8,1024]{1,0:T(8,128)}, /*index=5*/f32[512,512]{1,0:T(8,128)}, f32[512,512]{1,0:T(8,128)}) custom-call(s32[3]{0:T(128)} %pad_add_fusion.1.index_ref, f32[1024,512]{1,0:T(8,128)} %get-tuple-element.79.keep_ref, ...), custom_call_target="tpu_custom_call" | custom-call | flops 193273528320 | bytes 27262976 | tf_op jit(solution)/shard_map/glu_backward/pallas_call | solution.py:608
  327.2 20.9 %weight_gradient.4 = (f32[512,2048]{1,0:T(8,128)}, f32[512,512]{1,0:T(8,128)}, f32[512,512]{1,0:T(8,128)}, f32[512,512]{1,0:T(8,128)}, f32[512,512]{1,0:T(8,128)}) custom-call(s32[3]{0:T(128)} %pad_add_fusion.1.index_ref, f32[512,1024]{1,0:T(8,128)} %get-tuple-element.87.keep_ref, f32[512,1024]{1,0:T(8,128)} %get-tuple-element.88.send_ref, ...), custom_call_target="tpu_custom_call" | custom-call | flops 386547056640 | bytes 20971520 | tf_op jit(solution)/shard_map/weight_gradient/pallas_call | solution.py:498
  354.8 13.2 %weight_gradient.5 = (f32[512,1024]{1,0:T(8,128)}, f32[512,512]{1,0:T(8,128)}, f32[512,512]{1,0:T(8,128)}) custom-call(s32[3]{0:T(128)} %pad_add_fusion.1.index_ref, f32[512,1024]{1,0:T(8,128)} %get-tuple-element.247.rest_2_.keep_ref, f32[512,1024]{1,0:T(8,128)} %get-tuple-element.246.rest_3_.send_ref, f32[1024,1024]{1,0:T(8,128)} %get-tuple-element.91.right_ref, ...), custom_call_target="tpu_custom_call" | custom-call | flops 193273528320 | bytes 12582912 | tf_op jit(solution)/shard_map/weight_gradient/pallas_call | solution.py:498
  369.7 5.6 all-to-all-start.4
  392.2 9.4 %all-to-all-done.4 = f32[2,8,32,4,128]{4,3,2,0,1:T(4,128)S(1)} async-done(((f32[2,8,32,4,128]{4,3,2,0,1:T(4,128)}), f32[2,8,32,4,128]{4,3,2,0,1:T(4,128)S(1)}, u32[]{:S(2)}, u32[]{:S(2)}) %all-to-all-start.4) | async-done | bytes 1048608 | tf_op jit(solution)/shard_map/all_to_all | solution.py:896
  412.9 11.4 %fusion.refs_1_ = f32[1024,512]{1,0:T(8,128)} fusion(f32[1024,2048]{1,0:T(8,128)} %tie.36.refs_0_, f32[2048,1024]{1,0:T(8,128)} %param.32, s32[]{:T(128)S(6)} %select_n.101), kind=kOutput, calls=%fused_computation.2 | convolution fusion | flops 6442450944 | bytes 14680068 | tf_op jit(solution)/shard_map/dot_general | solution.py:42
  439.5 10.4 %all-to-all-done.5 = f32[2,8,32,4,128]{4,3,2,0,1:T(4,128)} async-done(((f32[2,8,32,4,128]{4,3,2,0,1:T(4,128)}), f32[2,8,32,4,128]{4,3,2,0,1:T(4,128)}, u32[]{:S(2)}, u32[]{:S(2)}) %all-to-all-start.5) | async-done | bytes 1048608 | tf_op jit(solution)/shard_map/all_to_all | solution.py:896
  452.0 14.9 %conv_backward.2 = (f32[8,32,8,128]{3,2,1,0:T(8,128)}, f32[32,8,128]{2,1,0:T(8,128)S(1)}, f32[32,8,128]{2,1,0:T(8,128)S(1)}) custom-call(f32[8,32,8,128]{3,2,1,0:T(8,128)S(1)} %all-to-all-done.unit_ref, f32[8,32,8,128]{3,2,1,0:T(8,128)S(1)} %copy-done.14, f32[8,32,8,128]{3,2,1,0:T(8,128)S(1)} %get-tuple-element.252.grad_ref, f32[32,8,128]{2,1,0:T(8,128)S(1)} %copy-done.9, ...), custom_call_target="tpu_custom_call" | custom-call | flops 96636764160 | bytes 4194304 | tf_op jit(solution)/shard_map/conv_backward/pallas_call | solution.py:274
  475.8 15.2 %conv_backward.3 = (f32[8,32,8,128]{3,2,1,0:T(8,128)S(1)}, f32[32,8,128]{2,1,0:T(8,128)S(1)}, f32[32,8,128]{2,1,0:T(8,128)S(1)}) custom-call(f32[8,32,8,128]{3,2,1,0:T(8,128)} %all-to-all-done.2.unit_ref, f32[8,32,8,128]{3,2,1,0:T(8,128)S(1)} %copy-done.12, f32[8,32,8,128]{3,2,1,0:T(8,128)S(1)} %get-tuple-element.253.grad_ref, f32[32,8,128]{2,1,0:T(8,128)S(1)} %copy-done.8, ...), custom_call_target="tpu_custom_call" | custom-call | flops 96636764160 | bytes 4194304 | tf_op jit(solution)/shard_map/conv_backward/pallas_call | solution.py:274
  504.4 4.7 all-to-all-start.7
  509.2 11.5 %fusion.4.refs_1_ = f32[1024,512]{1,0:T(8,128)} fusion(f32[1024,2048]{1,0:T(8,128)} %tie.43, f32[2048,1024]{1,0:T(8,128)} %param.32, s32[]{:T(128)S(6)} %select_n.100), kind=kOutput, calls=%fused_computation.6 | convolution fusion | flops 6442450944 | bytes 14680068 | tf_op jit(solution)/shard_map/dot_general | solution.py:42
  527.1 8.2 %collective-permute-done.34.refs_0_ = f32[2,64,2048]{2,1,0:T(8,128)} collective-permute-done((f32[2,64,2048]{2,1,0:T(8,128)}, f32[2,64,2048]{2,1,0:T(8,128)}, u32[]{:S(2)}, u32[]{:S(2)}) %collective-permute-start.34) | collective-permute-done | bytes 1048608 | tf_op jit(solution)/shard_map/ppermute | solution.py:700
  538.9 4.7 collective-permute-start.35
  549.6 16.3 %collective-permute-done.32 = f32[2,64,1024]{2,1,0:T(8,128)} collective-permute-done((f32[2,64,1024]{2,1,0:T(8,128)}, f32[2,64,1024]{2,1,0:T(8,128)}, u32[]{:S(2)}, u32[]{:S(2)}) %collective-permute-start.32) | collective-permute-done | bytes 524320 | tf_op jit(solution)/shard_map/ppermute | solution.py:700
  572.7 6.1 %all-to-all-start.8 = ((f32[8,164,128]{2,1,0:T(8,128)}), f32[8,164,128]{2,1,0:T(8,128)}, u32[]{:S(2)}, u32[]{:S(2)}) async-start(f32[8,164,128]{2,1,0:T(8,128)} %broadcast_in_dim.11), calls=%async_computation.8 | async-start | bytes 1376256 | tf_op jit(solution)/shard_map/all_to_all | solution.py:703
  (519 shorter events, 242.2 us)
Async XLA Ops:
  10.6 46.7 %collective-permute-start = (f32[1024,512]{1,0:T(8,128)}, f32[1024,512]{1,0:T(8,128)S(1)}, u32[]{:S(2)}, u32[]{:S(2)}) collective-permute-start(f32[1024,512]{1,0:T(8,128)} %tie.24), channel_id=1, source_target_pairs={{0,1},{1,0},{2,3},{3,2},{4,5},{5,4},{6,7},{7,6},{8,9},{9,8},{10,11... | collective-permute-start | bytes 6291464 | tf_op jit(solution)/shard_map/ppermute | solution.py:697
  20.4 40.0 %all-to-all-start = ((f32[8,32,8,128]{3,2,1,0:T(8,128)}), f32[8,32,8,128]{3,2,1,0:T(8,128)S(1)}, u32[]{:S(2)}, u32[]{:S(2)}) async-start(f32[8,32,8,128]{3,2,1,0:T(8,128)} %bitcast.224), calls=%async_computation | async-start | bytes 2097152 | tf_op jit(solution)/shard_map/all_to_all | solution.py:703
  58.7 25.1 %collective-permute-start.1 = (f32[8,512]{1,0:T(8,128)}, f32[8,512]{1,0:T(8,128)S(1)}, u32[]{:S(2)}, u32[]{:S(2)}) collective-permute-start(f32[8,512]{1,0:T(8,128)} %tie.26), channel_id=1, source_target_pairs={{0,1},{1,0},{2,3},{3,2},{4,5},{5,4},{6,7},{7,6},{8,9},{9,8},{10,11... | collective-permute-start | bytes 49160 | tf_op jit(solution)/shard_map/ppermute | solution.py:697
  60.4 29.5 %all-to-all-start.2 = ((f32[8,32,8,128]{3,2,1,0:T(8,128)}), f32[8,32,8,128]{3,2,1,0:T(8,128)}, u32[]{:S(2)}, u32[]{:S(2)}) async-start(f32[8,32,8,128]{3,2,1,0:T(8,128)} %tie.25), calls=%async_computation.2 | async-start | bytes 2097152 | tf_op jit(solution)/shard_map/all_to_all | solution.py:703
  90.0 28.8 %all-to-all-start.1 = ((f32[8,32,8,128]{3,2,1,0:T(8,128)}), f32[8,32,8,128]{3,2,1,0:T(8,128)}, u32[]{:S(2)}, u32[]{:S(2)}) async-start(f32[8,32,8,128]{3,2,1,0:T(8,128)} %get-tuple-element.65), calls=%async_computation.1 | async-start | bytes 2097152 | tf_op jit(solution)/shard_map/all_to_all | solution.py:703
  118.8 29.7 %all-to-all-start.3 = ((f32[8,32,8,128]{3,2,1,0:T(8,128)}), f32[8,32,8,128]{3,2,1,0:T(8,128)}, u32[]{:S(2)}, u32[]{:S(2)}) async-start(f32[8,32,8,128]{3,2,1,0:T(8,128)} %get-tuple-element.66), calls=%async_computation.3 | async-start | bytes 2097152 | tf_op jit(solution)/shard_map/all_to_all | solution.py:703
  125.6 25.3 %collective-permute-start.2 = (f32[256,1024]{1,0:T(8,128)}, f32[256,1024]{1,0:T(8,128)}, u32[]{:S(2)}, u32[]{:S(2)}) collective-permute-start(f32[256,1024]{1,0:T(8,128)} %bitcast.178), channel_id=1, source_target_pairs={{0,1},{1,0},{2,3},{3,2},{4,5},{5,4},{6,7},{7,6},{8,9},{9,8},{10,11... | collective-permute-start | bytes 3145736 | tf_op jit(solution)/shard_map/ppermute | solution.py:697
  177.3 26.4 %collective-permute-start.5 = (f32[512,512]{1,0:T(8,128)}, f32[512,512]{1,0:T(8,128)}, u32[]{:S(2)}, u32[]{:S(2)}) collective-permute-start(f32[512,512]{1,0:T(8,128)} %get-tuple-element.258.resid_ref), channel_id=1, source_target_pairs={{0,1},{1,0},{2,3},{3,2},{4,5},{5,4},{6,7},{7,6},{8,9},{9,8},{10,11... | collective-permute-start | bytes 3145736 | tf_op jit(solution)/shard_map/ppermute | solution.py:697
  180.9 51.0 %collective-permute-start.4 = (f32[512,512]{1,0:T(8,128)}, f32[512,512]{1,0:T(8,128)}, u32[]{:S(2)}, u32[]{:S(2)}) collective-permute-start(f32[512,512]{1,0:T(8,128)} %get-tuple-element.255.refs_1_.resid_ref), channel_id=1, source_target_pairs={{0,1},{1,0},{2,3},{3,2},{4,5},{5,4},{6,7},{7,6},{8,9},{9,8},{10,11... | collective-permute-start | bytes 3145736 | tf_op jit(solution)/shard_map/ppermute | solution.py:697
  229.8 29.2 %collective-permute-start.6 = (f32[512,512]{1,0:T(8,128)}, f32[512,512]{1,0:T(8,128)}, u32[]{:S(2)}, u32[]{:S(2)}) collective-permute-start(f32[512,512]{1,0:T(8,128)} %get-tuple-element.75), channel_id=1, source_target_pairs={{0,1},{1,0},{2,3},{3,2},{4,5},{5,4},{6,7},{7,6},{8,9},{9,8},{10,11... | collective-permute-start | bytes 3145736 | tf_op jit(solution)/shard_map/ppermute | solution.py:697
  230.5 28.5 %collective-permute-start.7 = (f32[512,128]{1,0:T(8,128)}, f32[512,128]{1,0:T(8,128)}, u32[]{:S(2)}, u32[]{:S(2)}) collective-permute-start(f32[512,128]{1,0:T(8,128)} %get-tuple-element.76.rest_2_), channel_id=1, source_target_pairs={{0,1},{1,0},{2,3},{3,2},{4,5},{5,4},{6,7},{7,6},{8,9},{9,8},{10,11... | collective-permute-start | bytes 786440 | tf_op jit(solution)/shard_map/ppermute | solution.py:697
  258.3 32.0 %collective-permute-start.8 = (f32[512,512]{1,0:T(8,128)}, f32[512,512]{1,0:T(8,128)}, u32[]{:S(2)}, u32[]{:S(2)}) collective-permute-start(f32[512,512]{1,0:T(8,128)} %get-tuple-element.74.rest_0_), channel_id=1, source_target_pairs={{0,1},{1,0},{2,3},{3,2},{4,5},{5,4},{6,7},{7,6},{8,9},{9,8},{10,11... | collective-permute-start | bytes 3145736 | tf_op jit(solution)/shard_map/ppermute | solution.py:697
  297.7 27.1 %collective-permute-start.15 = (f32[4,64,1024]{2,1,0:T(8,128)}, f32[4,64,1024]{2,1,0:T(8,128)}, u32[]{:S(2)}, u32[]{:S(2)}) collective-permute-start(f32[4,64,1024]{2,1,0:T(8,128)} %bitcast.24.rest_10_), channel_id=1, source_target_pairs={{0,2},{2,0},{4,6},{6,4},{8,10},{10,8},{12,14},{14,12},{1,3},{3,1},... | collective-permute-start | bytes 3145736 | tf_op jit(solution)/shard_map/ppermute | solution.py:700
  299.9 51.9 %collective-permute-start.17 = (f32[4,64,1024]{2,1,0:T(8,128)}, f32[4,64,1024]{2,1,0:T(8,128)}, u32[]{:S(2)}, u32[]{:S(2)}) collective-permute-start(f32[4,64,1024]{2,1,0:T(8,128)} %bitcast.25.rest_11_), channel_id=1, source_target_pairs={{0,2},{2,0},{4,6},{6,4},{8,10},{10,8},{12,14},{14,12},{1,3},{3,1},... | collective-permute-start | bytes 3145736 | tf_op jit(solution)/shard_map/ppermute | solution.py:700
  320.6 27.6 %collective-permute-start.16 = (f32[512,512]{1,0:T(8,128)}, f32[512,512]{1,0:T(8,128)}, u32[]{:S(2)}, u32[]{:S(2)}) collective-permute-start(f32[512,512]{1,0:T(8,128)} %get-tuple-element.92), channel_id=1, source_target_pairs={{0,1},{1,0},{2,3},{3,2},{4,5},{5,4},{6,7},{7,6},{8,9},{9,8},{10,11... | collective-permute-start | bytes 3145736 | tf_op jit(solution)/shard_map/ppermute | solution.py:697
  322.0 80.7 %collective-permute-start.14 = (f32[512,512]{1,0:T(8,128)}, f32[512,512]{1,0:T(8,128)}, u32[]{:S(2)}, u32[]{:S(2)}) collective-permute-start(f32[512,512]{1,0:T(8,128)} %get-tuple-element.86.refs_1_.rest_0_), channel_id=1, source_target_pairs={{0,1},{1,0},{2,3},{3,2},{4,5},{5,4},{6,7},{7,6},{8,9},{9,8},{10,11... | collective-permute-start | bytes 3145736 | tf_op jit(solution)/shard_map/ppermute | solution.py:697
  348.2 29.6 %collective-permute-start.18 = (f32[512,512]{1,0:T(8,128)}, f32[512,512]{1,0:T(8,128)}, u32[]{:S(2)}, u32[]{:S(2)}) collective-permute-start(f32[512,512]{1,0:T(8,128)} %get-tuple-element.93.refs_1_), channel_id=1, source_target_pairs={{0,16},{16,0},{1,17},{17,1},{2,18},{18,2},{3,19},{19,3},{4,20},{20... | collective-permute-start | bytes 3145736 | tf_op jit(solution)/shard_map/ppermute | solution.py:844
  351.3 29.8 %collective-permute-start.19 = (f32[512,512]{1,0:T(8,128)}, f32[512,512]{1,0:T(8,128)}, u32[]{:S(2)}, u32[]{:S(2)}) collective-permute-start(f32[512,512]{1,0:T(8,128)} %get-tuple-element.95), channel_id=1, source_target_pairs={{0,16},{16,0},{1,17},{17,1},{2,18},{18,2},{3,19},{19,3},{4,20},{20... | collective-permute-start | bytes 3145736 | tf_op jit(solution)/shard_map/ppermute | solution.py:844
  369.7 32.0 %all-to-all-start.4 = ((f32[2,8,32,4,128]{4,3,2,0,1:T(4,128)}), f32[2,8,32,4,128]{4,3,2,0,1:T(4,128)S(1)}, u32[]{:S(2)}, u32[]{:S(2)}) async-start(f32[2,8,32,4,128]{4,3,2,0,1:T(4,128)} %copy.237), calls=%async_computation.4 | async-start | bytes 2097152 | tf_op jit(solution)/shard_map/all_to_all | solution.py:896
  377.8 48.0 %collective-permute-start.27 = (f32[2,64,2048]{2,1,0:T(8,128)}, f32[2,64,2048]{2,1,0:T(8,128)}, u32[]{:S(2)}, u32[]{:S(2)}) collective-permute-start(f32[2,64,2048]{2,1,0:T(8,128)} %dynamic-slice_bitcast_fusion.1), channel_id=1, source_target_pairs={{0,4},{2,6},{4,0},{6,2},{8,12},{10,14},{12,8},{14,10},{1,5},{3,7},... | collective-permute-start | bytes 3145736 | tf_op jit(solution)/shard_map/ppermute | solution.py:700
  382.6 28.0 %collective-permute-start.25 = (f32[512,512]{1,0:T(8,128)}, f32[512,512]{1,0:T(8,128)}, u32[]{:S(2)}, u32[]{:S(2)}) collective-permute-start(f32[512,512]{1,0:T(8,128)} %get-tuple-element.101), channel_id=1, source_target_pairs={{0,16},{16,0},{1,17},{17,1},{2,18},{18,2},{3,19},{19,3},{4,20},{20... | collective-permute-start | bytes 3145736 | tf_op jit(solution)/shard_map/ppermute | solution.py:844
  386.7 50.0 %collective-permute-start.26 = (f32[4,64,1536]{2,1,0:T(8,128)}, f32[4,64,1536]{2,1,0:T(8,128)}, u32[]{:S(2)}, u32[]{:S(2)}) collective-permute-start(f32[4,64,1536]{2,1,0:T(8,128)} %bitcast.28.refs_1_), channel_id=1, source_target_pairs={{0,2},{2,0},{4,6},{6,4},{8,10},{10,8},{12,14},{14,12},{1,3},{3,1},... | collective-permute-start | bytes 4718600 | tf_op jit(solution)/shard_map/ppermute | solution.py:700
  389.4 81.8 %collective-permute-start.23 = (f32[4,64,512]{2,1,0:T(8,128)}, f32[4,64,512]{2,1,0:T(8,128)}, u32[]{:S(2)}, u32[]{:S(2)}) collective-permute-start(f32[4,64,512]{2,1,0:T(8,128)} %bitcast.29.refs_2_), channel_id=1, source_target_pairs={{0,2},{2,0},{4,6},{6,4},{8,10},{10,8},{12,14},{14,12},{1,3},{3,1},... | collective-permute-start | bytes 1572872 | tf_op jit(solution)/shard_map/ppermute | solution.py:700
  406.4 43.5 %all-to-all-start.5 = ((f32[2,8,32,4,128]{4,3,2,0,1:T(4,128)}), f32[2,8,32,4,128]{4,3,2,0,1:T(4,128)}, u32[]{:S(2)}, u32[]{:S(2)}) async-start(f32[2,8,32,4,128]{4,3,2,0,1:T(4,128)} %copy.239), calls=%async_computation.5 | async-start | bytes 2097152 | tf_op jit(solution)/shard_map/all_to_all | solution.py:896
  424.4 119.3 %collective-permute-start.22 = (f32[1024,512]{1,0:T(8,128)}, f32[1024,512]{1,0:T(8,128)}, u32[]{:S(2)}, u32[]{:S(2)}) collective-permute-start(f32[1024,512]{1,0:T(8,128)} %fusion.refs_1_), channel_id=1, source_target_pairs={{0,1},{1,0},{2,3},{3,2},{4,5},{5,4},{6,7},{7,6},{8,9},{9,8},{10,11... | collective-permute-start | bytes 6291464 | tf_op jit(solution)/shard_map/ppermute | solution.py:697
  430.7 42.3 %collective-permute-start.28 = (f32[1,64,2048]{2,1,0:T(8,128)}, f32[1,64,2048]{2,1,0:T(8,128)}, u32[]{:S(2)}, u32[]{:S(2)}) collective-permute-start(f32[1,64,2048]{2,1,0:T(8,128)} %constant_dynamic-slice_fusion.2), channel_id=1, source_target_pairs={{0,8},{2,10},{4,12},{6,14},{8,0},{10,2},{12,4},{14,6},{1,9},{3,11}... | collective-permute-start | bytes 1572872 | tf_op jit(solution)/shard_map/ppermute | solution.py:700
  435.3 85.4 %collective-permute-start.31 = (f32[4,64,1024]{2,1,0:T(8,128)}, f32[4,64,1024]{2,1,0:T(8,128)}, u32[]{:S(2)}, u32[]{:S(2)}) collective-permute-start(f32[4,64,1024]{2,1,0:T(8,128)} %bitcast.33.rest_0_), channel_id=1, source_target_pairs={{0,2},{2,0},{4,6},{6,4},{8,10},{10,8},{12,14},{14,12},{1,3},{3,1},... | collective-permute-start | bytes 3145736 | tf_op jit(solution)/shard_map/ppermute | solution.py:700
  466.9 36.3 %all-to-all-start.6 = ((f32[8,32,8,128]{3,2,1,0:T(8,128)}), f32[8,32,8,128]{3,2,1,0:T(8,128)S(1)}, u32[]{:S(2)}, u32[]{:S(2)}) async-start(f32[8,32,8,128]{3,2,1,0:T(8,128)} %get-tuple-element.102.refs_1_), calls=%async_computation.6 | async-start | bytes 2097152 | tf_op jit(solution)/shard_map/all_to_all | solution.py:703
  500.6 34.7 %collective-permute-start.34 = (f32[2,64,2048]{2,1,0:T(8,128)}, f32[2,64,2048]{2,1,0:T(8,128)}, u32[]{:S(2)}, u32[]{:S(2)}) collective-permute-start(f32[2,64,2048]{2,1,0:T(8,128)} %dynamic-slice_bitcast_fusion), channel_id=1, source_target_pairs={{0,4},{2,6},{4,0},{6,2},{8,12},{10,14},{12,8},{14,10},{1,5},{3,7},... | collective-permute-start | bytes 3145736 | tf_op jit(solution)/shard_map/ppermute | solution.py:700
  504.4 65.0 %all-to-all-start.7 = ((f32[8,32,8,128]{3,2,1,0:T(8,128)}), f32[8,32,8,128]{3,2,1,0:T(8,128)S(1)}, u32[]{:S(2)}, u32[]{:S(2)}) async-start(f32[8,32,8,128]{3,2,1,0:T(8,128)} %tie.42.refs_2_), calls=%async_computation.7 | async-start | bytes 2097152 | tf_op jit(solution)/shard_map/all_to_all | solution.py:703
  525.0 40.8 %collective-permute-start.32 = (f32[2,64,1024]{2,1,0:T(8,128)}, f32[2,64,1024]{2,1,0:T(8,128)}, u32[]{:S(2)}, u32[]{:S(2)}) collective-permute-start(f32[2,64,1024]{2,1,0:T(8,128)} %dynamic-slice_bitcast_fusion.2), channel_id=1, source_target_pairs={{0,4},{2,6},{4,0},{6,2},{8,12},{10,14},{12,8},{14,10},{1,5},{3,7},... | collective-permute-start | bytes 1572872 | tf_op jit(solution)/shard_map/ppermute | solution.py:700
  538.9 28.6 %collective-permute-start.35 = (f32[1,64,2048]{2,1,0:T(8,128)}, f32[1,64,2048]{2,1,0:T(8,128)}, u32[]{:S(2)}, u32[]{:S(2)}) collective-permute-start(f32[1,64,2048]{2,1,0:T(8,128)} %constant_dynamic-slice_fusion), channel_id=1, source_target_pairs={{0,8},{2,10},{4,12},{6,14},{8,0},{10,2},{12,4},{14,6},{1,9},{3,11}... | collective-permute-start | bytes 1572872 | tf_op jit(solution)/shard_map/ppermute | solution.py:700
  (137 other events, 918.1 us)

commit v3 on v2

--- a/solution.py
+++ b/solution.py
@@ -144,7 +144,8 @@
     lax.fori_loop(0, block, one, 0, unroll=block)
 
 
-def conv_back_kernel(unit_ref, slope_ref, grad_ref, kernel_ref, table_ref, *rest):
+def conv_back_kernel(spans, unit_ref, slope_ref, kernel_ref, table_ref, *rest):
+    grad_refs = rest[:spans]
     back_ref, lags_ref, sums_ref, cross_ref = rest[-4:]
     groups, block, sequences, rows = unit_ref.shape
     count, half = groups * sequences, rows // 2
@@ -191,7 +192,8 @@
         bias = table_ref[channel, 1:2, :]
         skip = table_ref[channel, 2:3, :]
         normed = unit * gain + bias
-        grad = (grad_ref[:, channel] * slope_ref[:, channel]).reshape(count, rows)
+        grad = jnp.concatenate([ref[:, 0, channel] for ref in grad_refs], axis=1)
+        grad = (grad * slope_ref[:, channel]).reshape(count, rows)
         nothing = jnp.zeros((sequences, rows), jnp.float32)
         signal = half_blocks(grad, left)
         turned = pltpu.roll(grad, half, 1)
@@ -265,16 +267,18 @@
         name="conv_forward",
     )(unit, kernel, table, *tokens)
 
-def long_conv_back(unit, slope, grad, kernel, table, tokens):
+def long_conv_back(unit, slope, grads, band, kernel, table, tokens):
     groups, part, sequences, rows = unit.shape
     block = channel_blocks(groups, part)
     wide = pl.BlockSpec((groups, block, sequences, rows), lambda i: (0, i, 0, 0))
     lags = pl.BlockSpec((block, groups, rows), lambda i: (i, 0, 0))
     few = pl.BlockSpec((block, 8, rows), lambda i: (i, 0, 0))
     return pl.pallas_call(
-        conv_back_kernel,
+        partial(conv_back_kernel, len(grads)),
         grid=(part // block,),
-        in_specs=[wide, wide, wide, lags, few] + [anywhere] * len(tokens),
+        in_specs=[wide, wide, lags, few]
+        + [pl.BlockSpec((groups, 1, block, *v.shape[3:]), lambda i: (0, band, i, 0, 0)) for v in grads]
+        + [anywhere] * len(tokens),
         out_specs=[wide, lags, few],
         out_shape=[
             jax.ShapeDtypeStruct(unit.shape, jnp.float32),
@@ -289,7 +293,7 @@
             transcendentals=0,
         ),
         name="conv_backward",
-    )(unit, slope, grad, kernel, table, *tokens)
+    )(unit, slope, kernel, table, *grads, *tokens)
 
 
 def turned_dot(left, right):
@@ -457,6 +461,7 @@
 def weight_kernel(rows, turns, index_ref, keep_ref, send_ref, right_ref, *rest):
     high_ref, low_ref = rest[-2:]
     kept_ref, *sent_refs = rest[-3 - turns : -2]
+    parts_of = max(1, turns // 2)
     size = keep_ref.shape[0]
     turn = pl.program_id(0)
 
@@ -470,23 +475,39 @@
     right, right_low = split(right_ref[...])
     chunk = min(size, 256)
 
-    def parts(at, ref):
+    def parts(at, place):
         for start in range(0, size, chunk):
             rows_at = slice(at + start, at + start + chunk)
             left, left_low = high_ref[rows_at], low_ref[rows_at]
             part = dot(left, right) + dot(left_low, right) + dot(left, right_low)
             for first in range(0, chunk, rows):
                 block = (start + first) // rows
-                stays = (block % 2 == index_ref[2]).astype(jnp.int32)
-                to = pl.multiple_of(stays * (size // 2) + block // 2 * rows, rows)
-                ref[pl.ds(to, rows)] = part[first : first + rows]
-
-    parts(size, kept_ref)
+                place(block, part[first : first + rows])
+
+    def keep(block, values):
+        stays = (block % 2 == index_ref[2]).astype(jnp.int32)
+        to = pl.multiple_of(stays * (size // 2) + block // 2 * rows, rows)
+        kept_ref[pl.ds(to, rows)] = values
+
+    parts(size, keep)
     for piece in range(turns):
+        group, lane = piece // 2, piece % 2 * right.shape[1]
+
+        def send(block, values):
+            at = (pl.ds(block // 2 * rows, rows), pl.ds(lane, values.shape[1]))
+            goes = block % 2 != index_ref[2]
+
+            @pl.when(goes)
+            def _():
+                sent_refs[group][at] = values
+
+            @pl.when(jnp.logical_not(goes))
+            def _():
+                sent_refs[parts_of + group][at] = values
 
         @pl.when(turn == piece)
         def _():
-            parts(0, sent_refs[piece])
+            parts(0, send)
 
 
 def weight_grad(index, groups, keep, send, right, tokens):
@@ -503,11 +524,11 @@
             in_specs=[whole, whole, pl.BlockSpec((depth, block), lambda j, c: (0, j))]
             + [anywhere] * len(tokens),
             out_specs=[pl.BlockSpec((size, block), lambda j, c: (0, j))]
-            + [pl.BlockSpec((size, block), lambda j, c: (0, 0))] * turns,
+            + [pl.BlockSpec((size // 2, 2 * block), lambda j, c: (0, 0))] * turns,
             scratch_shapes=[pltpu.VMEM((2 * size, depth), jnp.bfloat16)] * 2,
         ),
         out_shape=[jax.ShapeDtypeStruct((size, columns), jnp.float32)]
-        + [jax.ShapeDtypeStruct((size, block), jnp.float32)] * turns,
+        + [jax.ShapeDtypeStruct((size // 2, 2 * block), jnp.float32)] * turns,
         compiler_params=pltpu.CompilerParams(vmem_limit_bytes=56 * 1024 * 1024),
         cost_estimate=pl.CostEstimate(
             flops=12 * window * size * depth * columns,
@@ -658,6 +679,41 @@
     )
 
 
+def first_norm_kernel(inputs_ref, resid_ref, rows_ref, *rest):
+    out_ref = rest[-1]
+    bands = len(rest) // 2
+    channels = inputs_ref.shape[1]
+    width = 2.0 * channels
+    columns = rows_ref[...].T
+    mean, scale, total, along = [columns[:, i : i + 1] for i in range(4)]
+    for band in range(bands):
+        scaled = rest[band][...].T
+        lanes = slice(band * scaled.shape[1], (band + 1) * scaled.shape[1])
+        unit = (inputs_ref[:, lanes] - mean) * scale
+        out_ref[:, lanes] = resid_ref[:, lanes] + scale * (
+            scaled - total / width - unit * (along / width)
+        )
+
+
+def first_norm_back(inputs, resid, rows, backs, tokens):
+    count, channels = inputs.shape
+    block = min(256, count)
+    wide = pl.BlockSpec((block, channels), lambda j: (j, 0))
+    bands = [pl.BlockSpec((v.shape[0], block), lambda j: (0, j)) for v in backs]
+    tokens = list(tokens) + [backs[0]] * (len(backs) - len(tokens))
+    return pl.pallas_call(
+        first_norm_kernel,
+        grid=(count // block,),
+        in_specs=[wide, wide, pl.BlockSpec((8, block), lambda j: (0, j))]
+        + bands
+        + [anywhere] * len(tokens),
+        out_specs=wide,
+        out_shape=jax.ShapeDtypeStruct((count, channels), jnp.float32),
+        compiler_params=pltpu.CompilerParams(vmem_limit_bytes=32 * 1024 * 1024),
+        name="first_norm_backward",
+    )(inputs, resid, rows, *backs, *tokens)
+
+
 def body(
     inputs,
     cotangent,
@@ -723,10 +779,15 @@
         got = to_seq(send, step)
         return keep + (tie(got, *earlier) if earlier else got)
 
-    def finish(values, start):
+    def finish(values, start, *earlier):
         for step in steps[start:]:
-            values = halve(values, step)
+            values = halve(values, step, *earlier)
         return values[0]
+
+    def halves_of(values, step):
+        pairs = values.reshape(-1, 2, *values.shape[1:])
+        mine = (seq_index & step) // step
+        return [lax.dynamic_index_in_dim(pairs, at, 1, keepdims=False) for at in (mine, 1 - mine)]
 
     own_at = chan_index * channels
     other_at = channels - own_at
@@ -790,12 +851,13 @@
     kernels = [kernel[i * share : (i + 1) * share] for i in range(bands)]
     tables = [table[i * share : (i + 1) * share] for i in range(bands)]
 
-    unit_parts, slope_parts, mixed, mixed_other = [], [], [], []
+    unit_parts, unit_turned, slope_parts, mixed, mixed_other = [], [], [], [], []
     for i in range(bands):
         turned = unit1[:, i * band : (i + 1) * band].T.reshape(groups, share, sequences, rows)
+        unit_turned.append(turned)
         unit_parts.append(spread(tie(turned, kernel, grad_hidden_own) if i else turned))
     for i in range(bands):
-        tokens = (grad_hidden, lines) if i else (grad_out_other,)
+        tokens = (grad_hidden, lines) if i else ()
         mixed_part, slope_part = long_conv(unit_parts[i], kernels[i], tables[i], tokens)
         slope_parts.append(slope_part)
         arrived = spread(mixed_part).reshape(band, count)
@@ -843,28 +905,24 @@
     def to_dp(values):
         return lax.ppermute(values, "dp", swap)
 
-    def ready(keep, others, first, last):
+    def ready(keep, others, groups_at):
         half, size = keep.shape[0] // 2, others[0].shape[1]
-        other = jnp.concatenate([v[:half] for v in others[first:last]], axis=1)
-        total = keep[:half, first * size : last * size] + other
+        total = jnp.concatenate([keep[:half, g * size : (g + 1) * size] + others[g] for g in groups_at], axis=1)
         return total.reshape(groups // 2, -1, total.shape[1])
 
-    def joined(keep, others, got, first, last):
+    def joined(keep, others, got, groups_at):
         half, size = keep.shape[0] // 2, others[0].shape[1]
-        other = jnp.concatenate([v[half:] for v in others[first:last]], axis=1)
-        return (keep[half:, first * size : last * size] + other).reshape(got.shape) + got
+        stay = others[len(others) // 2 :]
+        total = jnp.concatenate([keep[half:, g * size : (g + 1) * size] + stay[g] for g in groups_at], axis=1)
+        return total.reshape(got.shape) + got
 
     out_keep, out_send = weight_grad(
         index, groups, *grad_out_turned, hidden, (sent[1], arrived[0], other_sums[0])
     )
     out_other = [to_dp(v) for v in out_send]
-    pieces = len(out_other)
-    middle, late = pieces // 2, pieces - pieces // 4
+    every = range(len(out_other) // 2)
     out_keep = tie(out_keep, arrived[1], other_sums[1])
-    out_ready = [
-        ready(out_keep, out_other, 0, middle),
-        ready(out_keep, out_other, middle, pieces),
-    ]
+    out_ready = [ready(out_keep, out_other, [g]) for g in every]
 
     grad_resid, grad_both, mixed_kept, norm_sums, glu_sums, *mixed_sent = glu_back(
         index,
@@ -880,8 +938,15 @@
         gates,
         out_ready,
     )
+    locals_flat = jnp.concatenate(
+        [
+            jnp.sum(glu_sums, axis=0),
+            jnp.sum(norm_sums, axis=0),
+            jnp.sum(sum(hidden_sums), axis=0),
+        ]
+    )
     out_got = [to_seq(v, steps[0]) for v in out_ready]
-    out_first = joined(out_keep, out_other, tie(out_got[0], mixed_sent[1]), 0, middle)
+    out_first = joined(out_keep, out_other, tie(out_got[0], mixed_sent[1]), [0])
     in_keep, in_send = weight_grad(
         index, groups, normed_keep, normed_send, grad_pre, (mixed_sent[1], out_first)
     )
@@ -892,63 +957,41 @@
     tokens = (in_send[0],)
     for i, at in enumerate(spots):
         total = mixed_kept[:, at] + tie(to_chan(mixed_sent[i]), *tokens)
-        moved = total.reshape(bands, groups, share, few, rows)
-        spread_spans.append(lax.all_to_all(moved, "seq", 1, 1, tiled=True))
+        moved = total.reshape(bands, groups, share, few, rows).swapaxes(0, 1)
+        spread_spans.append(spread(moved))
         if not i:
-            out_second = joined(out_keep, out_other, tie(out_got[1], moved), middle, pieces)
-            glu_keep, glu_send = weight_grad(
-                index, groups, *mixed_pair, grad_both, (moved, out_second)
-            )
+            out_second = joined(out_keep, out_other, tie(out_got[1], moved), [1])
+            in_keep = tie(in_keep, out_second)
+            in_ready = ready(in_keep, in_other, every)
+            glu_keep, glu_send = weight_grad(index, groups, *mixed_pair, grad_both, (in_ready,))
             glu_other = [to_dp(v) for v in glu_send]
-            in_keep = tie(in_keep, glu_send[0])
-            in_ready = [
-                ready(in_keep, in_other, 0, late),
-                ready(in_keep, in_other, late, pieces),
-            ]
-            tokens = (*in_ready, spread_spans[0])
-    grad_parts = jnp.concatenate(spread_spans, axis=3)
+            tokens = (glu_send[0], spread_spans[0])
     hidden = tie(hidden, out_keep, moved)
     output_send = contract(hidden, columns_other, 1, 0)
     glu_keep = tie(glu_keep, output_send)
-    glu_ready = ready(glu_keep, glu_other, 0, len(glu_other))
-    in_got = [to_seq(v, steps[0]) for v in in_ready]
+    glu_other = [tie(v, output_send) for v in glu_other]
+    glu_ready = ready(glu_keep, glu_other, [0])
+    in_got = to_seq(in_ready, steps[0])
     out_half = jnp.concatenate([out_first, out_second], axis=2)
     out_more = halve(out_half, steps[1], output_send)
-    in_first = joined(in_keep, in_other, tie(in_got[0], output_send), 0, late)
+    in_half = joined(in_keep, in_other, tie(in_got, output_send), every)
     glu_got = to_seq(glu_ready, steps[0])
-    backs, grad_kernels, conv_sums = [], [], []
+    grad_backs, backs, grad_kernels, conv_sums = [], [], [], []
     for i in range(bands):
         if i:
-            in_second = joined(in_keep, in_other, tie(in_got[1], backs[0][0]), late, pieces)
-            out_most = halve(out_more, steps[2], backs[0][0]) if len(steps) > 2 else out_more
-            tokens = (in_second, out_most)
+            before = grad_backs[0]
+            out_most = halve(out_more, steps[2], before) if len(steps) > 2 else out_more
+            glu_half = joined(glu_keep, glu_other, tie(glu_got, before), [0])
+            tokens = (out_most, glu_half)
         else:
-            tokens = (glu_ready, in_first, out_more)
+            tokens = (glu_ready, in_half, out_more)
         back, grad_kernel, conv_sum = long_conv_back(
-            unit_parts[i], slope_parts[i], grad_parts[i], kernels_turned[i], tables[i], tokens
+            unit_parts[i], slope_parts[i], spread_spans, i, kernels_turned[i], tables[i], tokens
         )
-        if i:
-            back = tie(back, backs[0][1])
-            hidden = tie(hidden, output_send, back)
-            output_keep = contract(hidden, columns_own, 1, 0)
-            output = to_chan(output_send) + (
-                output_keep + jnp.concatenate(resids, axis=0) + ffn_out_bias
-            )
-            glu_half = joined(glu_keep, glu_other, tie(glu_got, output_keep), 0, len(glu_other))
-            in_more = halve(
-                jnp.concatenate([in_first, in_second], axis=2), steps[1], output_keep
-            )
-        backs.append((back, spread(back).reshape(band, count)))
+        grad_backs.append(back)
         grad_kernels.append(grad_kernel)
         conv_sums.append(conv_sum)
-    backs = [v[1] for v in backs]
-    scaled = jnp.concatenate([v.T for v in backs], axis=1)
-    sums = jnp.stack([jnp.sum(scaled, axis=1), jnp.sum(scaled * unit1, axis=1)])
-    sums = sums + to_chan(sums)
-    total, along = sums[0][:, None], sums[1][:, None]
-    grad_inputs = tie(grad_resid, backs[1]) + scale1 * (
-        scaled - total / width - unit1 * (along / width)
-    )
+    backs.append(spread(grad_backs[0]).reshape(band, count))
 
     grad_kernel = jnp.concatenate(grad_kernels, axis=0)
     pulled = jnp.einsum(
@@ -978,26 +1021,46 @@
     states = jnp.concatenate(
         [grad_decay, grad_freq, grad_coef[0], grad_coef[1], sums[:, :3], grad_step[:, None]], axis=1
     )
-    locals_flat = jnp.concatenate(
-        [
-            jnp.sum(glu_sums, axis=0),
-            jnp.sum(norm_sums, axis=0),
-            jnp.sum(sum(hidden_sums), axis=0),
-        ]
-    )
-    columns = 2 * rows
-    own_states = jnp.pad(states, ((0, 0), (0, columns - states.shape[1]))).reshape(-1, rows)
-    few = own_states.shape[0]
-    smalls = jnp.concatenate([own_states, locals_flat.reshape(-1, rows)], axis=0)
-    glu_more = halve(glu_half, steps[1])
-    smalls = tie(smalls + to_dp(smalls), backs[1], glu_more)
-    smalls = spread(jnp.broadcast_to(smalls, (groups, *smalls.shape)))
-    states = smalls[:, :few].reshape(groups, bands, share, columns)
-    states = states.swapaxes(0, 1).reshape(channels, columns)
-    locals_flat = jnp.sum(smalls[:, few:], axis=0).reshape(-1)
+    columns = states.shape[1]
+    states = jnp.pad(states.reshape(-1), (0, -states.size % (8 * rows))).reshape(-1, rows)
+    states_rows = states.shape[0]
+    smalls = jnp.concatenate([states, locals_flat.reshape(-1, rows)], axis=0)
+    smalls = smalls + to_dp(smalls)
+    glu_more = halve(glu_half, steps[1], grad_backs[1])
+    in_more = halve(in_half, steps[1], grad_backs[1])
+    back = tie(grad_backs[1], backs[0], glu_more, in_more)
+    backs.append(spread(back).reshape(band, count))
+    last_step = steps[min(2, len(steps) - 1)]
+    last_halves = [halves_of(v, last_step) for v in (in_more, glu_more)]
+    smalls = jnp.broadcast_to(smalls, (groups, *smalls.shape))
+    hidden = tie(hidden, output_send, back, smalls, *[v[1] for v in last_halves])
+    output_keep = contract(hidden, columns_own, 1, 0)
+    output = to_chan(output_send) + (
+        output_keep + jnp.concatenate(resids, axis=0) + ffn_out_bias
+    )
+    smalls = spread(tie(smalls, backs[1], output))
+    last_got = [to_seq(tie(v[1], backs[1], output), last_step) for v in last_halves]
+    turned = tie(jnp.concatenate([v.reshape(band, count) for v in unit_turned], axis=0), backs[0])
+    sums = [
+        jnp.stack([jnp.sum(v, axis=0), jnp.sum(v * turned[i * band : (i + 1) * band], axis=0)])
+        for i, v in enumerate(backs)
+    ]
+    sums = sum(sums).reshape(-1, rows)
+    token_sums = (sums + to_chan(sums)).reshape(2, count)
+
+    states = smalls[:, :states_rows].reshape(groups, -1)[:, : part * columns]
+    states = states.reshape(groups, bands, share, columns).swapaxes(0, 1).reshape(channels, columns)
+    states = tie(states.T, smalls).T
+    locals_flat = jnp.sum(smalls[:, states_rows:], axis=0).reshape(-1)
+    norm_rows = jnp.concatenate(
+        [mean.reshape(1, count), scale1.reshape(1, count), token_sums, jnp.zeros((4, count), jnp.float32)],
+        axis=0,
+    )
+    grad_inputs = first_norm_back(flat, grad_resid, norm_rows, backs, ())
     grad_ffn_out = finish(out_most, 3).T
-    grad_ffn_in = finish(in_more, 2)
-    grad_glu = finish(glu_more, 2)
+    in_last, glu_last = [v[0] + tie(got, states, locals_flat) for v, got in zip(last_halves, last_got)]
+    grad_ffn_in = finish(in_last, 3)
+    grad_glu = finish(glu_last, 3)
     c = channels
     return (
         output.reshape(sequences, rows, channels),

time: 617 us -> 596 us (0.966)
  waiting for transfers between devices: 101 us -> 83.2 us
  local copies, waits for them, and re-layouts: 91.6 us -> 84 us
    all_to_all x2 -> x0, waiting for transfers between devices: 19.8 us -> none  [body(): spread_spans.append(lax.all_to_all(moved, 'seq', 1, 1, tiled=True))]
    all_to_all x7 -> x9, starting transfers between devices: 35.4 us -> 49.4 us  [spread(): return lax.all_to_all(values, 'seq', 0, 0, tiled=True)]
    slice x10 -> x1, local copies, waits for them, and re-layouts: 12.3 us -> 0.02 us  [body(): states = smalls[:, :states_rows].reshape(groups, -1)[:, :part * columns]]
    ppermute x14, waiting for transfers between devices: 27.4 us -> 15.6 us  [to_chan(): return lax.ppermute(values, 'chan', swap)]
    all_to_all x2 -> x0, starting transfers between devices: 9.88 us -> none  [body(): spread_spans.append(lax.all_to_all(moved, 'seq', 1, 1, tiled=True))]
    ppermute x11 -> x10, waiting for transfers between devices: 24.5 us -> 34.1 us  [to_seq(): return lax.ppermute(values, 'seq', [(a, a ^ step) for a in range(groups)])]
    ppermute x11, waiting for transfers between devices: 0.03 us -> 7.71 us  [to_dp(): return lax.ppermute(values, 'dp', swap)]
    pallas_call x2 -> x3, Pallas kernels: 30.1 us -> 34.4 us  [the longest x2 31.1 us: long_conv_back(): pl.pallas_call(partial(conv_back_kernel, len(grads)), grid=(part // block...]
  transfers between devices with their start and end apart: 45 -> 44, of which waited for: 11 -> 16; matrix products, arithmetic and copies ran while one was open for 34% -> 33% of each run, Pallas kernels for 28% -> 30%
where the time goes in v3:
time: 596 us; the launch traced here: 584 us
  Pallas kernels  174 us (29%)
  local copies, waits for them, and re-layouts  84 us (14%)
  other arithmetic  83.4 us (14%)
  waiting for transfers between devices  83.2 us (14%)
  starting transfers between devices  81.2 us (14%)
  matrix products  69.4 us (12%)
  blocking collectives  6.53 us (1%)
    pallas_call x3, Pallas kernels, weight_grad(): pl.pallas_call(partial(weight_kernel, size // groups, turns), grid_spec=p...  58.3 us
    dot_general x9, matrix products, contract(): lax.dot_general(left, right, (((left_dim,), (right_dim,)), ((), ())), pre...  57 us
    pallas_call x2, Pallas kernels, feed_forward(): pl.pallas_call(feed_forward_kernel, grid_spec=pltpu.PrefetchScalarGridSpe...  52 us
    all_to_all x9, starting transfers between devices, spread(): return lax.all_to_all(values, 'seq', 0, 0, tiled=True)  49.4 us
    unnamed x253, local copies, waits for them, and re-layouts  45.6 us
    ppermute x10, waiting for transfers between devices, to_seq(): return lax.ppermute(values, 'seq', [(a, a ^ step) for a in range(groups)])  34.1 us
    pallas_call x2, Pallas kernels, long_conv_back(): pl.pallas_call(partial(conv_back_kernel, len(grads)), grid=(part // block...  31.1 us
    all_to_all x9, waiting for transfers between devices, spread(): return lax.all_to_all(values, 'seq', 0, 0, tiled=True)  25.8 us
  transfers between devices with their start and end apart: 44, of which 16 were waited for; matrix products, arithmetic and copies ran while one was open for 33% of the time, Pallas kernels for 30%

profile of v3, /device:TPU:0, one launch (start us, length us, event | category | flops | bytes accessed | tf_op | source)
XLA Modules:
  0.0 584.4 jit_solution(17963336826687087337)
XLA Ops:
  2.8 6.5 %psum.7.refs_1_ = f32[16,128]{1,0:T(8,128)} all-reduce(f32[16,128]{1,0:T(8,128)S(1)} %pad_maximum_fusion.16), channel_id=1, replica_groups=mesh['dp'=2,'seq'=8,'chan'=2] {'chan'}, use_global_device_ids=true, to_apply=%region_2.0 | all-reduce | flops 2048 | bytes 16384 | tf_op jit(solution)/shard_map/psum | solution.py:798
  19.2 5.8 all-to-all-start
  41.9 11.0 %convolution_bitcast_fusion.refs_2_ = f32[1024,2048]{1,0:T(8,128)} fusion(f32[1024,512]{1,0:T(8,128)S(1)} %bitcast.210, f32[2048,1024]{1,0:T(8,128)} %param.32, s32[]{:T(128)S(6)} %select_n.100), kind=kOutput, calls=%fused_computation | convolution fusion | flops 6442450944 | bytes 14680068 | tf_op jit(solution)/shard_map/dot_general | solution.py:42
  55.3 6.0 %all-to-all-start.2 = ((f32[8,32,8,128]{3,2,1,0:T(8,128)}), f32[8,32,8,128]{3,2,1,0:T(8,128)}, u32[]{:S(2)}, u32[]{:S(2)}) async-start(f32[8,32,8,128]{3,2,1,0:T(8,128)} %tie.31), calls=%async_computation.2 | async-start | bytes 2097152 | tf_op jit(solution)/shard_map/all_to_all | solution.py:759
  68.1 12.9 %fusion.7.rest_0_.back_ref = f32[1024,2048]{1,0:T(8,128)} fusion(f32[1024,2048]{1,0:T(8,128)} %convolution_bitcast_fusion.refs_2_, f32[1024,512]{1,0:T(8,128)} %collective-permute-done.refs_1_.refs_0_, f32[2048,1024]{1,0:T(8,128)} %param.32, s32[]{:T(128)S(6)} %select_n.101), kind=kOutput, calls=%fused_computation.9 | convolution fusion | flops 6444548096 | bytes 23068676 | tf_op jit(solution)/shard_map/dot_general | solution.py:42
  81.1 6.4 %fusion.79 = f32[8,2048]{1,0:T(8,128)S(1)} fusion(f32[1024,2048]{1,0:T(8,128)} %weight_ref.3, f32[8,512]{1,0:T(8,128)S(1)} %get-tuple-element.291, f32[8,512]{1,0:T(8,128)S(1)} %get-tuple-element.290), kind=kOutput, calls=%fused_computation.231 | convolution fusion | flops 201334784 | bytes 8486912 | tf_op jit(solution)/shard_map/dot_general | solution.py:816
  87.6 6.0 %all-to-all-start.1 = ((f32[8,32,8,128]{3,2,1,0:T(8,128)}), f32[8,32,8,128]{3,2,1,0:T(8,128)}, u32[]{:S(2)}, u32[]{:S(2)}) async-start(f32[8,32,8,128]{3,2,1,0:T(8,128)} %copy-done.7), calls=%async_computation.1 | async-start | bytes 2097152 | tf_op jit(solution)/shard_map/all_to_all | solution.py:759
  93.7 4.9 conv_forward.3
  101.2 16.0 %all-to-all-done.1 = f32[8,32,8,128]{3,2,1,0:T(8,128)} async-done(((f32[8,32,8,128]{3,2,1,0:T(8,128)}), f32[8,32,8,128]{3,2,1,0:T(8,128)}, u32[]{:S(2)}, u32[]{:S(2)}) %all-to-all-start.1) | async-done | bytes 1048608 | tf_op jit(solution)/shard_map/all_to_all | solution.py:759
  117.2 4.6 all-to-all-start.3
  125.3 5.3 copy.279
  137.9 7.9 %all-to-all-done.3 = f32[8,32,8,128]{3,2,1,0:T(8,128)} async-done(((f32[8,32,8,128]{3,2,1,0:T(8,128)}), f32[8,32,8,128]{3,2,1,0:T(8,128)}, u32[]{:S(2)}, u32[]{:S(2)}) %all-to-all-start.3) | async-done | bytes 1048608 | tf_op jit(solution)/shard_map/all_to_all | solution.py:759
  157.9 13.0 %collective-permute-done.3 = f32[256,1024]{1,0:T(8,128)S(1)} collective-permute-done((f32[256,1024]{1,0:T(8,128)}, f32[256,1024]{1,0:T(8,128)S(1)}, u32[]{:S(2)}, u32[]{:S(2)}) %collective-permute-start.3) | collective-permute-done | bytes 1048608 | tf_op jit(solution)/shard_map/ppermute | solution.py:753
  200.4 26.1 %feed_forward.2 = (f32[1024,2048]{1,0:T(8,128)}, f32[1024,2048]{1,0:T(8,128)}, f32[512,1024]{1,0:T(8,128)}, f32[512,1024]{1,0:T(8,128)}, f32[1024,512]{1,0:T(8,1...) custom-call(s32[3]{0:T(128)} %pad_add_fusion.1.index_ref, ...), custom_call_target="tpu_custom_call" | custom-call | flops 386547056640 | bytes 29360128 | tf_op jit(solution)/shard_map/feed_forward/pallas_call | solution.py:405
  228.6 25.9 %feed_forward.3 = (f32[1024,2048]{1,0:T(8,128)}, f32[1024,2048]{1,0:T(8,128)}, f32[512,1024]{1,0:T(8,128)}, f32[512,1024]{1,0:T(8,128)}, f32[1024,512]{1,0:T(8,1...) custom-call(s32[3]{0:T(128)} %pad_add_fusion.1.index_ref, ...), custom_call_target="tpu_custom_call", output_to_operand_aliasing={{0}: (7, {}), {1}: (8, {}), {2}: (9, {}), {3}: (10, {}), {4... | custom-call | flops 386547056640 | bytes 29360128 | tf_op jit(solution)/shard_map/feed_forward/pallas_call | solution.py:405
  256.7 22.3 %weight_gradient.3 = (f32[512,2048]{1,0:T(8,128)}, f32[256,1024]{1,0:T(8,128)}, f32[256,1024]{1,0:T(8,128)}, f32[256,1024]{1,0:T(8,128)}, f32[256,1024]{1,0:T(8,128)}) custom-call(s32[3]{0:T(128)} %pad_add_fusion.1.index_ref, f32[512,1024]{1,0:T(8,128)} %copy.240.rest_0_.keep_ref, f32[512,1024]{1,0:T(8,128)} %copy.241.rest_1_.send_ref, ...), custom_call_target="tpu_custom_call" | custom-call | flops 386547056640 | bytes 20971520 | tf_op jit(solution)/shard_map/weight_gradient/pallas_call | solution.py:519
  286.5 5.4 slice_add_fusion.8
  294.7 20.3 %glu_backward.1 = (f32[1024,512]{1,0:T(8,128)}, f32[1024,1024]{1,0:T(8,128)}, f32[512,1024]{1,0:T(8,128)}, f32[8,1536]{1,0:T(8,128)}, f32[8,1024]{1,0:T(8,128)}, /*index=5*/f32[512,512]{1,0:T(8,128)}, f32[512,512]{1,0:T(8,128)}) custom-call(s32[3]{0:T(128)} %pad_add_fusion.1.index_ref, f32[1024,512]{1,0:T(8,128)} %get-tuple-element.79.keep_ref, ...), custom_call_target="tpu_custom_call" | custom-call | flops 193273528320 | bytes 27262976 | tf_op jit(solution)/shard_map/glu_backward/pallas_call | solution.py:629
  320.6 22.3 %weight_gradient.4 = (f32[512,2048]{1,0:T(8,128)}, f32[256,1024]{1,0:T(8,128)}, f32[256,1024]{1,0:T(8,128)}, f32[256,1024]{1,0:T(8,128)}, f32[256,1024]{1,0:T(8,128)}) custom-call(s32[3]{0:T(128)} %pad_add_fusion.1.index_ref, f32[512,1024]{1,0:T(8,128)} %get-tuple-element.86.keep_ref, f32[512,1024]{1,0:T(8,128)} %get-tuple-element.87.send_ref, ...), custom_call_target="tpu_custom_call" | custom-call | flops 386547056640 | bytes 20971520 | tf_op jit(solution)/shard_map/weight_gradient/pallas_call | solution.py:519
  347.9 5.7 all-to-all-start.4
  363.3 4.6 slice_add_fusion.4
  370.8 13.7 %weight_gradient.5 = (f32[512,1024]{1,0:T(8,128)}, f32[256,1024]{1,0:T(8,128)}, f32[256,1024]{1,0:T(8,128)}) custom-call(s32[3]{0:T(128)} %pad_add_fusion.1.index_ref, f32[512,1024]{1,0:T(8,128)} %get-tuple-element.249.rest_2_.keep_ref, f32[512,1024]{1,0:T(8,128)} %get-tuple-element.248.rest_3_.send_ref, f32[1024,1024]{1,0:T(8,128)} %get-tuple-element.85.right_ref, ...), custom_call_target="tpu_custom_call" | custom-call | flops 193273528320 | bytes 12582912 | tf_op jit(solution)/shard_map/weight_gradient/pallas_call | solution.py:519
  393.6 11.5 %fusion.refs_1_ = f32[1024,512]{1,0:T(8,128)} fusion(f32[1024,2048]{1,0:T(8,128)} %tie.43.refs_0_, f32[2048,1024]{1,0:T(8,128)} %param.32, s32[]{:T(128)S(6)} %select_n.101), kind=kOutput, calls=%fused_computation.2 | convolution fusion | flops 6442450944 | bytes 14680068 | tf_op jit(solution)/shard_map/dot_general | solution.py:42
  417.9 9.3 %collective-permute-done.26.refs_0_ = f32[4,64,2048]{2,1,0:T(8,128)} collective-permute-done((f32[4,64,2048]{2,1,0:T(8,128)}, f32[4,64,2048]{2,1,0:T(8,128)}, u32[]{:S(2)}, u32[]{:S(2)}) %collective-permute-start.26) | collective-permute-done | bytes 2097184 | tf_op jit(solution)/shard_map/ppermute | solution.py:756
  433.7 15.8 %conv_backward.2 = (f32[8,32,8,128]{3,2,1,0:T(8,128)}, f32[32,8,128]{2,1,0:T(8,128)S(1)}, f32[32,8,128]{2,1,0:T(8,128)S(1)}) custom-call(f32[8,32,8,128]{3,2,1,0:T(8,128)S(1)} %all-to-all-done.unit_ref, f32[8,32,8,128]{3,2,1,0:T(8,128)S(1)} %copy-done.20, f32[32,8,128]{2,1,0:T(8,128)S(1)} %copy-done.15, f32[32,8,128]{2,1,0:T(8,128)S(1)} %copy-done.11, ...), custom_call_target="tpu_custom_call" | custom-call | flops 96636764160 | bytes 4194304 | tf_op jit(solution)/shard_map/conv_backward/pallas_call | solution.py:276
  449.4 6.6 %all-to-all-start.6 = ((f32[8,32,8,128]{3,2,1,0:T(8,128)}), f32[8,32,8,128]{3,2,1,0:T(8,128)S(1)}, u32[]{:S(2)}, u32[]{:S(2)}) async-start(f32[8,32,8,128]{3,2,1,0:T(8,128)} %get-tuple-element.101.refs_1_), calls=%async_computation.6 | async-start | bytes 2097152 | tf_op jit(solution)/shard_map/all_to_all | solution.py:759
  461.7 15.4 %conv_backward.3 = (f32[8,32,8,128]{3,2,1,0:T(8,128)S(1)}, f32[32,8,128]{2,1,0:T(8,128)S(1)}, f32[32,8,128]{2,1,0:T(8,128)S(1)}) custom-call(f32[8,32,8,128]{3,2,1,0:T(8,128)} %all-to-all-done.2.unit_ref, f32[8,32,8,128]{3,2,1,0:T(8,128)S(1)} %copy-done.18, f32[32,8,128]{2,1,0:T(8,128)S(1)} %copy-done.14, f32[32,8,128]{2,1,0:T(8,128)S(1)} %copy-done.13, ...), custom_call_target="tpu_custom_call" | custom-call | flops 96636764160 | bytes 4194304 | tf_op jit(solution)/shard_map/conv_backward/pallas_call | solution.py:276
  488.8 5.1 collective-permute-done.29.refs_0_
  497.9 5.9 %all-to-all-start.7 = ((f32[8,32,8,128]{3,2,1,0:T(8,128)}), f32[8,32,8,128]{3,2,1,0:T(8,128)S(1)}, u32[]{:S(2)}, u32[]{:S(2)}) async-start(f32[8,32,8,128]{3,2,1,0:T(8,128)} %tie.53.refs_2_), calls=%async_computation.7 | async-start | bytes 2097152 | tf_op jit(solution)/shard_map/all_to_all | solution.py:759
  508.4 10.5 %fusion.4 = f32[1024,512]{1,0:T(8,128)S(1)} fusion(f32[1024,2048]{1,0:T(8,128)} %tie.54, f32[2048,1024]{1,0:T(8,128)} %param.32, s32[]{:T(128)S(6)} %select_n.100), kind=kOutput, calls=%fused_computation.6 | convolution fusion | flops 6442450944 | bytes 14680068 | tf_op jit(solution)/shard_map/dot_general | solution.py:42
  526.0 5.0 all-to-all-start.8
  557.5 16.7 %collective-permute-done.34.refs_0_ = f32[1,64,2048]{2,1,0:T(8,128)} collective-permute-done((f32[1,64,2048]{2,1,0:T(8,128)}, f32[1,64,2048]{2,1,0:T(8,128)}, u32[]{:S(2)}, u32[]{:S(2)}) %collective-permute-start.34) | collective-permute-done | bytes 524320 | tf_op jit(solution)/shard_map/ppermute | solution.py:756
  (505 shorter events, 227.4 us)
Async XLA Ops:
  10.6 56.7 %collective-permute-start = (f32[1024,512]{1,0:T(8,128)}, f32[1024,512]{1,0:T(8,128)}, u32[]{:S(2)}, u32[]{:S(2)}) collective-permute-start(f32[1024,512]{1,0:T(8,128)} %tie.32), channel_id=1, source_target_pairs={{0,1},{1,0},{2,3},{3,2},{4,5},{5,4},{6,7},{7,6},{8,9},{9,8},{10,11... | collective-permute-start | bytes 6291464 | tf_op jit(solution)/shard_map/ppermute | solution.py:753
  19.2 36.1 %all-to-all-start = ((f32[8,32,8,128]{3,2,1,0:T(8,128)}), f32[8,32,8,128]{3,2,1,0:T(8,128)S(1)}, u32[]{:S(2)}, u32[]{:S(2)}) async-start(f32[8,32,8,128]{3,2,1,0:T(8,128)} %bitcast.229), calls=%async_computation | async-start | bytes 2097152 | tf_op jit(solution)/shard_map/all_to_all | solution.py:759
  55.3 32.3 %all-to-all-start.2 = ((f32[8,32,8,128]{3,2,1,0:T(8,128)}), f32[8,32,8,128]{3,2,1,0:T(8,128)}, u32[]{:S(2)}, u32[]{:S(2)}) async-start(f32[8,32,8,128]{3,2,1,0:T(8,128)} %tie.31), calls=%async_computation.2 | async-start | bytes 2097152 | tf_op jit(solution)/shard_map/all_to_all | solution.py:759
  87.6 29.6 %all-to-all-start.1 = ((f32[8,32,8,128]{3,2,1,0:T(8,128)}), f32[8,32,8,128]{3,2,1,0:T(8,128)}, u32[]{:S(2)}, u32[]{:S(2)}) async-start(f32[8,32,8,128]{3,2,1,0:T(8,128)} %copy-done.7), calls=%async_computation.1 | async-start | bytes 2097152 | tf_op jit(solution)/shard_map/all_to_all | solution.py:759
  117.2 28.6 %all-to-all-start.3 = ((f32[8,32,8,128]{3,2,1,0:T(8,128)}), f32[8,32,8,128]{3,2,1,0:T(8,128)}, u32[]{:S(2)}, u32[]{:S(2)}) async-start(f32[8,32,8,128]{3,2,1,0:T(8,128)} %copy-done.8), calls=%async_computation.3 | async-start | bytes 2097152 | tf_op jit(solution)/shard_map/all_to_all | solution.py:759
  124.3 23.9 %collective-permute-start.2 = (f32[256,1024]{1,0:T(8,128)}, f32[256,1024]{1,0:T(8,128)}, u32[]{:S(2)}, u32[]{:S(2)}) collective-permute-start(f32[256,1024]{1,0:T(8,128)} %bitcast.180), channel_id=1, source_target_pairs={{0,1},{1,0},{2,3},{3,2},{4,5},{5,4},{6,7},{7,6},{8,9},{9,8},{10,11... | collective-permute-start | bytes 3145736 | tf_op jit(solution)/shard_map/ppermute | solution.py:753
  148.2 22.7 %collective-permute-start.3 = (f32[256,1024]{1,0:T(8,128)}, f32[256,1024]{1,0:T(8,128)S(1)}, u32[]{:S(2)}, u32[]{:S(2)}) collective-permute-start(f32[256,1024]{1,0:T(8,128)} %tie.34), channel_id=1, source_target_pairs={{0,1},{1,0},{2,3},{3,2},{4,5},{5,4},{6,7},{7,6},{8,9},{9,8},{10,11... | collective-permute-start | bytes 3145736 | tf_op jit(solution)/shard_map/ppermute | solution.py:753
  174.0 26.4 %collective-permute-start.5 = (f32[512,512]{1,0:T(8,128)}, f32[512,512]{1,0:T(8,128)}, u32[]{:S(2)}, u32[]{:S(2)}) collective-permute-start(f32[512,512]{1,0:T(8,128)} %get-tuple-element.258.resid_ref), channel_id=1, source_target_pairs={{0,1},{1,0},{2,3},{3,2},{4,5},{5,4},{6,7},{7,6},{8,9},{9,8},{10,11... | collective-permute-start | bytes 3145736 | tf_op jit(solution)/shard_map/ppermute | solution.py:753
  177.8 50.8 %collective-permute-start.4 = (f32[512,512]{1,0:T(8,128)}, f32[512,512]{1,0:T(8,128)}, u32[]{:S(2)}, u32[]{:S(2)}) collective-permute-start(f32[512,512]{1,0:T(8,128)} %get-tuple-element.255.refs_1_.resid_ref), channel_id=1, source_target_pairs={{0,1},{1,0},{2,3},{3,2},{4,5},{5,4},{6,7},{7,6},{8,9},{9,8},{10,11... | collective-permute-start | bytes 3145736 | tf_op jit(solution)/shard_map/ppermute | solution.py:753
  226.5 30.1 %collective-permute-start.6 = (f32[512,512]{1,0:T(8,128)}, f32[512,512]{1,0:T(8,128)}, u32[]{:S(2)}, u32[]{:S(2)}) collective-permute-start(f32[512,512]{1,0:T(8,128)} %get-tuple-element.75), channel_id=1, source_target_pairs={{0,1},{1,0},{2,3},{3,2},{4,5},{5,4},{6,7},{7,6},{8,9},{9,8},{10,11... | collective-permute-start | bytes 3145736 | tf_op jit(solution)/shard_map/ppermute | solution.py:753
  227.4 29.3 %collective-permute-start.7 = (f32[512,128]{1,0:T(8,128)}, f32[512,128]{1,0:T(8,128)}, u32[]{:S(2)}, u32[]{:S(2)}) collective-permute-start(f32[512,128]{1,0:T(8,128)} %get-tuple-element.76.rest_2_), channel_id=1, source_target_pairs={{0,1},{1,0},{2,3},{3,2},{4,5},{5,4},{6,7},{7,6},{8,9},{9,8},{10,11... | collective-permute-start | bytes 786440 | tf_op jit(solution)/shard_map/ppermute | solution.py:753
  254.6 25.4 %collective-permute-start.8 = (f32[512,512]{1,0:T(8,128)}, f32[512,512]{1,0:T(8,128)}, u32[]{:S(2)}, u32[]{:S(2)}) collective-permute-start(f32[512,512]{1,0:T(8,128)} %get-tuple-element.74.rest_0_), channel_id=1, source_target_pairs={{0,1},{1,0},{2,3},{3,2},{4,5},{5,4},{6,7},{7,6},{8,9},{9,8},{10,11... | collective-permute-start | bytes 3145736 | tf_op jit(solution)/shard_map/ppermute | solution.py:753
  255.4 24.2 %collective-permute-start.9 = (f32[512,128]{1,0:T(8,128)}, f32[512,128]{1,0:T(8,128)}, u32[]{:S(2)}, u32[]{:S(2)}) collective-permute-start(f32[512,128]{1,0:T(8,128)} %get-tuple-element.78.rest_3_), channel_id=1, source_target_pairs={{0,1},{1,0},{2,3},{3,2},{4,5},{5,4},{6,7},{7,6},{8,9},{9,8},{10,11... | collective-permute-start | bytes 786440 | tf_op jit(solution)/shard_map/ppermute | solution.py:753
  291.9 26.4 %collective-permute-start.14 = (f32[4,64,1024]{2,1,0:T(8,128)}, f32[4,64,1024]{2,1,0:T(8,128)}, u32[]{:S(2)}, u32[]{:S(2)}) collective-permute-start(f32[4,64,1024]{2,1,0:T(8,128)} %bitcast.24.rest_10_), channel_id=1, source_target_pairs={{0,2},{2,0},{4,6},{6,4},{8,10},{10,8},{12,14},{14,12},{1,3},{3,1},... | collective-permute-start | bytes 3145736 | tf_op jit(solution)/shard_map/ppermute | solution.py:756
  294.0 59.6 %collective-permute-start.16 = (f32[4,64,1024]{2,1,0:T(8,128)}, f32[4,64,1024]{2,1,0:T(8,128)}, u32[]{:S(2)}, u32[]{:S(2)}) collective-permute-start(f32[4,64,1024]{2,1,0:T(8,128)} %bitcast.25.rest_11_), channel_id=1, source_target_pairs={{0,2},{2,0},{4,6},{6,4},{8,10},{10,8},{12,14},{14,12},{1,3},{3,1},... | collective-permute-start | bytes 3145736 | tf_op jit(solution)/shard_map/ppermute | solution.py:756
  315.0 28.6 %collective-permute-start.17 = (f32[512,512]{1,0:T(8,128)}, f32[512,512]{1,0:T(8,128)}, u32[]{:S(2)}, u32[]{:S(2)}) collective-permute-start(f32[512,512]{1,0:T(8,128)} %get-tuple-element.92), channel_id=1, source_target_pairs={{0,1},{1,0},{2,3},{3,2},{4,5},{5,4},{6,7},{7,6},{8,9},{9,8},{10,11... | collective-permute-start | bytes 3145736 | tf_op jit(solution)/shard_map/ppermute | solution.py:753
  347.9 38.6 %all-to-all-start.4 = ((f32[8,2,32,4,128]{4,3,2,1,0:T(4,128)}), f32[8,2,32,4,128]{4,3,2,1,0:T(4,128)}, u32[]{:S(2)}, u32[]{:S(2)}) async-start(f32[8,2,32,4,128]{4,3,2,1,0:T(4,128)} %bitcast.182.refs_1_), calls=%async_computation.4 | async-start | bytes 2097152 | tf_op jit(solution)/shard_map/all_to_all | solution.py:759
  353.7 32.9 %collective-permute-start.12 = (f32[512,512]{1,0:T(8,128)}, f32[512,512]{1,0:T(8,128)}, u32[]{:S(2)}, u32[]{:S(2)}) collective-permute-start(f32[512,512]{1,0:T(8,128)} %get-tuple-element.84.refs_1_.rest_0_), channel_id=1, source_target_pairs={{0,1},{1,0},{2,3},{3,2},{4,5},{5,4},{6,7},{7,6},{8,9},{9,8},{10,11... | collective-permute-start | bytes 3145736 | tf_op jit(solution)/shard_map/ppermute | solution.py:753
  361.3 44.7 %collective-permute-start.21 = (f32[2,64,2048]{2,1,0:T(8,128)}, f32[2,64,2048]{2,1,0:T(8,128)}, u32[]{:S(2)}, u32[]{:S(2)}) collective-permute-start(f32[2,64,2048]{2,1,0:T(8,128)} %dynamic-slice_bitcast_fusion.1), channel_id=1, source_target_pairs={{0,4},{2,6},{4,0},{6,2},{8,12},{10,14},{12,8},{14,10},{1,5},{3,7},... | collective-permute-start | bytes 3145736 | tf_op jit(solution)/shard_map/ppermute | solution.py:756
  369.3 57.9 %collective-permute-start.26 = (f32[4,64,2048]{2,1,0:T(8,128)}, f32[4,64,2048]{2,1,0:T(8,128)}, u32[]{:S(2)}, u32[]{:S(2)}) collective-permute-start(f32[4,64,2048]{2,1,0:T(8,128)} %bitcast.29.rest_0_), channel_id=1, source_target_pairs={{0,2},{2,0},{4,6},{6,4},{8,10},{10,8},{12,14},{14,12},{1,3},{3,1},... | collective-permute-start | bytes 6291464 | tf_op jit(solution)/shard_map/ppermute | solution.py:756
  384.5 27.9 %collective-permute-start.23 = (f32[256,1024]{1,0:T(8,128)}, f32[256,1024]{1,0:T(8,128)}, u32[]{:S(2)}, u32[]{:S(2)}) collective-permute-start(f32[256,1024]{1,0:T(8,128)} %get-tuple-element.95.refs_1_), channel_id=1, source_target_pairs={{0,16},{16,0},{1,17},{17,1},{2,18},{18,2},{3,19},{19,3},{4,20},{20... | collective-permute-start | bytes 3145736 | tf_op jit(solution)/shard_map/ppermute | solution.py:906
  384.5 27.9 %collective-permute-start.27 = (f32[256,1024]{1,0:T(8,128)}, f32[256,1024]{1,0:T(8,128)}, u32[]{:S(2)}, u32[]{:S(2)}) collective-permute-start(f32[256,1024]{1,0:T(8,128)} %get-tuple-element.102), channel_id=1, source_target_pairs={{0,16},{16,0},{1,17},{17,1},{2,18},{18,2},{3,19},{19,3},{4,20},{20... | collective-permute-start | bytes 3145736 | tf_op jit(solution)/shard_map/ppermute | solution.py:906
  389.8 42.2 %all-to-all-start.5 = ((f32[8,2,32,4,128]{4,3,2,1,0:T(4,128)}), f32[8,2,32,4,128]{4,3,2,1,0:T(4,128)S(1)}, u32[]{:S(2)}, u32[]{:S(2)}) async-start(f32[8,2,32,4,128]{4,3,2,1,0:T(4,128)} %bitcast.218), calls=%async_computation.5 | async-start | bytes 2097152 | tf_op jit(solution)/shard_map/all_to_all | solution.py:759
  405.1 113.8 %collective-permute-start.20 = (f32[1024,512]{1,0:T(8,128)}, f32[1024,512]{1,0:T(8,128)}, u32[]{:S(2)}, u32[]{:S(2)}) collective-permute-start(f32[1024,512]{1,0:T(8,128)} %fusion.refs_1_), channel_id=1, source_target_pairs={{0,1},{1,0},{2,3},{3,2},{4,5},{5,4},{6,7},{7,6},{8,9},{9,8},{10,11... | collective-permute-start | bytes 6291464 | tf_op jit(solution)/shard_map/ppermute | solution.py:753
  409.5 50.9 %collective-permute-start.22 = (f32[1,64,2048]{2,1,0:T(8,128)}, f32[1,64,2048]{2,1,0:T(8,128)}, u32[]{:S(2)}, u32[]{:S(2)}) collective-permute-start(f32[1,64,2048]{2,1,0:T(8,128)} %constant_dynamic-slice_fusion.2), channel_id=1, source_target_pairs={{0,8},{2,10},{4,12},{6,14},{8,0},{10,2},{12,4},{14,6},{1,9},{3,11}... | collective-permute-start | bytes 1572872 | tf_op jit(solution)/shard_map/ppermute | solution.py:756
  416.4 39.6 %collective-permute-start.28 = (f32[4,64,1024]{2,1,0:T(8,128)}, f32[4,64,1024]{2,1,0:T(8,128)}, u32[]{:S(2)}, u32[]{:S(2)}) collective-permute-start(f32[4,64,1024]{2,1,0:T(8,128)} %bitcast.34.rest_2_), channel_id=1, source_target_pairs={{0,2},{2,0},{4,6},{6,4},{8,10},{10,8},{12,14},{14,12},{1,3},{3,1},... | collective-permute-start | bytes 3145736 | tf_op jit(solution)/shard_map/ppermute | solution.py:756
  431.4 54.7 %collective-permute-start.30 = (f32[2,64,2048]{2,1,0:T(8,128)}, f32[2,64,2048]{2,1,0:T(8,128)}, u32[]{:S(2)}, u32[]{:S(2)}) collective-permute-start(f32[2,64,2048]{2,1,0:T(8,128)} %dynamic-slice_bitcast_fusion), channel_id=1, source_target_pairs={{0,4},{2,6},{4,0},{6,2},{8,12},{10,14},{12,8},{14,10},{1,5},{3,7},... | collective-permute-start | bytes 3145736 | tf_op jit(solution)/shard_map/ppermute | solution.py:756
  449.4 47.1 %all-to-all-start.6 = ((f32[8,32,8,128]{3,2,1,0:T(8,128)}), f32[8,32,8,128]{3,2,1,0:T(8,128)S(1)}, u32[]{:S(2)}, u32[]{:S(2)}) async-start(f32[8,32,8,128]{3,2,1,0:T(8,128)} %get-tuple-element.101.refs_1_), calls=%async_computation.6 | async-start | bytes 2097152 | tf_op jit(solution)/shard_map/all_to_all | solution.py:759
  497.9 26.8 %all-to-all-start.7 = ((f32[8,32,8,128]{3,2,1,0:T(8,128)}), f32[8,32,8,128]{3,2,1,0:T(8,128)S(1)}, u32[]{:S(2)}, u32[]{:S(2)}) async-start(f32[8,32,8,128]{3,2,1,0:T(8,128)} %tie.53.refs_2_), calls=%async_computation.7 | async-start | bytes 2097152 | tf_op jit(solution)/shard_map/all_to_all | solution.py:759
  526.0 24.7 %all-to-all-start.8 = ((f32[8,108,128]{2,1,0:T(8,128)}), f32[8,108,128]{2,1,0:T(8,128)}, u32[]{:S(2)}, u32[]{:S(2)}) async-start(f32[8,108,128]{2,1,0:T(8,128)} %tie.56), calls=%async_computation.8 | async-start | bytes 917504 | tf_op jit(solution)/shard_map/all_to_all | solution.py:759
  541.3 32.9 %collective-permute-start.34 = (f32[1,64,2048]{2,1,0:T(8,128)}, f32[1,64,2048]{2,1,0:T(8,128)}, u32[]{:S(2)}, u32[]{:S(2)}) collective-permute-start(f32[1,64,2048]{2,1,0:T(8,128)} %tie.60), channel_id=1, source_target_pairs={{0,8},{2,10},{4,12},{6,14},{8,0},{10,2},{12,4},{14,6},{1,9},{3,11}... | collective-permute-start | bytes 1572872 | tf_op jit(solution)/shard_map/ppermute | solution.py:756
  544.3 34.1 %collective-permute-start.33 = (f32[1,64,1024]{2,1,0:T(8,128)}, f32[1,64,1024]{2,1,0:T(8,128)S(1)}, u32[]{:S(2)}, u32[]{:S(2)}) collective-permute-start(f32[1,64,1024]{2,1,0:T(8,128)} %tie.58), channel_id=1, source_target_pairs={{0,8},{2,10},{4,12},{6,14},{8,0},{10,2},{12,4},{14,6},{1,9},{3,11}... | collective-permute-start | bytes 786440 | tf_op jit(solution)/shard_map/ppermute | solution.py:756
  (131 other events, 854.7 us)
